TPU v7x, 32 devices: a whole 2x2x4 slice. The times are simulated.
32 devices in a mesh: row: 8 (over z, x), col: 4 (over y, core).
Axes of the slice: x: 2, y: 2, z: 4, core: 2. Of those that a mesh axis runs over, the one named last changes fastest.
Arguments:
- features: bfloat16 [16384, 128], P(('col', 'row')), may hold values from -6 to 6
- weight: bfloat16 [128, 128], replicated, may hold values from -0.5 to 0.5
- bias_terms: float32 [128], replicated, may hold values from -3 to 3
- blocks: bfloat16 [640, 512, 128], P('row', 'col'), may hold values from -0.15625 to 0.15625
- block_rows: int32 [640, 4], P('row', 'col'), may hold values from 0 to 15, as said below
- block_cols: int32 [640, 4], P('row', 'col'), may hold values from 0 to 31, as said below
- tile_slot_count: int32 [8, 4], P('row', 'col'), may hold values from 10 to 80, as said below
- cotangent: bfloat16 [16384, 128], P(('row', 'col')), may hold values from -6 to 6
Outputs:
- hidden_out: bfloat16 [16384, 128], P(('row', 'col'))
- feat_grad: float32 [16384, 128], P(('col', 'row'))
- weight_grad: float32 [128, 128], replicated
- bias_grad: float32 [128], replicated
Inputs may be any that keep to these rules, and one draw needn't show every extreme that they name: `block_rows`: only the first tile_slot_count slots of a tile are live; the live slots of one tile name distinct pairs of row block and column block. `block_cols`: column block of each slot, paired with block_rows. `tile_slot_count`: some tile has all 80 slots live.
All inputs are finite; a program needn't handle non-finite values.
Results may differ from a plain program's by a relative error of at most 0.019.
Values may be sent and summed in bfloat16 or wider, within the bound.
No kernel may reach another device: no remote copies, remote signals or barrier semaphores. Data moves between devices by JAX's collectives and lax.ppermute only.
A program may use at most 64 MiB of HBM per device.

v0:
```python
from functools import partial
import math

import jax
import jax.numpy as jnp
from jax import lax
from jax.sharding import PartitionSpec as P

BS = 128


def picker_lookup(slot_index_list, active_flags, segment_index):
    target_rows = jnp.arange(segment_index, dtype=jnp.int32)[:, None]
    return (slot_index_list[None, :] == target_rows).astype(jnp.float32) * active_flags[None, :]


def per_tile_forward(
    local_block_list,
    row_index_list,
    column_index_list,
    active_flags,
    source_features,
    row_block_index,
):
    channels = source_features.shape[1]
    picked = source_features.reshape(-1, BS, channels)[column_index_list]
    block_product = jnp.einsum(
        "kab,kbf->kaf", local_block_list, picked, preferred_element_type=jnp.float32
    )
    tile_picker = picker_lookup(row_index_list, active_flags, row_block_index)
    reduced_output = jnp.einsum(
        "rk,kaf->raf", tile_picker, block_product, precision=lax.Precision.HIGHEST
    )
    return reduced_output.reshape(row_block_index * BS, channels)


def per_tile_backward(
    local_block_list,
    row_index_list,
    column_index_list,
    active_flags,
    source_features,
    column_block_index,
):
    channels = source_features.shape[1]
    picked = source_features.reshape(-1, BS, channels)[row_index_list]
    block_product = jnp.einsum(
        "kab,kaf->kbf", local_block_list, picked, preferred_element_type=jnp.float32
    )
    tile_picker = picker_lookup(column_index_list, active_flags, column_block_index)
    reduced_output = jnp.einsum(
        "sj,jop->sop", tile_picker, block_product, precision=lax.Precision.HIGHEST
    )
    return reduced_output.reshape(column_block_index * BS, channels)


def on_device(
    features, weight, bias_terms, blocks, block_rows, block_cols, tile_slot_count, cotangent
):
    own_rows = features.shape[0]
    row_devices = lax.axis_size("row")
    col_devices = lax.axis_size("col")
    row_block_index = own_rows * col_devices // BS
    column_block_index = own_rows * row_devices // BS
    row_index_list = block_rows[:, 0]
    column_index_list = block_cols[:, 0]
    active_flags = (jnp.arange(blocks.shape[0], dtype=jnp.int32) < tile_slot_count[0, 0]).astype(
        jnp.float32
    )
    column_node_range = lax.all_gather(features, "row", axis=0, tiled=True)
    row_partial_sums = per_tile_forward(
        blocks, row_index_list, column_index_list, active_flags, column_node_range, row_block_index
    )
    aggregate = lax.psum_scatter(
        row_partial_sums.astype(jnp.bfloat16), "col", scatter_dimension=0, tiled=True
    )
    preact = jnp.dot(aggregate, weight, preferred_element_type=jnp.float32) + bias_terms
    hidden, pullback = jax.vjp(partial(jax.nn.gelu, approximate=True), preact)
    dpreact = pullback(cotangent.astype(jnp.float32))[0]
    dpreact_b = dpreact.astype(jnp.bfloat16)
    scaling = 1.0 / math.sqrt(own_rows * row_devices * col_devices)
    weight_terms = (
        jnp.einsum("nf,nh->fh", aggregate, dpreact_b, preferred_element_type=jnp.float32) * scaling
    )
    bias_part = jnp.sum(dpreact, axis=0) * scaling
    back = jnp.einsum("nh,fh->nf", dpreact_b, weight, preferred_element_type=jnp.float32).astype(
        jnp.bfloat16
    )
    row_node_range = lax.all_gather(back, "col", axis=0, tiled=True)
    column_partial_sums = per_tile_backward(
        blocks, row_index_list, column_index_list, active_flags, row_node_range, column_block_index
    )
    column_sums, weight_slice, bias_slice = (
        lax.psum_scatter(
            column_partial_sums.astype(jnp.bfloat16), "row", scatter_dimension=0, tiled=True
        ).astype(jnp.float32),
        lax.psum_scatter(
            weight_terms.astype(jnp.bfloat16), "row", scatter_dimension=0, tiled=True
        ).astype(jnp.float32),
        lax.psum_scatter(
            bias_part.astype(jnp.bfloat16), "row", scatter_dimension=0, tiled=True
        ).astype(jnp.float32),
    )
    weight_slice, bias_slice = lax.psum((weight_slice, bias_slice), "col")
    weight_grad, bias_grad = (
        lax.all_gather(weight_slice, "row", axis=0, tiled=True),
        lax.all_gather(bias_slice, "row", axis=0, tiled=True),
    )
    return (hidden.astype(jnp.bfloat16), column_sums, weight_grad, bias_grad)


def solution(mesh):
    return jax.shard_map(
        on_device,
        mesh=mesh,
        in_specs=(
            P(("col", "row"), None),
            P(),
            P(),
            P("row", "col", None),
            P("row", "col"),
            P("row", "col"),
            P("row", "col"),
            P(("row", "col"), None),
        ),
        out_specs=(P(("row", "col"), None), P(("col", "row"), None), P(), P()),
        check_vma=False,
    )
```

profile of v0, /device:TPU:0, one launch (start us, length us, event | category | flops | bytes accessed | tf_op | source)
XLA Modules:
  0.0 228.4 jit_solution(902617862996357713)
XLA Ops:
  7.2 0.7 all-gather.2.cloned.1.call-update
  7.9 0.0 reduce-scatter.4.cloned.1.call-start
  8.6 0.7 fusion.22
  9.3 43.7 %all-gather.2.cloned.1.call-done = bf16[4096,128]{1,0:T(8,128)(2,1)} async-done(((bf16[512,128]{1,0:T(8,128)(2,1)}), bf16[4096,128]{1,0:T(8,128)(2,1)}) %all-gather.2.cloned.1.call-update) | async-done | bytes 1048592 | tf_op jit(solution)/shard_map/all_gather | solution.py:70
  53.0 3.8 %gather_fusion = bf16[80,128,128]{2,1,0:T(8,128)(2,1)} fusion(bf16[32,128,128]{2,1,0:T(8,128)(2,1)} %bitcast.37, s32[1024]{0:T(1024)S(1)} %pad_clamp_fusion.1), kind=kCustom, calls=%fused_computation | custom fusion | bytes 5243200 | tf_op jit(solution)/shard_map/gather | solution.py:26
  56.8 6.0 %convolution_bitcast_fusion.1 = f32[80,128,128]{1,2,0:T(8,128)} fusion(bf16[80,128,128]{2,1,0:T(8,128)(2,1)} %gather_fusion, bf16[80,128,128]{2,1,0:T(8,128)(2,1)S(1)} %copy-done), kind=kOutput, calls=%fused_computation.3 | convolution fusion | flops 335544320 | bytes 10485760 | tf_op jit(solution)/shard_map/kab,kbf->kaf/dot_general | solution.py:27
  62.8 6.4 %copy.19 = f32[80,128,128]{2,0,1:T(8,128)} copy(f32[80,128,128]{1,2,0:T(8,128)} %convolution_bitcast_fusion.1) | data formatting | bytes 10485760 | tf_op jit(solution)/shard_map/kab,kbf->kaf/dot_general | solution.py:27
  69.3 5.1 %convolution_convert_fusion.1 = bf16[16,128,128]{2,0,1:T(8,128)(2,1)S(1)} fusion(f32[80,128,128]{2,0,1:T(8,128)} %copy.19, f32[80]{0:T(128)S(1)} %compare_convert_fusion, s32[80]{0:T(128)S(1)} %bitcast.40), kind=kOutput, calls=%fused_computation.5 | convolution fusion | flops 251922944 | bytes 5767808 | tf_op jit(solution)/shard_map/rk,kaf->raf/dot_general | solution.py:31
  74.3 0.9 copy.20
  75.3 0.0 reduce-scatter.8.cloned.1.call-start
  75.4 20.5 %reduce-scatter.4.cloned.1.call-done = bf16[512,128]{1,0:T(8,128)(2,1)} async-done(((bf16[2048,128]{1,0:T(8,128)(2,1)}), bf16[512,128]{1,0:T(8,128)(2,1)}) %reduce-scatter.4.cloned.1.call-update) | async-done | bytes 131088 | tf_op jit(solution)/shard_map/reduce_scatter | solution.py:74
  95.9 1.9 fusion.26
  97.8 0.2 convolution_convert_fusion.2
  98.0 1.8 fusion
  99.8 0.0 reduce-scatter.6.cloned.1.call-start
  99.8 6.8 %all_gather.13 = bf16[2048,128]{1,0:T(8,128)(2,1)S(1)} all-gather(bf16[512,128]{1,0:T(8,128)(2,1)S(1)} %convolution_convert_fusion.2), channel_id=1, replica_groups=mesh['row'=8,'col'=4] {'col'}, dimensions={0}, use_global_device_ids=true | all-gather | bytes 655360 | tf_op jit(solution)/shard_map/all_gather | solution.py:89
  106.6 2.5 %gather_fusion.1 = bf16[80,128,128]{2,1,0:T(8,128)(2,1)} fusion(bf16[16,128,128]{2,1,0:T(8,128)(2,1)S(1)} %bitcast.36, s32[1024]{0:T(1024)S(1)} %pad_clamp_fusion), kind=kCustom, calls=%fused_computation.1 | custom fusion | bytes 5243200 | tf_op jit(solution)/shard_map/gather | solution.py:46
  109.2 5.1 %convolution_bitcast_fusion = f32[80,128,128]{1,2,0:T(8,128)} fusion(bf16[80,128,128]{2,1,0:T(8,128)(2,1)} %gather_fusion.1, bf16[80,128,128]{2,1,0:T(8,128)(2,1)S(1)} %copy-done), kind=kOutput, calls=%fused_computation.2 | convolution fusion | flops 335544320 | bytes 10485760 | tf_op jit(solution)/shard_map/kab,kaf->kbf/dot_general | solution.py:47
  114.2 6.4 %copy.22 = f32[80,128,128]{2,0,1:T(8,128)} copy(f32[80,128,128]{1,2,0:T(8,128)} %convolution_bitcast_fusion) | data formatting | bytes 10485760 | tf_op jit(solution)/shard_map/kab,kaf->kbf/dot_general | solution.py:47
  120.7 5.1 %convolution_convert_fusion = bf16[32,128,128]{2,0,1:T(8,128)(2,1)S(1)} fusion(f32[80,128,128]{2,0,1:T(8,128)} %copy.22, f32[80]{0:T(128)S(1)} %compare_convert_fusion, s32[80]{0:T(128)S(1)} %bitcast.41), kind=kOutput, calls=%fused_computation.4 | convolution fusion | flops 503845888 | bytes 6292096 | tf_op jit(solution)/shard_map/sj,jop->sop/dot_general | solution.py:51
  125.8 1.4 copy.23
  127.2 0.6 fusion.28
  129.1 21.4 %all-reduce.1 = bf16[128]{0:T(256)(128)(2,1)S(1)} all-reduce(bf16[128]{0:T(256)(128)(2,1)S(1)} %multiply_convert_fusion.1), channel_id=5, replica_groups=mesh['row'=8,'col'=4] {'row'}, use_global_device_ids=true, to_apply=%region_5.0.clone | all-reduce | flops 128 | bytes 512
  150.5 0.1 dynamic-slice_convert_fusion
  150.6 2.8 %reduce-scatter.8.cloned.1.call-done = bf16[16,128]{1,0:T(8,128)(2,1)} async-done(((bf16[128,128]{1,0:T(8,128)(2,1)}), bf16[16,128]{1,0:T(8,128)(2,1)}) %reduce-scatter.8.cloned.1.call-update) | async-done | bytes 4112 | tf_op jit(solution)/shard_map/reduce_scatter | solution.py:97
  153.4 6.0 %all-reduce.2 = (f32[16,128]{1,0:T(8,128)S(1)}, f32[16]{0:T(128)S(1)}) all-reduce(bf16[16,128]{1,0:T(8,128)(2,1)} %reduce-scatter.8.cloned.1.call-done, f32[16]{0:T(128)S(1)} %dynamic-slice_convert_fusion), channel_id=1, replica_groups=mesh['row'=8,'col'=4] {'col'}, use_global_device_ids=true, to_apply=%region_3.0 | all-reduce | flops 2064 | bytes 12416 | tf_op jit(solution)/shard_map/psum | solution.py:104
  159.4 30.7 %all_gather.14 = f32[128,128]{1,0:T(8,128)S(1)} all-gather(f32[16,128]{1,0:T(8,128)S(1)} %get-tuple-element.4), channel_id=1, replica_groups=mesh['row'=8,'col'=4] {'row'}, dimensions={0}, use_global_device_ids=true | all-gather | bytes 73728 | tf_op jit(solution)/shard_map/all_gather | solution.py:106
  190.1 0.2 dynamic-update-slice
  190.3 20.1 %all-reduce = f32[128]{0:T(128)} all-reduce(f32[128]{0:T(128)S(1)} %dynamic-update-slice), channel_id=1, replica_groups=mesh['row'=8,'col'=4] {'row'}, use_global_device_ids=true, to_apply=%add | all-reduce | flops 128 | bytes 1024
  210.4 9.2 %reduce-scatter.6.cloned.1.call-done = bf16[512,128]{1,0:T(8,128)(2,1)} async-done(((bf16[4096,128]{1,0:T(8,128)(2,1)}), bf16[512,128]{1,0:T(8,128)(2,1)}) %reduce-scatter.6.cloned.1.call-update) | async-done | bytes 131088 | tf_op jit(solution)/shard_map/reduce_scatter | solution.py:94
  219.6 1.6 convert_element_type.57
  221.3 0.6 copy.29
  (24 shorter events, 0.2 us)
Async XLA Ops:
  7.2 49.6 %copy-start = (bf16[80,128,128]{2,1,0:T(8,128)(2,1)S(1)}, bf16[80,128,128]{2,1,0:T(8,128)(2,1)}, u32[]{:S(2)}) copy-start(bf16[80,128,128]{2,1,0:T(8,128)(2,1)} %param.11) | copy-start | bytes 7864324
  7.2 45.8 %all-gather.2.cloned.1.call-start = ((), (), s32[]{:S(2)}) async-start(), calls=%async_computation.3 | async-start | bytes 1179648 | tf_op jit(solution)/shard_map/all_gather | solution.py:70
  7.9 88.0 %reduce-scatter.4.cloned.1.call-start = ((), (), s32[]{:S(2)}) async-start(), calls=%async_computation.4 | async-start | bytes 655360 | tf_op jit(solution)/shard_map/reduce_scatter | solution.py:74
  62.8 6.4 %copy-start.3 = (s32[80,1]{0,1:T(1,128)S(1)}, s32[80,1]{0,1:T(1,128)}, u32[]{:S(2)}) copy-start(s32[80,1]{0,1:T(1,128)} %param.12) | copy-start | bytes 964
  69.2 26.6 %copy-start.1 = (bf16[128,128]{1,0:T(8,128)(2,1)S(1)}, bf16[128,128]{1,0:T(8,128)(2,1)}, u32[]{:S(2)}) copy-start(bf16[128,128]{1,0:T(8,128)(2,1)} %param.9) | copy-start | bytes 98308
  69.2 26.6 %copy-start.5 = (bf16[512,128]{1,0:T(8,128)(2,1)S(1)}, bf16[512,128]{1,0:T(8,128)(2,1)}, u32[]{:S(2)}) copy-start(bf16[512,128]{1,0:T(8,128)(2,1)} %param.15) | copy-start | bytes 393220
  69.2 26.6 %copy-start.6 = (f32[128]{0:T(128)S(1)}, f32[128]{0:T(128)}, u32[]{:S(2)}) copy-start(f32[128]{0:T(128)} %param.10) | copy-start | bytes 1540
  75.3 78.1 %reduce-scatter.8.cloned.1.call-start = ((), (), s32[]{:S(2)}) async-start(), calls=%async_computation.6 | async-start | bytes 36864 | tf_op jit(solution)/shard_map/reduce_scatter | solution.py:97
  99.8 119.8 %reduce-scatter.6.cloned.1.call-start = ((), (), s32[]{:S(2)}) async-start(), calls=%async_computation.5 | async-start | bytes 1179648 | tf_op jit(solution)/shard_map/reduce_scatter | solution.py:94
  114.2 6.4 %copy-start.4 = (s32[80,1]{0,1:T(1,128)S(1)}, s32[80,1]{0,1:T(1,128)}, u32[]{:S(2)}) copy-start(s32[80,1]{0,1:T(1,128)} %param.13) | copy-start | bytes 964
  125.8 1.4 copy-start.2
Sparse Core Ops, SparseCore 0:
  10.1 42.8 all-gather.1
  75.4 20.4 reduce-scatter.3
  99.9 53.4 reduce-scatter.7
  157.1 62.5 reduce-scatter.5
where the time goes:
time: 229 us; the launch traced here: 228 us
  blocking collectives  84.9 us (37%)
  waiting for transfers between devices  77 us (34%)
  matrix products  25.1 us (11%)
  local copies, waits for them, and re-layouts  22.9 us (10%)
  between operations  15.8 us (7%)
  other arithmetic  2.39 us (1%)
    all_gather x1, waiting for transfers between devices, on_device(): column_node_range = lax.all_gather(features, 'row', axis=0, tiled=True)  43.7 us
    unnamed x2, blocking collectives  41.5 us
    all_gather x1, blocking collectives, on_device(): lax.all_gather(weight_slice, 'row', axis=0, tiled=True)  30.7 us
    reduce_scatter x1, waiting for transfers between devices, on_device(): lax.psum_scatter(row_partial_sums.astype(jnp.bfloat16), 'col', scatter_di...  20.5 us
    reduce_scatter x1, waiting for transfers between devices, on_device(): lax.psum_scatter(column_partial_sums.astype(jnp.bfloat16), 'row', scatter...  9.24 us
    all_gather x1, blocking collectives, on_device(): row_node_range = lax.all_gather(back, 'col', axis=0, tiled=True)  6.77 us
    dot_general x1, local copies, waits for them, and re-layouts, per_tile_backward(): jnp.einsum('kab,kaf->kbf', local_block_list, picked, preferred_element_ty...  6.44 us
    dot_general x1, local copies, waits for them, and re-layouts, per_tile_forward(): jnp.einsum('kab,kbf->kaf', local_block_list, picked, preferred_element_ty...  6.42 us
  transfers between devices with their start and end apart: 4, of which 4 were waited for; matrix products, arithmetic and copies ran while one was open for 10% of the time, Pallas kernels for 0%

commit v1 on v0

v1 whole, which is shorter than its diff:
```python
from functools import partial
import math

import jax
import jax.numpy as jnp
from jax import lax
from jax.experimental import pallas as pl
from jax.experimental.pallas import tpu as pltpu
from jax.sharding import PartitionSpec as P

BS = 128
C0 = 0.7978845608
C1 = 0.044715
ANY = pl.BlockSpec(memory_space=pl.ANY)
SMEM = pl.BlockSpec(memory_space=pltpu.SMEM)
VMEM = pl.BlockSpec(memory_space=pltpu.VMEM)


def mirror_masks(size):
    masks = []
    while size > 1:
        masks.append(size - 1)
        size //= 2
    return masks


def steps_to(offset, masks):
    steps = []
    for mask in masks:
        if offset & ((mask + 1) >> 1):
            steps.append(mask)
            offset ^= mask
    return steps


def tree(outer, inner, shortcut):
    assert outer & (outer - 1) == 0 and inner & (inner - 1) == 0
    outer_masks, inner_masks = mirror_masks(outer), mirror_masks(inner)
    found = []
    for o in range(outer):
        o_steps = steps_to(o, outer_masks)
        for i in range(inner):
            i_steps = steps_to(i, inner_masks)
            if o == 0 and i == 0:
                continue
            if i and not (shortcut and o == 1):
                parent = (o, i ^ i_steps[-1])
            else:
                parent = (o ^ o_steps[-1], i)
            depth = len(o_steps) + len(i_steps)
            found.append((depth, o * inner + i, parent[0] * inner + parent[1]))
    found.sort()
    return [(offset, parent) for _, offset, parent in found]


def row_tree(size):
    inner = 1
    while 2 * (2 * inner) * (2 * inner) <= size:
        inner *= 2
    return tree(size // inner, inner, True)


def col_tree(size):
    return tree(size // 2, 2, False)


def swap(x, axis, mask):
    size = lax.axis_size(axis)
    return lax.ppermute(x, axis, [(i, i ^ mask) for i in range(size)])


def spread(x, axis, routes):
    pieces = {0: x}
    for offset, parent in routes:
        pieces[offset] = swap(pieces[parent], axis, offset ^ parent)
    return [pieces[d] for d in range(len(pieces))]


def collect(pieces, axis, routes):
    terms = {d: [p] for d, p in enumerate(pieces)}
    for offset, parent in reversed(routes):
        total = terms[offset][0].astype(jnp.float32)
        for other in terms[offset][1:]:
            total = total + other.astype(jnp.float32)
        terms[parent].append(swap(total.astype(jnp.bfloat16), axis, offset ^ parent))
    return terms[0]


def unroll_of(slots):
    for u in (8, 4, 2):
        if slots % u == 0:
            return u
    return 1


def sparse_kernel(slots, count, per, transposed, idx, blocks, *refs):
    pieces, refs = refs[:count], refs[count:]
    outs, (held, source, total, piece_sem, block_sem) = refs[:-5], refs[-5:]
    here, there = idx[2 * slots + 1], idx[2 * slots + 2]
    live = idx[2 * slots]
    unroll = unroll_of(slots)
    copies = []
    for d in range(count):
        at = pl.multiple_of(lax.bitwise_xor(here, d) * per, per)
        copies.append(
            pltpu.make_async_copy(pieces[d], source.at[pl.ds(at, per)], piece_sem.at[d])
        )
    block_copy = pltpu.make_async_copy(blocks, held, block_sem)
    block_copy.start()
    for copy in copies:
        copy.start()
    sinks = total.shape[0] - 1
    total[...] = jnp.zeros_like(total)
    for copy in copies:
        copy.wait()
    block_copy.wait()

    def step(i, carry):
        products, targets = [], []
        for u in range(unroll):
            k = i * unroll + u
            row, col = idx[k], idx[slots + k]
            if transposed:
                products.append(
                    jnp.dot(source[row], held[k], preferred_element_type=jnp.float32)
                )
                target = col
            else:
                products.append(
                    jnp.dot(held[k], source[col], preferred_element_type=jnp.float32)
                )
                target = row
            targets.append(jnp.where(k < live, target, sinks))
        for product, target in zip(products, targets):
            total[target] = total[target] + product
        return carry

    lax.fori_loop(0, lax.div(live + unroll - 1, unroll), step, 0)
    for d, out in enumerate(outs):
        at = lax.bitwise_xor(there, d) * out.shape[0]
        out[...] = total[pl.ds(at, out.shape[0])].astype(out.dtype)


def sparse(idx, blocks, pieces, out_count, targets, transposed):
    slots = blocks.shape[0]
    count, per = len(pieces), pieces[0].shape[0]
    out_per = targets // out_count
    block = blocks.shape[1:]
    out_shape = [
        jax.ShapeDtypeStruct((out_per,) + block, jnp.float32 if d == 0 else jnp.bfloat16)
        for d in range(out_count)
    ]
    flops = 2 * slots * BS * BS * BS
    size = 2 * BS * BS
    need = size * (slots + count * per + 2 * (targets + 1) + targets + out_per) + (4 << 20)
    return pl.pallas_call(
        partial(sparse_kernel, slots, count, per, transposed),
        out_shape=out_shape,
        in_specs=[SMEM, ANY] + [ANY] * count,
        out_specs=[VMEM] * out_count,
        scratch_shapes=[
            pltpu.VMEM(blocks.shape, blocks.dtype),
            pltpu.VMEM((count * per,) + block, jnp.bfloat16),
            pltpu.VMEM((targets + 1,) + block, jnp.float32),
            pltpu.SemaphoreType.DMA((count,)),
            pltpu.SemaphoreType.DMA,
        ],
        compiler_params=pltpu.CompilerParams(vmem_limit_bytes=need),
        cost_estimate=pl.CostEstimate(
            flops=flops, bytes_accessed=size * (slots + count * per), transcendentals=0
        ),
    )(idx, blocks, *pieces)


def dense_kernel(scaling, terms, *refs):
    parts, refs = refs[:terms], refs[terms:]
    weight, bias, cotangent, hidden, back, weight_terms, bias_terms = refs
    rows = cotangent.shape[0]
    aggregate = parts[0][...].astype(jnp.float32)
    for part in parts[1:]:
        aggregate = aggregate + part[...].astype(jnp.float32)
    aggregate_b = aggregate.astype(jnp.bfloat16).reshape(rows, aggregate.shape[-1])
    v = jnp.dot(aggregate_b, weight[...], preferred_element_type=jnp.float32) + bias[...]
    square = v * v
    t = jnp.tanh(C0 * (v + C1 * (v * square)))
    half = 0.5 * (1.0 + t)
    hidden[...] = (v * half).astype(jnp.bfloat16)
    slope = half + (0.5 * v) * (1.0 - t * t) * (C0 * (1.0 + (3.0 * C1) * square))
    dpreact = cotangent[...].astype(jnp.float32) * slope
    dpreact_b = dpreact.astype(jnp.bfloat16)
    for n in range(rows // BS):
        back[n] = lax.dot_general(
            weight[...],
            dpreact_b[n * BS : (n + 1) * BS],
            (((1,), (1,)), ((), ())),
            preferred_element_type=jnp.float32,
        ).astype(jnp.bfloat16)
    weight_terms[...] = scaling * lax.dot_general(
        aggregate_b, dpreact_b, (((0,), (0,)), ((), ())), preferred_element_type=jnp.float32
    )
    bias_terms[...] = jnp.broadcast_to(
        scaling * jnp.sum(dpreact, axis=0, keepdims=True), bias_terms.shape
    )


def dense(parts, weight, bias, cotangent, scaling):
    rows, channels = cotangent.shape[0], weight.shape[0]
    return pl.pallas_call(
        partial(dense_kernel, scaling, len(parts)),
        out_shape=[
            jax.ShapeDtypeStruct(cotangent.shape, jnp.bfloat16),
            jax.ShapeDtypeStruct((rows // BS, channels, BS), jnp.bfloat16),
            jax.ShapeDtypeStruct(weight.shape, jnp.float32),
            jax.ShapeDtypeStruct((8, weight.shape[1]), jnp.float32),
        ],
        in_specs=[VMEM] * (len(parts) + 3),
        out_specs=[VMEM] * 4,
        compiler_params=pltpu.CompilerParams(vmem_limit_bytes=24 << 20),
        cost_estimate=pl.CostEstimate(
            flops=6 * rows * BS * BS, bytes_accessed=1 << 20, transcendentals=rows * BS
        ),
    )(*parts, weight, bias, cotangent)


def finish_kernel(*refs):
    parts, out = refs[:-1], refs[-1]
    for n in range(parts[0].shape[0]):
        total = parts[0][n].astype(jnp.float32)
        for part in parts[1:]:
            total = total + part[n].astype(jnp.float32)
        out[n * BS : (n + 1) * BS] = total.T


def finish(parts):
    per, channels, nodes = parts[0].shape
    return pl.pallas_call(
        finish_kernel,
        out_shape=jax.ShapeDtypeStruct((per * nodes, channels), jnp.float32),
        in_specs=[VMEM] * len(parts),
        out_specs=VMEM,
        compiler_params=pltpu.CompilerParams(vmem_limit_bytes=16 << 20),
    )(*parts)


def on_device(
    features, weight, bias_terms, blocks, block_rows, block_cols, tile_slot_count, cotangent
):
    own_rows, channels = features.shape
    row_devices, col_devices = lax.axis_size("row"), lax.axis_size("col")
    own_blocks = own_rows // BS
    row_blocks, column_blocks = own_blocks * col_devices, own_blocks * row_devices
    on_row, on_col = row_tree(row_devices), col_tree(col_devices)
    row_at = lax.axis_index("row").astype(jnp.int32)
    col_at = lax.axis_index("col").astype(jnp.int32)
    slots = jnp.concatenate([block_rows[:, 0], block_cols[:, 0], tile_slot_count[0]])
    idx_forward = jnp.concatenate([slots, jnp.stack([row_at, col_at])])
    idx_backward = jnp.concatenate([slots, jnp.stack([col_at, row_at])])

    own = features.reshape(own_blocks, BS, channels)
    columns = spread(own, "row", on_row)
    partial_sums = sparse(idx_forward, blocks, columns, col_devices, row_blocks, False)
    parts = collect(partial_sums, "col", on_col)

    scaling = 1.0 / math.sqrt(own_rows * row_devices * col_devices)
    hidden, back, weight_part, bias_part = dense(
        parts, weight, bias_terms.reshape(1, -1), cotangent, scaling
    )
    rows = spread(back, "col", on_col)
    gradient_sums = sparse(idx_backward, blocks, rows, row_devices, column_blocks, True)
    feat_grad = finish(collect(gradient_sums, "row", on_row))

    grads = jnp.concatenate([weight_part, bias_part], axis=0)
    for axis, masks in (("col", col_devices), ("row", row_devices)):
        mask = 1
        while mask < masks:
            grads = grads + swap(grads, axis, mask)
            mask *= 2
    return hidden, feat_grad, grads[:channels], grads[channels]


def solution(mesh):
    return jax.shard_map(
        on_device,
        mesh=mesh,
        in_specs=(
            P(("col", "row"), None),
            P(),
            P(),
            P("row", "col", None),
            P("row", "col"),
            P("row", "col"),
            P("row", "col"),
            P(("row", "col"), None),
        ),
        out_specs=(P(("row", "col"), None), P(("col", "row"), None), P(), P()),
        check_vma=False,
    )
```

time: 229 us -> 74.5 us (0.33)
  blocking collectives: 84.9 us -> 0 us
  waiting for transfers between devices: 77 us -> 29 us
  starting transfers between devices: 0.16 us -> 32.8 us
  matrix products: 25.1 us -> 0 us
  local copies, waits for them, and re-layouts: 22.9 us -> 4.7 us
  between operations: 15.8 us -> 1.41 us
  Pallas kernels: 0 us -> 6.76 us
    all_gather x1 -> x0, waiting for transfers between devices: 43.7 us -> none  [on_device(): column_node_range = lax.all_gather(features, 'row', axis=0, tiled=True)]
    unnamed x2 -> x0, blocking collectives: 41.5 us -> none
    all_gather x2 -> x0, blocking collectives: 37.5 us -> none  [the longest x1 30.7 us: on_device(): lax.all_gather(weight_slice, 'row', axis=0, tiled=True)]
    ppermute x0 -> x25, starting transfers between devices: none -> 32.8 us  [swap(): return lax.ppermute(x, axis, [(i, i ^ mask) for i in range(size)])]
    reduce_scatter x3 -> x0, waiting for transfers between devices: 32.6 us -> none  [the longest x1 20.5 us: on_device(): lax.psum_scatter(row_partial_sums.astype(jnp.bfloat16), 'col', scatter_di...]
    ppermute x0 -> x25, waiting for transfers between devices: none -> 29 us  [swap(): return lax.ppermute(x, axis, [(i, i ^ mask) for i in range(size)])]
    dot_general x7 -> x0, matrix products: 25.1 us -> none  [the longest x1 6.02 us: per_tile_forward(): jnp.einsum('kab,kbf->kaf', local_block_list, picked, preferred_element_ty...]
    dot_general x2 -> x0, local copies, waits for them, and re-layouts: 12.9 us -> none  [the longest x1 6.44 us: per_tile_backward(): jnp.einsum('kab,kaf->kbf', local_block_list, picked, preferred_element_ty...]
  transfers between devices with their start and end apart: 4 -> 25, of which waited for: 4 -> 15; matrix products, arithmetic and copies ran while one was open for 10% -> 3% of each run, Pallas kernels for 0% -> 3%
where the time goes in v1:
time: 74.5 us; the launch traced here: 74.9 us
  starting transfers between devices  32.8 us (44%)
  waiting for transfers between devices  29 us (39%)
  Pallas kernels  6.76 us (9%)
  local copies, waits for them, and re-layouts  4.7 us (6%)
  between operations  1.41 us (2%)
    ppermute x25, starting transfers between devices, swap(): return lax.ppermute(x, axis, [(i, i ^ mask) for i in range(size)])  32.8 us
    ppermute x25, waiting for transfers between devices, swap(): return lax.ppermute(x, axis, [(i, i ^ mask) for i in range(size)])  29 us
    pallas_call x2, Pallas kernels, sparse(): pl.pallas_call(partial(sparse_kernel, slots, count, per, transposed), out...  4.94 us
    unnamed x17, local copies, waits for them, and re-layouts  2.67 us
  transfers between devices with their start and end apart: 25, of which 15 were waited for; matrix products, arithmetic and copies ran while one was open for 3% of the time, Pallas kernels for 3%

profile of v1, /device:TPU:0, one launch (start us, length us, event | category | flops | bytes accessed | tf_op | source)
XLA Modules:
  0.0 74.9 jit_solution(8097088457452797170)
XLA Ops:
  0.6 5.1 %collective-permute-start.3 = (bf16[4,128,128]{2,1,0:T(8,128)(2,1)}, bf16[4,128,128]{2,1,0:T(8,128)(2,1)S(1)}, u32[]{:S(2)}, u32[]{:S(2)}) collective-permute-start(bf16[4,128,128]{2,1,0:T(8,128)(2,1)} %bitcast.11), channel_id=1, source_target_pairs={{0,24},{4,28},{8,16},{12,20},{16,8},{20,12},{24,0},{28,4},{1,25},{... | collective-permute-start | bytes 393224 | tf_op jit(solution)/shard_map/ppermute | solution.py:69
  5.8 1.5 %collective-permute-start = (bf16[4,128,128]{2,1,0:T(8,128)(2,1)}, bf16[4,128,128]{2,1,0:T(8,128)(2,1)S(1)}, u32[]{:S(2)}, u32[]{:S(2)}) collective-permute-start(bf16[4,128,128]{2,1,0:T(8,128)(2,1)} %bitcast.12), channel_id=1, source_target_pairs={{0,4},{4,0},{8,12},{12,8},{16,20},{20,16},{24,28},{28,24},{1,5},{5... | collective-permute-start | bytes 393224 | tf_op jit(solution)/shard_map/ppermute | solution.py:69
  7.2 2.3 %collective-permute-done.3.refs_6_ = bf16[4,128,128]{2,1,0:T(8,128)(2,1)S(1)} collective-permute-done((bf16[4,128,128]{2,1,0:T(8,128)(2,1)}, bf16[4,128,128]{2,1,0:T(8,128)(2,1)S(1)}, u32[]{:S(2)}, u32[]{:S(2)}) %collective-permute-start.3) | collective-permute-done | bytes 131104 | tf_op jit(solution)/shard_map/ppermute | solution.py:69
  9.6 2.4 %collective-permute-start.4 = (bf16[4,128,128]{2,1,0:T(8,128)(2,1)S(1)}, bf16[4,128,128]{2,1,0:T(8,128)(2,1)S(1)}, u32[]{:S(2)}, u32[]{:S(2)}) collective-permute-start(bf16[4,128,128]{2,1,0:T(8,128)(2,1)S(1)} %collective-permute-done.3.refs_6_), channel_id=1, source_target_pairs={{0,8},{4,12},{8,0},{12,4},{16,24},{20,28},{24,16},{28,20},{1,9},{5... | collective-permute-start | bytes 393224 | tf_op jit(solution)/shard_map/ppermute | solution.py:69
  12.0 1.5 %collective-permute-start.6 = (bf16[4,128,128]{2,1,0:T(8,128)(2,1)S(1)}, bf16[4,128,128]{2,1,0:T(8,128)(2,1)S(1)}, u32[]{:S(2)}, u32[]{:S(2)}) collective-permute-start(bf16[4,128,128]{2,1,0:T(8,128)(2,1)S(1)} %collective-permute-done.3.refs_6_), channel_id=1, source_target_pairs={{0,4},{4,0},{8,12},{12,8},{16,20},{20,16},{24,28},{28,24},{1,5},{5... | collective-permute-start | bytes 393224 | tf_op jit(solution)/shard_map/ppermute | solution.py:69
  13.5 2.0 %collective-permute-start.2 = (bf16[4,128,128]{2,1,0:T(8,128)(2,1)S(1)}, bf16[4,128,128]{2,1,0:T(8,128)(2,1)S(1)}, u32[]{:S(2)}, u32[]{:S(2)}) collective-permute-start(bf16[4,128,128]{2,1,0:T(8,128)(2,1)S(1)} %collective-permute-done.refs_1_), channel_id=1, source_target_pairs={{0,8},{4,12},{8,0},{12,4},{16,24},{20,28},{24,16},{28,20},{1,9},{5... | collective-permute-start | bytes 393224 | tf_op jit(solution)/shard_map/ppermute | solution.py:69
  16.2 1.5 %collective-permute-start.5 = (bf16[4,128,128]{2,1,0:T(8,128)(2,1)S(1)}, bf16[4,128,128]{2,1,0:T(8,128)(2,1)S(1)}, u32[]{:S(2)}, u32[]{:S(2)}) collective-permute-start(bf16[4,128,128]{2,1,0:T(8,128)(2,1)S(1)} %collective-permute-done.4.refs_4_), channel_id=1, source_target_pairs={{0,4},{4,0},{8,12},{12,8},{16,20},{20,16},{24,28},{28,24},{1,5},{5... | collective-permute-start | bytes 393224 | tf_op jit(solution)/shard_map/ppermute | solution.py:69
  19.2 1.4 %collective-permute-done.2.refs_3_ = bf16[4,128,128]{2,1,0:T(8,128)(2,1)S(1)} collective-permute-done((bf16[4,128,128]{2,1,0:T(8,128)(2,1)S(1)}, bf16[4,128,128]{2,1,0:T(8,128)(2,1)S(1)}, u32[]{:S(2)}, u32[]{:S(2)}) %collective-permute-start.2) | collective-permute-done | bytes 131104 | tf_op jit(solution)/shard_map/ppermute | solution.py:69
  21.2 1.7 %copy-done = bf16[80,128,128]{2,1,0:T(8,128)(2,1)S(1)} copy-done((bf16[80,128,128]{2,1,0:T(8,128)(2,1)S(1)}, bf16[80,128,128]{2,1,0:T(8,128)(2,1)}, u32[]{:S(2)}) %copy-start) | copy-done | bytes 2621464
  22.9 0.9 %copy-done.2 = bf16[512,128]{1,0:T(8,128)(2,1)S(1)} copy-done((bf16[512,128]{1,0:T(8,128)(2,1)S(1)}, bf16[512,128]{1,0:T(8,128)(2,1)}, u32[]{:S(2)}) %copy-start.2) | copy-done | bytes 131096
  23.8 2.8 %shard_map.111 = (f32[4,128,128]{2,1,0:T(8,128)S(1)}, bf16[4,128,128]{2,1,0:T(8,128)(2,1)S(1)}, bf16[4,128,128]{2,1,0:T(8,128)(2,1)S(1)}, bf16[4,128,128]{2,1,0:T(8,128)(2,1)S(1)}) custom-call(s32[163]{0:T(256)S(1)} %concatenate.12.idx, bf16[80,128,128]{2,1,0:T(8,128)(2,1)S(1)} %copy-done, bf16[4,128,128]{2,1,0:T(8,128)(2,1)S(1)} %bitcast.14, ...), custom_call_target="tpu_custom_call" | custom-call | flops 335544320 | bytes 3670016 | tf_op jit(solution)/shard_map/pallas_call | solution.py:156
  27.2 0.8 %collective-permute-done.7 = bf16[4,128,128]{2,1,0:T(8,128)(2,1)S(1)} collective-permute-done((bf16[4,128,128]{2,1,0:T(8,128)(2,1)S(1)}, bf16[4,128,128]{2,1,0:T(8,128)(2,1)S(1)}, u32[]{:S(2)}, u32[]{:S(2)}) %collective-permute-start.7) | collective-permute-done | bytes 131104 | tf_op jit(solution)/shard_map/ppermute | solution.py:69
  28.1 3.5 %collective-permute-start.8 = (bf16[4,128,128]{2,1,0:T(8,128)(2,1)S(1)}, bf16[4,128,128]{2,1,0:T(8,128)(2,1)S(1)}, u32[]{:S(2)}, u32[]{:S(2)}) collective-permute-start(bf16[4,128,128]{2,1,0:T(8,128)(2,1)S(1)} %add_convert_fusion.3), channel_id=1, source_target_pairs={{0,2},{1,3},{2,0},{3,1},{4,6},{5,7},{6,4},{7,5},{8,10},{9,11},{10,... | collective-permute-start | bytes 393224 | tf_op jit(solution)/shard_map/ppermute | solution.py:69
  31.5 3.8 %collective-permute-done.8.refs_1_ = bf16[4,128,128]{2,1,0:T(8,128)(2,1)S(1)} collective-permute-done((bf16[4,128,128]{2,1,0:T(8,128)(2,1)S(1)}, bf16[4,128,128]{2,1,0:T(8,128)(2,1)S(1)}, u32[]{:S(2)}, u32[]{:S(2)}) %collective-permute-start.8) | collective-permute-done | bytes 131104 | tf_op jit(solution)/shard_map/ppermute | solution.py:69
  35.4 1.0 %shard_map.112 = (bf16[512,128]{1,0:T(8,128)(2,1)}, bf16[4,128,128]{2,1,0:T(8,128)(2,1)S(1)}, f32[128,128]{1,0:T(8,128)S(1)}, f32[8,128]{1,0:T(8,128)S(1)}) custom-call(f32[4,128,128]{2,1,0:T(8,128)S(1)} %get-tuple-element.20.refs_0_, bf16[4,128,128]{2,1,0:T(8,128)(2,1)S(1)} %collective-permute-done.8.refs_1_, ...), custom_call_target="tpu_custom_call" | custom-call | flops 50331648 | bytes 1048576 | tf_op jit(solution)/shard_map/pallas_call | solution.py:208
  36.3 1.7 %collective-permute-start.11 = (bf16[4,128,128]{2,1,0:T(8,128)(2,1)S(1)}, bf16[4,128,128]{2,1,0:T(8,128)(2,1)S(1)}, u32[]{:S(2)}, u32[]{:S(2)}) collective-permute-start(bf16[4,128,128]{2,1,0:T(8,128)(2,1)S(1)} %get-tuple-element.25.refs_0_), channel_id=1, source_target_pairs={{0,2},{1,3},{2,0},{3,1},{4,6},{5,7},{6,4},{7,5},{8,10},{9,11},{10,... | collective-permute-start | bytes 393224 | tf_op jit(solution)/shard_map/ppermute | solution.py:69
  38.1 1.3 %collective-permute-done.20 = f32[136,128]{1,0:T(8,128)S(1)} collective-permute-done((f32[136,128]{1,0:T(8,128)S(1)}, f32[136,128]{1,0:T(8,128)S(1)}, u32[]{:S(2)}, u32[]{:S(2)}) %collective-permute-start.20) | collective-permute-done | bytes 69664 | tf_op jit(solution)/shard_map/ppermute | solution.py:69
  39.7 1.7 %collective-permute-done.11.refs_2_ = bf16[4,128,128]{2,1,0:T(8,128)(2,1)S(1)} collective-permute-done((bf16[4,128,128]{2,1,0:T(8,128)(2,1)S(1)}, bf16[4,128,128]{2,1,0:T(8,128)(2,1)S(1)}, u32[]{:S(2)}, u32[]{:S(2)}) %collective-permute-start.11) | collective-permute-done | bytes 131104 | tf_op jit(solution)/shard_map/ppermute | solution.py:69
  41.4 2.3 %collective-permute-done.21 = f32[136,128]{1,0:T(8,128)S(1)} collective-permute-done((f32[136,128]{1,0:T(8,128)S(1)}, f32[136,128]{1,0:T(8,128)S(1)}, u32[]{:S(2)}, u32[]{:S(2)}) %collective-permute-start.21) | collective-permute-done | bytes 69664 | tf_op jit(solution)/shard_map/ppermute | solution.py:69
  43.8 0.8 %collective-permute-start.22 = (f32[136,128]{1,0:T(8,128)S(1)}, f32[136,128]{1,0:T(8,128)S(1)}, u32[]{:S(2)}, u32[]{:S(2)}) collective-permute-start(f32[136,128]{1,0:T(8,128)S(1)} %add.36), channel_id=1, source_target_pairs={{0,4},{4,0},{8,12},{12,8},{16,20},{20,16},{24,28},{28,24},{1,5},{5... | collective-permute-start | bytes 208904 | tf_op jit(solution)/shard_map/ppermute | solution.py:69
  44.7 3.4 %collective-permute-done.22 = f32[136,128]{1,0:T(8,128)S(1)} collective-permute-done((f32[136,128]{1,0:T(8,128)S(1)}, f32[136,128]{1,0:T(8,128)S(1)}, u32[]{:S(2)}, u32[]{:S(2)}) %collective-permute-start.22) | collective-permute-done | bytes 69664 | tf_op jit(solution)/shard_map/ppermute | solution.py:69
  48.1 1.8 %collective-permute-start.23 = (f32[136,128]{1,0:T(8,128)S(1)}, f32[136,128]{1,0:T(8,128)S(1)}, u32[]{:S(2)}, u32[]{:S(2)}) collective-permute-start(f32[136,128]{1,0:T(8,128)S(1)} %add.37), channel_id=1, source_target_pairs={{0,8},{4,12},{8,0},{12,4},{16,24},{20,28},{24,16},{28,20},{1,9},{5... | collective-permute-start | bytes 208904 | tf_op jit(solution)/shard_map/ppermute | solution.py:69
  49.9 2.2 %shard_map.113 = (f32[4,128,128]{2,1,0:T(8,128)S(1)}, bf16[4,128,128]{2,1,0:T(8,128)(2,1)S(1)}, bf16[4,128,128]{2,1,0:T(8,128)(2,1)S(1)}, bf16[4,128,128]{2,1,0:...) custom-call(s32[163]{0:T(256)S(1)} %concatenate.13.idx, ...), custom_call_target="tpu_custom_call" | custom-call | flops 335544320 | bytes 3145728 | tf_op jit(solution)/shard_map/pallas_call | solution.py:156
  52.1 3.9 %collective-permute-start.14 = (bf16[4,128,128]{2,1,0:T(8,128)(2,1)S(1)}, bf16[4,128,128]{2,1,0:T(8,128)(2,1)S(1)}, u32[]{:S(2)}, u32[]{:S(2)}) collective-permute-start(bf16[4,128,128]{2,1,0:T(8,128)(2,1)S(1)} %get-tuple-element.30), channel_id=1, source_target_pairs={{0,4},{4,0},{8,12},{12,8},{16,20},{20,16},{24,28},{28,24},{1,5},{5... | collective-permute-start | bytes 393224 | tf_op jit(solution)/shard_map/ppermute | solution.py:69
  56.2 3.4 %collective-permute-start.17 = (bf16[4,128,128]{2,1,0:T(8,128)(2,1)S(1)}, bf16[4,128,128]{2,1,0:T(8,128)(2,1)S(1)}, u32[]{:S(2)}, u32[]{:S(2)}) collective-permute-start(bf16[4,128,128]{2,1,0:T(8,128)(2,1)S(1)} %get-tuple-element.31), channel_id=1, source_target_pairs={{0,8},{4,12},{8,0},{12,4},{16,24},{20,28},{24,16},{28,20},{1,9},{5... | collective-permute-start | bytes 393224 | tf_op jit(solution)/shard_map/ppermute | solution.py:69
  59.6 1.8 %collective-permute-done.24 = f32[136,128]{1,0:T(8,128)S(1)} collective-permute-done((f32[136,128]{1,0:T(8,128)S(1)}, f32[136,128]{1,0:T(8,128)S(1)}, u32[]{:S(2)}, u32[]{:S(2)}) %collective-permute-start.24) | collective-permute-done | bytes 69664 | tf_op jit(solution)/shard_map/ppermute | solution.py:69
  62.4 2.9 %collective-permute-done.18 = bf16[4,128,128]{2,1,0:T(8,128)(2,1)S(1)} collective-permute-done((bf16[4,128,128]{2,1,0:T(8,128)(2,1)S(1)}, bf16[4,128,128]{2,1,0:T(8,128)(2,1)S(1)}, u32[]{:S(2)}, u32[]{:S(2)}) %collective-permute-start.18) | collective-permute-done | bytes 131104 | tf_op jit(solution)/shard_map/ppermute | solution.py:69
  65.8 1.3 %collective-permute-done.15 = bf16[4,128,128]{2,1,0:T(8,128)(2,1)S(1)} collective-permute-done((bf16[4,128,128]{2,1,0:T(8,128)(2,1)S(1)}, bf16[4,128,128]{2,1,0:T(8,128)(2,1)S(1)}, u32[]{:S(2)}, u32[]{:S(2)}) %collective-permute-start.15) | collective-permute-done | bytes 131104 | tf_op jit(solution)/shard_map/ppermute | solution.py:69
  67.2 1.7 %collective-permute-start.16 = (bf16[4,128,128]{2,1,0:T(8,128)(2,1)S(1)}, bf16[4,128,128]{2,1,0:T(8,128)(2,1)S(1)}, u32[]{:S(2)}, u32[]{:S(2)}) collective-permute-start(bf16[4,128,128]{2,1,0:T(8,128)(2,1)S(1)} %add_convert_fusion.1), channel_id=1, source_target_pairs={{0,24},{4,28},{8,16},{12,20},{16,8},{20,12},{24,0},{28,4},{1,25},{... | collective-permute-start | bytes 393224 | tf_op jit(solution)/shard_map/ppermute | solution.py:69
  69.4 0.9 %collective-permute-done.19.refs_3_ = bf16[4,128,128]{2,1,0:T(8,128)(2,1)S(1)} collective-permute-done((bf16[4,128,128]{2,1,0:T(8,128)(2,1)S(1)}, bf16[4,128,128]{2,1,0:T(8,128)(2,1)S(1)}, u32[]{:S(2)}, u32[]{:S(2)}) %collective-permute-start.19) | collective-permute-done | bytes 131104 | tf_op jit(solution)/shard_map/ppermute | solution.py:69
  70.4 3.7 %collective-permute-done.16.refs_1_ = bf16[4,128,128]{2,1,0:T(8,128)(2,1)S(1)} collective-permute-done((bf16[4,128,128]{2,1,0:T(8,128)(2,1)S(1)}, bf16[4,128,128]{2,1,0:T(8,128)(2,1)S(1)}, u32[]{:S(2)}, u32[]{:S(2)}) %collective-permute-start.16) | collective-permute-done | bytes 131104 | tf_op jit(solution)/shard_map/ppermute | solution.py:69
  74.0 0.8 %shard_map.114 = f32[512,128]{1,0:T(8,128)} custom-call(f32[4,128,128]{2,1,0:T(8,128)S(1)} %get-tuple-element.26.refs_0_, bf16[4,128,128]{2,1,0:T(8,128)(2,1)S(1)} %collective-permute-done.16.refs_1_, bf16[4,128,128]{2,1,0:T(8,128)(2,1)S(1)} %collective-permute-done.17.refs_2_, bf16[4,128,128]{2,1,0:T(8,128)(2,1)S(1)} %collective-permute-done.19.refs_3_), custom_call_target="tpu_custom_call" | custom-call | tf_op jit(solution)/shard_map/pallas_call | solution.py:236
  (53 shorter events, 5.5 us)
Async XLA Ops:
  0.6 34.7 %copy-start.5 = (f32[128]{0:T(128)S(1)}, f32[128]{0:T(128)}, u32[]{:S(2)}) copy-start(f32[128]{0:T(128)} %param.10) | copy-start | bytes 1540
  0.6 8.9 %collective-permute-start.3 = (bf16[4,128,128]{2,1,0:T(8,128)(2,1)}, bf16[4,128,128]{2,1,0:T(8,128)(2,1)S(1)}, u32[]{:S(2)}, u32[]{:S(2)}) collective-permute-start(bf16[4,128,128]{2,1,0:T(8,128)(2,1)} %bitcast.11), channel_id=1, source_target_pairs={{0,24},{4,28},{8,16},{12,20},{16,8},{20,12},{24,0},{28,4},{1,25},{... | collective-permute-start | bytes 393224 | tf_op jit(solution)/shard_map/ppermute | solution.py:69
  5.8 7.8 %collective-permute-start = (bf16[4,128,128]{2,1,0:T(8,128)(2,1)}, bf16[4,128,128]{2,1,0:T(8,128)(2,1)S(1)}, u32[]{:S(2)}, u32[]{:S(2)}) collective-permute-start(bf16[4,128,128]{2,1,0:T(8,128)(2,1)} %bitcast.12), channel_id=1, source_target_pairs={{0,4},{4,0},{8,12},{12,8},{16,20},{20,16},{24,28},{28,24},{1,5},{5... | collective-permute-start | bytes 393224 | tf_op jit(solution)/shard_map/ppermute | solution.py:69
  9.6 6.6 %collective-permute-start.4 = (bf16[4,128,128]{2,1,0:T(8,128)(2,1)S(1)}, bf16[4,128,128]{2,1,0:T(8,128)(2,1)S(1)}, u32[]{:S(2)}, u32[]{:S(2)}) collective-permute-start(bf16[4,128,128]{2,1,0:T(8,128)(2,1)S(1)} %collective-permute-done.3.refs_6_), channel_id=1, source_target_pairs={{0,8},{4,12},{8,0},{12,4},{16,24},{20,28},{24,16},{28,20},{1,9},{5... | collective-permute-start | bytes 393224 | tf_op jit(solution)/shard_map/ppermute | solution.py:69
  12.0 7.2 %collective-permute-start.1 = (bf16[4,128,128]{2,1,0:T(8,128)(2,1)}, bf16[4,128,128]{2,1,0:T(8,128)(2,1)S(1)}, u32[]{:S(2)}, u32[]{:S(2)}) collective-permute-start(bf16[4,128,128]{2,1,0:T(8,128)(2,1)} %bitcast.13), channel_id=1, source_target_pairs={{0,8},{4,12},{8,0},{12,4},{16,24},{20,28},{24,16},{28,20},{1,9},{5... | collective-permute-start | bytes 393224 | tf_op jit(solution)/shard_map/ppermute | solution.py:69
  12.0 7.2 %collective-permute-start.6 = (bf16[4,128,128]{2,1,0:T(8,128)(2,1)S(1)}, bf16[4,128,128]{2,1,0:T(8,128)(2,1)S(1)}, u32[]{:S(2)}, u32[]{:S(2)}) collective-permute-start(bf16[4,128,128]{2,1,0:T(8,128)(2,1)S(1)} %collective-permute-done.3.refs_6_), channel_id=1, source_target_pairs={{0,4},{4,0},{8,12},{12,8},{16,20},{20,16},{24,28},{28,24},{1,5},{5... | collective-permute-start | bytes 393224 | tf_op jit(solution)/shard_map/ppermute | solution.py:69
  13.5 7.0 %collective-permute-start.2 = (bf16[4,128,128]{2,1,0:T(8,128)(2,1)S(1)}, bf16[4,128,128]{2,1,0:T(8,128)(2,1)S(1)}, u32[]{:S(2)}, u32[]{:S(2)}) collective-permute-start(bf16[4,128,128]{2,1,0:T(8,128)(2,1)S(1)} %collective-permute-done.refs_1_), channel_id=1, source_target_pairs={{0,8},{4,12},{8,0},{12,4},{16,24},{20,28},{24,16},{28,20},{1,9},{5... | collective-permute-start | bytes 393224 | tf_op jit(solution)/shard_map/ppermute | solution.py:69
  16.2 5.0 %collective-permute-start.5 = (bf16[4,128,128]{2,1,0:T(8,128)(2,1)S(1)}, bf16[4,128,128]{2,1,0:T(8,128)(2,1)S(1)}, u32[]{:S(2)}, u32[]{:S(2)}) collective-permute-start(bf16[4,128,128]{2,1,0:T(8,128)(2,1)S(1)} %collective-permute-done.4.refs_4_), channel_id=1, source_target_pairs={{0,4},{4,0},{8,12},{12,8},{16,20},{20,16},{24,28},{28,24},{1,5},{5... | collective-permute-start | bytes 393224 | tf_op jit(solution)/shard_map/ppermute | solution.py:69
  18.3 26.3 %copy-start.6 = (s32[80,1]{0,1:T(1,128)S(1)}, s32[80,1]{0,1:T(1,128)}, u32[]{:S(2)}) copy-start(s32[80,1]{0,1:T(1,128)} %param.12) | copy-start | bytes 964
  18.4 26.2 %copy-start.7 = (s32[80,1]{0,1:T(1,128)S(1)}, s32[80,1]{0,1:T(1,128)}, u32[]{:S(2)}) copy-start(s32[80,1]{0,1:T(1,128)} %param.13) | copy-start | bytes 964
  21.2 1.7 %copy-start = (bf16[80,128,128]{2,1,0:T(8,128)(2,1)S(1)}, bf16[80,128,128]{2,1,0:T(8,128)(2,1)}, u32[]{:S(2)}) copy-start(bf16[80,128,128]{2,1,0:T(8,128)(2,1)} %blocks.3) | copy-start | bytes 7864324
  23.8 11.5 %copy-start.3 = (bf16[512,128]{1,0:T(8,128)(2,1)S(1)}, bf16[512,128]{1,0:T(8,128)(2,1)}, u32[]{:S(2)}) copy-start(bf16[512,128]{1,0:T(8,128)(2,1)} %refs_5_.1) | copy-start | bytes 393220
  23.8 11.5 %copy-start.4 = (bf16[128,128]{1,0:T(8,128)(2,1)S(1)}, bf16[128,128]{1,0:T(8,128)(2,1)}, u32[]{:S(2)}) copy-start(bf16[128,128]{1,0:T(8,128)(2,1)} %refs_3_.1) | copy-start | bytes 98308
  23.8 26.1 %copy-start.1 = (bf16[80,128,128]{2,1,0:T(8,128)(2,1)S(1)}, bf16[80,128,128]{2,1,0:T(8,128)(2,1)}, u32[]{:S(2)}) copy-start(bf16[80,128,128]{2,1,0:T(8,128)(2,1)} %blocks.3) | copy-start | bytes 7864324
  26.6 1.4 %collective-permute-start.7 = (bf16[4,128,128]{2,1,0:T(8,128)(2,1)S(1)}, bf16[4,128,128]{2,1,0:T(8,128)(2,1)S(1)}, u32[]{:S(2)}, u32[]{:S(2)}) collective-permute-start(bf16[4,128,128]{2,1,0:T(8,128)(2,1)S(1)} %get-tuple-element.22), channel_id=1, source_target_pairs={{0,1},{1,0},{2,3},{3,2},{4,5},{5,4},{6,7},{7,6},{8,9},{9,8},{10,11... | collective-permute-start | bytes 393224 | tf_op jit(solution)/shard_map/ppermute | solution.py:69
  26.7 4.9 %collective-permute-start.9 = (bf16[4,128,128]{2,1,0:T(8,128)(2,1)S(1)}, bf16[4,128,128]{2,1,0:T(8,128)(2,1)S(1)}, u32[]{:S(2)}, u32[]{:S(2)}) collective-permute-start(bf16[4,128,128]{2,1,0:T(8,128)(2,1)S(1)} %get-tuple-element.23), channel_id=1, source_target_pairs={{0,1},{1,0},{2,3},{3,2},{4,5},{5,4},{6,7},{7,6},{8,9},{9,8},{10,11... | collective-permute-start | bytes 393224 | tf_op jit(solution)/shard_map/ppermute | solution.py:69
  28.1 7.3 %collective-permute-start.8 = (bf16[4,128,128]{2,1,0:T(8,128)(2,1)S(1)}, bf16[4,128,128]{2,1,0:T(8,128)(2,1)S(1)}, u32[]{:S(2)}, u32[]{:S(2)}) collective-permute-start(bf16[4,128,128]{2,1,0:T(8,128)(2,1)S(1)} %add_convert_fusion.3), channel_id=1, source_target_pairs={{0,2},{1,3},{2,0},{3,1},{4,6},{5,7},{6,4},{7,5},{8,10},{9,11},{10,... | collective-permute-start | bytes 393224 | tf_op jit(solution)/shard_map/ppermute | solution.py:69
  36.3 5.0 %collective-permute-start.11 = (bf16[4,128,128]{2,1,0:T(8,128)(2,1)S(1)}, bf16[4,128,128]{2,1,0:T(8,128)(2,1)S(1)}, u32[]{:S(2)}, u32[]{:S(2)}) collective-permute-start(bf16[4,128,128]{2,1,0:T(8,128)(2,1)S(1)} %get-tuple-element.25.refs_0_), channel_id=1, source_target_pairs={{0,2},{1,3},{2,0},{3,1},{4,6},{5,7},{6,4},{7,5},{8,10},{9,11},{10,... | collective-permute-start | bytes 393224 | tf_op jit(solution)/shard_map/ppermute | solution.py:69
  38.1 1.3 %collective-permute-start.20 = (f32[136,128]{1,0:T(8,128)S(1)}, f32[136,128]{1,0:T(8,128)S(1)}, u32[]{:S(2)}, u32[]{:S(2)}) collective-permute-start(f32[136,128]{1,0:T(8,128)S(1)} %constant_dynamic-update-slice_fusion), channel_id=1, source_target_pairs={{0,1},{1,0},{2,3},{3,2},{4,5},{5,4},{6,7},{7,6},{8,9},{9,8},{10,11... | collective-permute-start | bytes 208904 | tf_op jit(solution)/shard_map/ppermute | solution.py:69
  39.4 4.4 %collective-permute-start.21 = (f32[136,128]{1,0:T(8,128)S(1)}, f32[136,128]{1,0:T(8,128)S(1)}, u32[]{:S(2)}, u32[]{:S(2)}) collective-permute-start(f32[136,128]{1,0:T(8,128)S(1)} %add.35), channel_id=1, source_target_pairs={{0,2},{1,3},{2,0},{3,1},{4,6},{5,7},{6,4},{7,5},{8,10},{9,11},{10,... | collective-permute-start | bytes 208904 | tf_op jit(solution)/shard_map/ppermute | solution.py:69
  39.7 10.2 %collective-permute-start.10 = (bf16[4,128,128]{2,1,0:T(8,128)(2,1)S(1)}, bf16[4,128,128]{2,1,0:T(8,128)(2,1)S(1)}, u32[]{:S(2)}, u32[]{:S(2)}) collective-permute-start(bf16[4,128,128]{2,1,0:T(8,128)(2,1)S(1)} %get-tuple-element.25.refs_0_), channel_id=1, source_target_pairs={{0,1},{1,0},{2,3},{3,2},{4,5},{5,4},{6,7},{7,6},{8,9},{9,8},{10,11... | collective-permute-start | bytes 393224 | tf_op jit(solution)/shard_map/ppermute | solution.py:69
  41.4 8.5 %collective-permute-start.12 = (bf16[4,128,128]{2,1,0:T(8,128)(2,1)S(1)}, bf16[4,128,128]{2,1,0:T(8,128)(2,1)S(1)}, u32[]{:S(2)}, u32[]{:S(2)}) collective-permute-start(bf16[4,128,128]{2,1,0:T(8,128)(2,1)S(1)} %collective-permute-done.11.refs_2_), channel_id=1, source_target_pairs={{0,1},{1,0},{2,3},{3,2},{4,5},{5,4},{6,7},{7,6},{8,9},{9,8},{10,11... | collective-permute-start | bytes 393224 | tf_op jit(solution)/shard_map/ppermute | solution.py:69
  43.8 4.4 %collective-permute-start.22 = (f32[136,128]{1,0:T(8,128)S(1)}, f32[136,128]{1,0:T(8,128)S(1)}, u32[]{:S(2)}, u32[]{:S(2)}) collective-permute-start(f32[136,128]{1,0:T(8,128)S(1)} %add.36), channel_id=1, source_target_pairs={{0,4},{4,0},{8,12},{12,8},{16,20},{20,16},{24,28},{28,24},{1,5},{5... | collective-permute-start | bytes 208904 | tf_op jit(solution)/shard_map/ppermute | solution.py:69
  48.1 7.9 %collective-permute-start.23 = (f32[136,128]{1,0:T(8,128)S(1)}, f32[136,128]{1,0:T(8,128)S(1)}, u32[]{:S(2)}, u32[]{:S(2)}) collective-permute-start(f32[136,128]{1,0:T(8,128)S(1)} %add.37), channel_id=1, source_target_pairs={{0,8},{4,12},{8,0},{12,4},{16,24},{20,28},{24,16},{28,20},{1,9},{5... | collective-permute-start | bytes 208904 | tf_op jit(solution)/shard_map/ppermute | solution.py:69
  52.1 10.0 %collective-permute-start.14 = (bf16[4,128,128]{2,1,0:T(8,128)(2,1)S(1)}, bf16[4,128,128]{2,1,0:T(8,128)(2,1)S(1)}, u32[]{:S(2)}, u32[]{:S(2)}) collective-permute-start(bf16[4,128,128]{2,1,0:T(8,128)(2,1)S(1)} %get-tuple-element.30), channel_id=1, source_target_pairs={{0,4},{4,0},{8,12},{12,8},{16,20},{20,16},{24,28},{28,24},{1,5},{5... | collective-permute-start | bytes 393224 | tf_op jit(solution)/shard_map/ppermute | solution.py:69
  56.0 5.4 %collective-permute-start.24 = (f32[136,128]{1,0:T(8,128)S(1)}, f32[136,128]{1,0:T(8,128)S(1)}, u32[]{:S(2)}, u32[]{:S(2)}) collective-permute-start(f32[136,128]{1,0:T(8,128)S(1)} %add.38), channel_id=1, source_target_pairs={{0,16},{4,20},{8,24},{12,28},{16,0},{20,4},{24,8},{28,12},{1,17},{... | collective-permute-start | bytes 208904 | tf_op jit(solution)/shard_map/ppermute | solution.py:69
  56.1 9.7 %collective-permute-start.13 = (bf16[4,128,128]{2,1,0:T(8,128)(2,1)S(1)}, bf16[4,128,128]{2,1,0:T(8,128)(2,1)S(1)}, u32[]{:S(2)}, u32[]{:S(2)}) collective-permute-start(bf16[4,128,128]{2,1,0:T(8,128)(2,1)S(1)} %get-tuple-element.28), channel_id=1, source_target_pairs={{0,4},{4,0},{8,12},{12,8},{16,20},{20,16},{24,28},{28,24},{1,5},{5... | collective-permute-start | bytes 393224 | tf_op jit(solution)/shard_map/ppermute | solution.py:69
  56.2 13.2 %collective-permute-start.17 = (bf16[4,128,128]{2,1,0:T(8,128)(2,1)S(1)}, bf16[4,128,128]{2,1,0:T(8,128)(2,1)S(1)}, u32[]{:S(2)}, u32[]{:S(2)}) collective-permute-start(bf16[4,128,128]{2,1,0:T(8,128)(2,1)S(1)} %get-tuple-element.31), channel_id=1, source_target_pairs={{0,8},{4,12},{8,0},{12,4},{16,24},{20,28},{24,16},{28,20},{1,9},{5... | collective-permute-start | bytes 393224 | tf_op jit(solution)/shard_map/ppermute | solution.py:69
  59.6 5.7 %collective-permute-start.18 = (bf16[4,128,128]{2,1,0:T(8,128)(2,1)S(1)}, bf16[4,128,128]{2,1,0:T(8,128)(2,1)S(1)}, u32[]{:S(2)}, u32[]{:S(2)}) collective-permute-start(bf16[4,128,128]{2,1,0:T(8,128)(2,1)S(1)} %get-tuple-element.33), channel_id=1, source_target_pairs={{0,8},{4,12},{8,0},{12,4},{16,24},{20,28},{24,16},{28,20},{1,9},{5... | collective-permute-start | bytes 393224 | tf_op jit(solution)/shard_map/ppermute | solution.py:69
  62.1 5.0 %collective-permute-start.15 = (bf16[4,128,128]{2,1,0:T(8,128)(2,1)S(1)}, bf16[4,128,128]{2,1,0:T(8,128)(2,1)S(1)}, u32[]{:S(2)}, u32[]{:S(2)}) collective-permute-start(bf16[4,128,128]{2,1,0:T(8,128)(2,1)S(1)} %add_convert_fusion.2), channel_id=1, source_target_pairs={{0,8},{4,12},{8,0},{12,4},{16,24},{20,28},{24,16},{28,20},{1,9},{5... | collective-permute-start | bytes 393224 | tf_op jit(solution)/shard_map/ppermute | solution.py:69
  65.3 5.0 %collective-permute-start.19 = (bf16[4,128,128]{2,1,0:T(8,128)(2,1)S(1)}, bf16[4,128,128]{2,1,0:T(8,128)(2,1)S(1)}, u32[]{:S(2)}, u32[]{:S(2)}) collective-permute-start(bf16[4,128,128]{2,1,0:T(8,128)(2,1)S(1)} %add_convert_fusion), channel_id=1, source_target_pairs={{0,4},{4,0},{8,12},{12,8},{16,20},{20,16},{24,28},{28,24},{1,5},{5... | collective-permute-start | bytes 393224 | tf_op jit(solution)/shard_map/ppermute | solution.py:69
  67.2 6.8 %collective-permute-start.16 = (bf16[4,128,128]{2,1,0:T(8,128)(2,1)S(1)}, bf16[4,128,128]{2,1,0:T(8,128)(2,1)S(1)}, u32[]{:S(2)}, u32[]{:S(2)}) collective-permute-start(bf16[4,128,128]{2,1,0:T(8,128)(2,1)S(1)} %add_convert_fusion.1), channel_id=1, source_target_pairs={{0,24},{4,28},{8,16},{12,20},{16,8},{20,12},{24,0},{28,4},{1,25},{... | collective-permute-start | bytes 393224 | tf_op jit(solution)/shard_map/ppermute | solution.py:69
  (1 other events, 0.9 us)

commit v2 on v1

v2 whole, which is shorter than its diff:
```python
from functools import partial
import math

import jax
import jax.numpy as jnp
import numpy as np
from jax import lax
from jax.experimental import pallas as pl
from jax.experimental.pallas import tpu as pltpu
from jax.sharding import PartitionSpec as P

BS = 128
C0 = 0.7978845608
C1 = 0.044715
QUICK = pl.CostEstimate(flops=1, bytes_accessed=1, transcendentals=0)
ANY = pl.BlockSpec(memory_space=pl.ANY)
HBM = pl.BlockSpec(memory_space=pltpu.HBM)
SMEM = pl.BlockSpec(memory_space=pltpu.SMEM)
VMEM = pl.BlockSpec(memory_space=pltpu.VMEM)


def mirror_masks(size):
    masks = []
    while size > 1:
        masks.append(size - 1)
        size //= 2
    return masks


def steps_to(offset, masks):
    steps = []
    for mask in masks:
        if offset & ((mask + 1) >> 1):
            steps.append(mask)
            offset ^= mask
    return steps


def tree(outer, inner, shortcut):
    assert outer & (outer - 1) == 0 and inner & (inner - 1) == 0
    outer_masks, inner_masks = mirror_masks(outer), mirror_masks(inner)
    found = []
    for o in range(outer):
        o_steps = steps_to(o, outer_masks)
        for i in range(inner):
            i_steps = steps_to(i, inner_masks)
            if o == 0 and i == 0:
                continue
            short = bool(i) and shortcut and o == 1
            if i and not short:
                parent = (o, i ^ i_steps[-1])
            else:
                parent = (o ^ o_steps[-1], i)
            depth = len(o_steps) + len(i_steps)
            found.append((depth, short, -o, i, parent))
    found.sort()
    return [(-o * inner + i, parent[0] * inner + parent[1]) for _, _, o, i, parent in found]


def inner_of(size):
    inner = 1
    while 2 * (2 * inner) * (2 * inner) <= size:
        inner *= 2
    return inner


def depth_of(offset, routes):
    parents = dict(routes)
    depth = 0
    while offset:
        offset, depth = parents[offset], depth + 1
    return depth


def swap(x, axis, mask):
    size = lax.axis_size(axis)
    return lax.ppermute(x, axis, [(i, i ^ mask) for i in range(size)])


def after(x, *others):
    return lax.optimization_barrier((x,) + others)[0]


def spread(pieces, axis, routes):
    pieces = dict(pieces)
    for offset, parent in routes:
        pieces[offset] = swap(pieces[parent], axis, offset ^ parent)
    return pieces


def add(terms):
    total = terms[0].astype(jnp.float32)
    for other in terms[1:]:
        total = total + other.astype(jnp.float32)
    return total


def collect(pieces, axis, routes):
    terms = {d: [p] for d, p in pieces.items()}
    for offset, parent in reversed(routes):
        total = add(terms.pop(offset)).astype(jnp.bfloat16)
        terms[parent].append(swap(total, axis, offset ^ parent))
    return terms


def unroll_of(slots):
    for u in (8, 4, 2):
        if slots % u == 0:
            return u
    return 1


def member(offset, chosen):
    mask = np.uint32(sum(1 << d for d in chosen)).astype(np.int32)
    return lax.bitwise_and(lax.shift_right_logical(jnp.int32(mask), offset), 1)


FORWARD_EARLY, FORWARD_LATE, BACK_FIRST, BACK_LAST = range(4)
LENGTHS, ROW_AT, COL_AT = 0, 4, 5


def prep_kernel(
    per, late, first, in_rows, in_cols, in_live, blocks,
    table, held, rows, cols, live, sem, small_sem,
):
    slots = blocks.shape[0]
    copy = pltpu.make_async_copy(blocks, held, sem)
    copy.start()
    small = [
        pltpu.make_async_copy(source, target, small_sem.at[n])
        for n, (source, target) in enumerate(((in_rows, rows), (in_cols, cols), (in_live, live)))
    ]
    for one in small:
        one.start()
    for one in small:
        one.wait()
    row_at, col_at = lax.axis_index("row"), lax.axis_index("col")

    def step(k, lengths):
        row, col = rows[k], cols[k]
        table[k] = row
        table[slots + k] = col
        in_use = (k < live[0]).astype(jnp.int32)
        offset = lax.bitwise_xor(row_at, lax.div(col, per))
        is_late, is_first = member(offset, late), member(offset, first)
        flags = (1 - is_late, is_late, is_first, 1 - is_first)
        for n, length in enumerate(lengths):
            table[(2 + n) * slots + length] = k
        return tuple(length + flag * in_use for length, flag in zip(lengths, flags))

    lengths = lax.fori_loop(0, slots, step, (jnp.int32(0),) * 4)
    for n, length in enumerate(lengths):
        table[6 * slots + n] = length
    table[6 * slots + ROW_AT] = row_at
    table[6 * slots + COL_AT] = col_at
    copy.wait()


def prep(block_rows, block_cols, tile_slot_count, blocks, per, late, first):
    slots = blocks.shape[0]
    return pl.pallas_call(
        partial(prep_kernel, per, late, first),
        out_shape=[
            jax.ShapeDtypeStruct((6 * slots + 8,), jnp.int32),
            jax.ShapeDtypeStruct(blocks.shape, blocks.dtype),
        ],
        in_specs=[HBM] * 4,
        out_specs=[SMEM, VMEM],
        scratch_shapes=[
            pltpu.SMEM((slots,), jnp.int32),
            pltpu.SMEM((slots,), jnp.int32),
            pltpu.SMEM((1,), jnp.int32),
            pltpu.SemaphoreType.DMA,
            pltpu.SemaphoreType.DMA((3,)),
        ],
        compiler_params=pltpu.CompilerParams(vmem_limit_bytes=50 << 20),
        cost_estimate=QUICK,
    )(block_rows.reshape(slots), block_cols.reshape(slots), tile_slot_count.reshape(1), blocks)


def sparse_kernel(which, offsets, here, there, sums, starts, *refs):
    transposed = which >= BACK_FIRST
    table, held = refs[:2]
    pieces, refs = refs[2 : 2 + len(offsets)], refs[2 + len(offsets) :]
    before = None
    if starts:
        before, refs = refs[0], refs[1:]
    if sums is None:
        total, source, sem = refs
    else:
        outs, (source, total, sem) = refs[: len(sums)], refs[len(sums) :]
    slots = held.shape[0]
    unroll = unroll_of(slots)
    per = pieces[0].shape[0]
    copies = []
    for n, offset in enumerate(offsets):
        at = lax.bitwise_xor(table[6 * slots + here], offset) * per
        copies.append(
            pltpu.make_async_copy(pieces[n], source.at[pl.ds(at, per)], sem.at[n])
        )
        copies[-1].start()
    places = []
    if sums is not None:
        out_per = outs[0].shape[0]
        places = [
            pl.ds(lax.bitwise_xor(table[6 * slots + there], d) * out_per, out_per) for d in sums
        ]
    if starts:
        for place in places:
            total[place] = before[place]
    elif places:
        for place, out in zip(places, outs):
            total[place] = jnp.zeros(out.shape, jnp.float32)
    else:
        total[...] = jnp.zeros_like(total)
    sink = total.shape[0] - 1
    length = table[6 * slots + which]
    for copy in copies:
        copy.wait()

    def step(i, carry):
        products, targets = [], []
        for u in range(unroll):
            n = i * unroll + u
            in_use = n < length
            k = jnp.where(in_use, table[(2 + which) * slots + n], 0)
            row, col = table[k], table[slots + k]
            if transposed:
                row = jnp.where(in_use, row, lax.bitwise_xor(table[6 * slots + here], offsets[0]) * per)
                products.append(
                    jnp.dot(source[row], held[k], preferred_element_type=jnp.float32)
                )
                target = col
            else:
                col = jnp.where(in_use, col, lax.bitwise_xor(table[6 * slots + here], offsets[0]) * per)
                products.append(
                    jnp.dot(held[k], source[col], preferred_element_type=jnp.float32)
                )
                target = row
            targets.append(jnp.where(in_use, target, sink))
        for product, target in zip(products, targets):
            total[target] = total[target] + product
        return carry

    lax.fori_loop(0, lax.div(length + unroll - 1, unroll), step, 0)
    if sums is not None:
        for out, place in zip(outs, places):
            out[...] = total[place].astype(out.dtype)


def sparse(which, table, held, pieces, here, there, sources, targets, before=None, sums=None, out_per=0):
    offsets = sorted(pieces)
    per = pieces[offsets[0]].shape[0]
    block = held.shape[1:]
    whole = jax.ShapeDtypeStruct((targets + 1,) + block, jnp.float32)
    scratch = [
        pltpu.VMEM((sources,) + block, jnp.bfloat16),
        pltpu.VMEM(whole.shape, whole.dtype),
        pltpu.SemaphoreType.DMA((len(offsets),)),
    ]
    if sums is None:
        out_shape = whole
        scratch.pop(1)
    else:
        out_shape = [jax.ShapeDtypeStruct((out_per,) + block, sums[d]) for d in sums]
    operands = [table, held] + [pieces[d] for d in offsets]
    in_specs = [SMEM, VMEM] + [ANY] * len(offsets)
    if before is not None:
        operands.append(before)
        in_specs.append(VMEM)
    size = 2 * BS * BS
    need = size * (held.shape[0] + 2 * sources + 5 * (targets + 1)) + (6 << 20)
    return pl.pallas_call(
        partial(
            sparse_kernel,
            which,
            tuple(offsets),
            here,
            there,
            None if sums is None else tuple(sums),
            before is not None,
        ),
        out_shape=out_shape,
        in_specs=in_specs,
        out_specs=jax.tree.map(lambda _: VMEM, out_shape),
        scratch_shapes=scratch,
        compiler_params=pltpu.CompilerParams(vmem_limit_bytes=need),
        cost_estimate=QUICK,
    )(*operands)


def dense_kernel(scaling, count, weight, bias, *refs):
    parts = [refs[3 * n : 3 * n + 3] for n in range(count)]
    hidden, *backs, grads = refs[3 * count :]
    weight_grad = bias_grad = None
    for n, (mine, theirs, cotangent) in enumerate(parts):
        rows, channels = cotangent.shape[0], mine.shape[-1]
        aggregate = mine[...].astype(jnp.float32) + theirs[...].astype(jnp.float32)
        aggregate_b = aggregate.astype(jnp.bfloat16).reshape(rows, channels)
        v = jnp.dot(aggregate_b, weight[...], preferred_element_type=jnp.float32) + bias[...]
        square = v * v
        t = jnp.tanh(C0 * (v + C1 * (v * square)))
        half = 0.5 * (1.0 + t)
        if n == 0:
            hidden[...] = (v * half).astype(jnp.bfloat16)
        slope = half + (0.5 * v) * (1.0 - t * t) * (C0 * (1.0 + (3.0 * C1) * square))
        dpreact = cotangent[...].astype(jnp.float32) * slope
        dpreact_b = dpreact.astype(jnp.bfloat16)
        for m in range(rows // BS):
            backs[n][m] = lax.dot_general(
                weight[...],
                dpreact_b[m * BS : (m + 1) * BS],
                (((1,), (1,)), ((), ())),
                preferred_element_type=jnp.float32,
            ).astype(jnp.bfloat16)
        weight_part = scaling * lax.dot_general(
            aggregate_b, dpreact_b, (((0,), (0,)), ((), ())), preferred_element_type=jnp.float32
        )
        bias_part = scaling * jnp.sum(dpreact, axis=0, keepdims=True)
        if n == 0:
            weight_grad, bias_grad = weight_part, bias_part
        else:
            weight_grad, bias_grad = weight_grad + weight_part, bias_grad + bias_part
    channels = weight.shape[0]
    grads[:channels] = weight_grad
    grads[channels:] = jnp.broadcast_to(bias_grad, (grads.shape[0] - channels, bias_grad.shape[1]))


def dense(weight, bias, parts, scaling):
    cotangent = parts[0][2]
    rows, (channels, units) = cotangent.shape[0], weight.shape
    out_shape = [jax.ShapeDtypeStruct(cotangent.shape, jnp.bfloat16)]
    out_shape += [jax.ShapeDtypeStruct((rows // BS, channels, BS), jnp.bfloat16)] * len(parts)
    out_shape.append(jax.ShapeDtypeStruct((channels + 16, units), jnp.float32))
    operands = [weight, bias] + [x for part in parts for x in part]
    return pl.pallas_call(
        partial(dense_kernel, scaling, len(parts)),
        out_shape=out_shape,
        in_specs=[VMEM] * len(operands),
        out_specs=[VMEM] * len(out_shape),
        compiler_params=pltpu.CompilerParams(vmem_limit_bytes=32 << 20),
        cost_estimate=QUICK,
    )(*operands)


def finish_kernel(*refs):
    parts, out = refs[:-1], refs[-1]
    for n in range(parts[0].shape[0]):
        total = parts[0][n].astype(jnp.float32)
        for part in parts[1:]:
            total = total + part[n].astype(jnp.float32)
        out[n * BS : (n + 1) * BS] = total.T


def finish(parts):
    per, channels, nodes = parts[0].shape
    return pl.pallas_call(
        finish_kernel,
        out_shape=jax.ShapeDtypeStruct((per * nodes, channels), jnp.float32),
        in_specs=[VMEM] * len(parts),
        out_specs=VMEM,
        compiler_params=pltpu.CompilerParams(vmem_limit_bytes=16 << 20),
    )(*parts)


def on_device(
    features, weight, bias_terms, blocks, block_rows, block_cols, tile_slot_count, cotangent
):
    own_rows, channels = features.shape
    row_devices, col_devices = lax.axis_size("row"), lax.axis_size("col")
    per = own_rows // BS
    row_blocks, column_blocks = per * col_devices, per * row_devices
    inner = inner_of(row_devices)
    on_row = tree(row_devices // inner, inner, True)
    on_col = tree(col_devices // 2, 2, False)
    across = col_devices - 2
    on_col = [route for route in on_col if route[0] != across]
    late_columns = [d for d, _ in on_row[-(row_devices // 4) :]]
    parents = [parent for _, parent in on_row]
    first = [d for d, parent in on_row if parent and d not in parents]

    table, held = prep(
        block_rows, block_cols, tile_slot_count, blocks, per, late_columns, first
    )
    pieces = {0: features.reshape(per, BS, channels)}
    near = [route for route in on_row if not route[1]]
    far = [route for route in on_row if route[1]]
    top = near[0][0]
    second = [d for d, p in far if p == top and p ^ d >= inner][0]
    far.sort(key=lambda route: (depth_of(route[0], on_row), route[0] != second))
    pieces |= spread({0: pieces[0]}, "row", near[:1])
    pieces |= spread({0: after(pieces[0], table)}, "row", near[1:])
    pieces[top] = after(pieces[top], *(pieces[d] for d, _ in near[1:]))
    for offset, parent in far:
        source = pieces[parent]
        if parent in [d for d, _ in near[1:]]:
            source = after(source, pieces[second])
        pieces[offset] = swap(source, "row", offset ^ parent)
    other_cotangent = swap(after(cotangent, pieces[second]), "col", across)
    early = {d: p for d, p in pieces.items() if d not in late_columns}
    late = {d: p for d, p in pieces.items() if d in late_columns}
    late[late_columns[0]] = after(late[late_columns[0]], other_cotangent)
    total = sparse(FORWARD_EARLY, table, held, early, ROW_AT, COL_AT, column_blocks, row_blocks)
    sums = sparse(
        FORWARD_LATE, table, held, late, ROW_AT, COL_AT, column_blocks, row_blocks, total,
        {d: jnp.float32 if d in (0, across) else jnp.bfloat16 for d in range(col_devices)}, per,
    )

    terms = collect(dict(enumerate(sums)), "col", on_col)
    mine = add(terms[0]).astype(jnp.bfloat16)
    others = add(terms[across]).astype(jnp.bfloat16)
    to_mine, to_others = swap(others, "col", across), swap(mine, "col", across)
    scaling = 1.0 / math.sqrt(own_rows * row_devices * col_devices)
    bias = bias_terms.reshape(1, -1)
    hidden, back, other_back, grads = dense(
        weight, bias,
        [(mine, to_mine, cotangent), (others, to_others, other_cotangent)], scaling,
    )
    grads = grads + swap(grads, "col", 1)
    for mask in mirror_masks(col_devices // 2)[1:]:
        grads = grads + swap(grads, "col", 2 * mask)

    rows = spread({0: back, across: other_back}, "col", on_col)
    rows[0] = after(rows[0], grads)
    types = {d: jnp.bfloat16 if d else jnp.float32 for d in range(row_devices)}
    rest = [d for d in range(row_devices) if d not in first]
    leave_first, leave_last = [
        sparse(
            which, table, held, rows, COL_AT, ROW_AT, row_blocks, column_blocks,
            None, {d: types[d] for d in chosen}, per,
        )
        for which, chosen in ((BACK_FIRST, first), (BACK_LAST, rest))
    ]
    sums = dict(zip(first, leave_first)) | dict(zip(rest, leave_last))

    chain = [far[-1][0]]
    while chain[-1]:
        chain.append(dict(on_row)[chain[-1]])
    terms = {d: [p] for d, p in sums.items()}
    came, seen = {}, []
    for offset, parent in reversed(on_row):
        total = add(terms.pop(offset)).astype(jnp.bfloat16)
        mask = offset ^ parent
        if offset in chain:
            if mask not in seen:
                seen.append(mask)
                rounded = grads.astype(jnp.bfloat16)
                total, rounded = lax.optimization_barrier((total, rounded))
                grads = rounded.astype(jnp.float32) + swap(rounded, "row", mask).astype(jnp.float32)
        elif parent == 0:
            total = after(total, came[chain[0]])
        else:
            total = after(total, leave_last[0])
        came[offset] = swap(total, "row", mask)
        terms[parent].append(came[offset])
    for mask in mirror_masks(inner) + [inner * m for m in mirror_masks(row_devices // inner)]:
        if mask not in seen:
            rounded = grads.astype(jnp.bfloat16)
            grads = rounded.astype(jnp.float32) + swap(rounded, "row", mask).astype(jnp.float32)
    feat_grad = finish(terms[0])
    return hidden, feat_grad, grads[:channels], grads[channels]


def solution(mesh):
    return jax.shard_map(
        on_device,
        mesh=mesh,
        in_specs=(
            P(("col", "row"), None),
            P(),
            P(),
            P("row", "col", None),
            P("row", "col"),
            P("row", "col"),
            P("row", "col"),
            P(("row", "col"), None),
        ),
        out_specs=(P(("row", "col"), None), P(("col", "row"), None), P(), P()),
        check_vma=False,
    )
```

time: 74.5 us -> 73.2 us (0.983)
  Pallas kernels: 6.76 us -> 15.3 us
  waiting for transfers between devices: 29 us -> 22.9 us
  local copies, waits for them, and re-layouts: 4.7 us -> 2.47 us
  starting transfers between devices: 32.8 us -> 30.6 us
    pallas_call x3 -> x6, Pallas kernels: 5.92 us -> 14.4 us  [the longest x4 10.9 us: sparse(): pl.pallas_call(partial(sparse_kernel, which, tuple(offsets), here, there,...]
    ppermute x25, waiting for transfers between devices: 29 us -> 22.9 us  [swap(): return lax.ppermute(x, axis, [(i, i ^ mask) for i in range(size)])]
    ppermute x25, starting transfers between devices: 32.8 us -> 30.6 us  [swap(): return lax.ppermute(x, axis, [(i, i ^ mask) for i in range(size)])]
    unnamed x17 -> x12, local copies, waits for them, and re-layouts: 2.67 us -> 1.32 us
    concatenate x3 -> x0, local copies, waits for them, and re-layouts: 0.88 us -> none  [the longest x1 0.8 us: on_device(): idx_forward = jnp.concatenate([slots, jnp.stack([row_at, col_at])])]
  transfers between devices with their start and end apart: 25 -> 25, of which waited for: 15 -> 13; matrix products, arithmetic and copies ran while one was open for 3% -> 2% of each run, Pallas kernels for 3% -> 13%
where the time goes in v2:
time: 73.2 us; the launch traced here: 73 us
  starting transfers between devices  30.6 us (42%)
  waiting for transfers between devices  22.9 us (31%)
  Pallas kernels  15.3 us (21%)
  local copies, waits for them, and re-layouts  2.47 us (3%)
  between operations  1.52 us (2%)
    ppermute x25, starting transfers between devices, swap(): return lax.ppermute(x, axis, [(i, i ^ mask) for i in range(size)])  30.6 us
    ppermute x25, waiting for transfers between devices, swap(): return lax.ppermute(x, axis, [(i, i ^ mask) for i in range(size)])  22.9 us
    pallas_call x4, Pallas kernels, sparse(): pl.pallas_call(partial(sparse_kernel, which, tuple(offsets), here, there,...  10.9 us
    pallas_call x1, Pallas kernels, prep(): pl.pallas_call(partial(prep_kernel, per, late, first), out_shape=[jax.Sha...  2.57 us
  transfers between devices with their start and end apart: 25, of which 13 were waited for; matrix products, arithmetic and copies ran while one was open for 2% of the time, Pallas kernels for 13%

profile of v2, /device:TPU:0, one launch (start us, length us, event | category | flops | bytes accessed | tf_op | source)
XLA Modules:
  0.0 73.0 jit_solution(16993883497856253893)
XLA Ops:
  0.7 5.1 %collective-permute-start.1 = (bf16[4,128,128]{2,1,0:T(8,128)(2,1)}, bf16[4,128,128]{2,1,0:T(8,128)(2,1)S(1)}, u32[]{:S(2)}, u32[]{:S(2)}) collective-permute-start(bf16[4,128,128]{2,1,0:T(8,128)(2,1)} %bitcast.8), channel_id=1, source_target_pairs={{0,24},{4,28},{8,16},{12,20},{16,8},{20,12},{24,0},{28,4},{1,25},{... | collective-permute-start | bytes 393224 | tf_op jit(solution)/shard_map/ppermute | solution.py:77
  6.4 0.6 copy-done.4
  7.1 0.7 copy-done.5
  7.7 2.6 %shard_map.111 = (s32[488]{0:T(512)S(1)}, bf16[80,128,128]{2,1,0:T(8,128)(2,1)S(1)}) custom-call(s32[80]{0:T(128)S(1)} %bitcast.13, s32[80]{0:T(128)S(1)} %bitcast.14, s32[1]{0:T(128)} %bitcast.7.in_live, bf16[80,128,128]{2,1,0:T(8,128)(2,1)} %blocks.1), custom_call_target="tpu_custom_call" | custom-call | flops 1 | bytes 1 | tf_op jit(solution)/shard_map/pallas_call | solution.py:161
  10.4 1.6 %collective-permute-start = (bf16[4,128,128]{2,1,0:T(8,128)(2,1)S(1)}, bf16[4,128,128]{2,1,0:T(8,128)(2,1)S(1)}, u32[]{:S(2)}, u32[]{:S(2)}) collective-permute-start(bf16[4,128,128]{2,1,0:T(8,128)(2,1)S(1)} %bitcast.10), channel_id=1, source_target_pairs={{0,4},{4,0},{8,12},{12,8},{16,20},{20,16},{24,28},{28,24},{1,5},{5... | collective-permute-start | bytes 393224 | tf_op jit(solution)/shard_map/ppermute | solution.py:77
  12.0 3.4 %collective-permute-done.2.refs_4_ = bf16[4,128,128]{2,1,0:T(8,128)(2,1)S(1)} collective-permute-done((bf16[4,128,128]{2,1,0:T(8,128)(2,1)S(1)}, bf16[4,128,128]{2,1,0:T(8,128)(2,1)S(1)}, u32[]{:S(2)}, u32[]{:S(2)}) %collective-permute-start.2) | collective-permute-done | bytes 131104 | tf_op jit(solution)/shard_map/ppermute | solution.py:77
  15.4 1.9 %collective-permute-start.3 = (bf16[4,128,128]{2,1,0:T(8,128)(2,1)S(1)}, bf16[4,128,128]{2,1,0:T(8,128)(2,1)S(1)}, u32[]{:S(2)}, u32[]{:S(2)}) collective-permute-start(bf16[4,128,128]{2,1,0:T(8,128)(2,1)S(1)} %collective-permute-done.1.refs_6_), channel_id=1, source_target_pairs={{0,8},{4,12},{8,0},{12,4},{16,24},{20,28},{24,16},{28,20},{1,9},{5... | collective-permute-start | bytes 393224 | tf_op jit(solution)/shard_map/ppermute | solution.py:77
  17.4 1.5 %collective-permute-start.7 = (bf16[4,128,128]{2,1,0:T(8,128)(2,1)S(1)}, bf16[4,128,128]{2,1,0:T(8,128)(2,1)S(1)}, u32[]{:S(2)}, u32[]{:S(2)}) collective-permute-start(bf16[4,128,128]{2,1,0:T(8,128)(2,1)S(1)} %collective-permute-done.1.refs_6_), channel_id=1, source_target_pairs={{0,4},{4,0},{8,12},{12,8},{16,20},{20,16},{24,28},{28,24},{1,5},{5... | collective-permute-start | bytes 393224 | tf_op jit(solution)/shard_map/ppermute | solution.py:77
  18.9 1.5 %collective-permute-done.3.refs_5_ = bf16[4,128,128]{2,1,0:T(8,128)(2,1)S(1)} collective-permute-done((bf16[4,128,128]{2,1,0:T(8,128)(2,1)S(1)}, bf16[4,128,128]{2,1,0:T(8,128)(2,1)S(1)}, u32[]{:S(2)}, u32[]{:S(2)}) %collective-permute-start.3) | collective-permute-done | bytes 131104 | tf_op jit(solution)/shard_map/ppermute | solution.py:77
  20.4 2.1 %collective-permute-start.4 = (bf16[4,128,128]{2,1,0:T(8,128)(2,1)S(1)}, bf16[4,128,128]{2,1,0:T(8,128)(2,1)S(1)}, u32[]{:S(2)}, u32[]{:S(2)}) collective-permute-start(bf16[4,128,128]{2,1,0:T(8,128)(2,1)S(1)} %collective-permute-done.refs_3_), channel_id=1, source_target_pairs={{0,8},{4,12},{8,0},{12,4},{16,24},{20,28},{24,16},{28,20},{1,9},{5... | collective-permute-start | bytes 393224 | tf_op jit(solution)/shard_map/ppermute | solution.py:77
  22.5 1.5 %collective-permute-start.5 = (bf16[512,128]{1,0:T(8,128)(2,1)S(1)}, bf16[512,128]{1,0:T(8,128)(2,1)S(1)}, u32[]{:S(2)}, u32[]{:S(2)}) collective-permute-start(bf16[512,128]{1,0:T(8,128)(2,1)S(1)} %copy-done.1), channel_id=1, source_target_pairs={{0,2},{1,3},{2,0},{3,1},{4,6},{5,7},{6,4},{7,5},{8,10},{9,11},{10,... | collective-permute-start | bytes 393224 | tf_op jit(solution)/shard_map/ppermute | solution.py:77
  24.0 1.5 %collective-permute-start.6 = (bf16[4,128,128]{2,1,0:T(8,128)(2,1)S(1)}, bf16[4,128,128]{2,1,0:T(8,128)(2,1)S(1)}, u32[]{:S(2)}, u32[]{:S(2)}) collective-permute-start(bf16[4,128,128]{2,1,0:T(8,128)(2,1)S(1)} %collective-permute-done.3.refs_5_), channel_id=1, source_target_pairs={{0,4},{4,0},{8,12},{12,8},{16,20},{20,16},{24,28},{28,24},{1,5},{5... | collective-permute-start | bytes 393224 | tf_op jit(solution)/shard_map/ppermute | solution.py:77
  25.5 3.6 %shard_map.112.refs_4_ = f32[17,128,128]{2,1,0:T(8,128)S(1)} custom-call(s32[488]{0:T(512)S(1)} %get-tuple-element.38.refs_0_, bf16[80,128,128]{2,1,0:T(8,128)(2,1)S(1)} %get-tuple-element.39.refs_1_, bf16[4,128,128]{2,1,0:T(8,128)(2,1)S(1)} %bitcast.11, bf16[4,128,128]{2,1,0:T(8,128)(2,1)S(1)} %collective-permute-done.refs_3_, ...), custom_call_target="tpu_custom_call" | custom-call | flops 1 | bytes 1 | tf_op jit(solution)/shard_map/pallas_call | solution.py:273
  29.2 1.8 %shard_map.113 = (f32[4,128,128]{2,1,0:T(8,128)S(1)}, bf16[4,128,128]{2,1,0:T(8,128)(2,1)S(1)}, f32[4,128,128]{2,1,0:T(8,128)S(1)}, bf16[4,128,128]{2,1,0:T(8,128)(2,1)S(1)}) custom-call(s32[488]{0:T(512)S(1)} %get-tuple-element.38.refs_0_, bf16[80,128,128]{2,1,0:T(8,128)(2,1)S(1)} %get-tuple-element.39.refs_1_, ...), custom_call_target="tpu_custom_call" | custom-call | flops 1 | bytes 1 | tf_op jit(solution)/shard_map/pallas_call | solution.py:273
  31.6 0.8 %collective-permute-done.8 = bf16[4,128,128]{2,1,0:T(8,128)(2,1)S(1)} collective-permute-done((bf16[4,128,128]{2,1,0:T(8,128)(2,1)S(1)}, bf16[4,128,128]{2,1,0:T(8,128)(2,1)S(1)}, u32[]{:S(2)}, u32[]{:S(2)}) %collective-permute-start.8) | collective-permute-done | bytes 131104 | tf_op jit(solution)/shard_map/ppermute | solution.py:77
  32.7 2.0 %collective-permute-start.10 = (bf16[4,128,128]{2,1,0:T(8,128)(2,1)S(1)}, bf16[4,128,128]{2,1,0:T(8,128)(2,1)S(1)}, u32[]{:S(2)}, u32[]{:S(2)}) collective-permute-start(bf16[4,128,128]{2,1,0:T(8,128)(2,1)S(1)} %add_convert_fusion.3.refs_3_), channel_id=1, source_target_pairs={{0,2},{1,3},{2,0},{3,1},{4,6},{5,7},{6,4},{7,5},{8,10},{9,11},{10,... | collective-permute-start | bytes 393224 | tf_op jit(solution)/shard_map/ppermute | solution.py:77
  34.7 4.2 %collective-permute-done.11.refs_4_ = bf16[4,128,128]{2,1,0:T(8,128)(2,1)S(1)} collective-permute-done((bf16[4,128,128]{2,1,0:T(8,128)(2,1)S(1)}, bf16[4,128,128]{2,1,0:T(8,128)(2,1)S(1)}, u32[]{:S(2)}, u32[]{:S(2)}) %collective-permute-start.11) | collective-permute-done | bytes 131104 | tf_op jit(solution)/shard_map/ppermute | solution.py:77
  38.9 2.0 %collective-permute-done.10.refs_1_ = bf16[4,128,128]{2,1,0:T(8,128)(2,1)S(1)} collective-permute-done((bf16[4,128,128]{2,1,0:T(8,128)(2,1)S(1)}, bf16[4,128,128]{2,1,0:T(8,128)(2,1)S(1)}, u32[]{:S(2)}, u32[]{:S(2)}) %collective-permute-start.10) | collective-permute-done | bytes 131104 | tf_op jit(solution)/shard_map/ppermute | solution.py:77
  40.9 1.0 %shard_map.114 = (bf16[512,128]{1,0:T(8,128)(2,1)}, bf16[4,128,128]{2,1,0:T(8,128)(2,1)S(1)}, bf16[4,128,128]{2,1,0:T(8,128)(2,1)S(1)}, f32[144,128]{1,0:T(8,128)S(1)}) custom-call(bf16[128,128]{1,0:T(8,128)(2,1)S(1)} %copy-done.2, f32[1,128]{1,0:T(1,128)S(1)} %bitcast.12, bf16[4,128,128]{2,1,0:T(8,128)(2,1)S(1)} %add_convert_fusion.4.refs_0_, ...), custom_call_target="tpu_custom_call" | custom-call | flops 1 | bytes 1 | tf_op jit(solution)/shard_map/pallas_call | solution.py:336
  42.4 1.2 %collective-permute-done.12 = f32[144,128]{1,0:T(8,128)S(1)} collective-permute-done((f32[144,128]{1,0:T(8,128)S(1)}, f32[144,128]{1,0:T(8,128)S(1)}, u32[]{:S(2)}, u32[]{:S(2)}) %collective-permute-start.12) | collective-permute-done | bytes 73760 | tf_op jit(solution)/shard_map/ppermute | solution.py:77
  43.7 2.3 %shard_map.116 = (bf16[4,128,128]{2,1,0:T(8,128)(2,1)S(1)}, bf16[4,128,128]{2,1,0:T(8,128)(2,1)S(1)}, bf16[4,128,128]{2,1,0:T(8,128)(2,1)S(1)}) custom-call(s32[488]{0:T(512)S(1)} %get-tuple-element.38.refs_0_, bf16[80,128,128]{2,1,0:T(8,128)(2,1)S(1)} %get-tuple-element.39.refs_1_, bf16[4,128,128]{2,1,0:T(8,128)(2,1)S(1)} %get-tuple-element.52.refs_2_, ...), custom_call_target="tpu_custom_call" | custom-call | flops 1 | bytes 1 | tf_op jit(solution)/shard_map/pallas_call | solution.py:273
  46.2 1.9 %collective-permute-start.16 = (bf16[4,128,128]{2,1,0:T(8,128)(2,1)S(1)}, bf16[4,128,128]{2,1,0:T(8,128)(2,1)S(1)}, u32[]{:S(2)}, u32[]{:S(2)}) collective-permute-start(bf16[4,128,128]{2,1,0:T(8,128)(2,1)S(1)} %get-tuple-element.59), channel_id=1, source_target_pairs={{0,4},{4,0},{8,12},{12,8},{16,20},{20,16},{24,28},{28,24},{1,5},{5... | collective-permute-start | bytes 393224 | tf_op jit(solution)/shard_map/ppermute | solution.py:77
  48.2 3.1 %shard_map.115 = (f32[4,128,128]{2,1,0:T(8,128)S(1)}, bf16[4,128,128]{2,1,0:T(8,128)(2,1)S(1)}, bf16[4,128,128]{2,1,0:T(8,128)(2,1)S(1)}, bf16[4,128,128]{2,1,0:T(8,128)(2,1)S(1)}, bf16[4,128,128]{2,1,0:T(8,128)(2,1)S(1)}) custom-call(s32[488]{0:T(512)S(1)} %get-tuple-element.38.refs_0_, bf16[80,128,128]{2,1,0:T(8,128)(2,1)S(1)} %get-tuple-element.39.refs_1_, ...), custom_call_target="tpu_custom_call" | custom-call | flops 1 | bytes 1 | tf_op jit(solution)/shard_map/pallas_call | solution.py:273
  52.6 1.1 %collective-permute-start.21 = (bf16[4,128,128]{2,1,0:T(8,128)(2,1)S(1)}, bf16[4,128,128]{2,1,0:T(8,128)(2,1)S(1)}, u32[]{:S(2)}, u32[]{:S(2)}) collective-permute-start(bf16[4,128,128]{2,1,0:T(8,128)(2,1)S(1)} %get-tuple-element.68), channel_id=1, source_target_pairs={{0,4},{4,0},{8,12},{12,8},{16,20},{20,16},{24,28},{28,24},{1,5},{5... | collective-permute-start | bytes 393224 | tf_op jit(solution)/shard_map/ppermute | solution.py:77
  53.7 1.6 %collective-permute-start.15 = (bf16[4,128,128]{2,1,0:T(8,128)(2,1)S(1)}, bf16[4,128,128]{2,1,0:T(8,128)(2,1)S(1)}, u32[]{:S(2)}, u32[]{:S(2)}) collective-permute-start(bf16[4,128,128]{2,1,0:T(8,128)(2,1)S(1)} %get-tuple-element.57), channel_id=1, source_target_pairs={{0,8},{4,12},{8,0},{12,4},{16,24},{20,28},{24,16},{28,20},{1,9},{5... | collective-permute-start | bytes 393224 | tf_op jit(solution)/shard_map/ppermute | solution.py:77
  55.7 1.6 %collective-permute-start.20 = (bf16[4,128,128]{2,1,0:T(8,128)(2,1)S(1)}, bf16[4,128,128]{2,1,0:T(8,128)(2,1)S(1)}, u32[]{:S(2)}, u32[]{:S(2)}) collective-permute-start(bf16[4,128,128]{2,1,0:T(8,128)(2,1)S(1)} %add_convert_fusion.1), channel_id=1, source_target_pairs={{0,8},{4,12},{8,0},{12,4},{16,24},{20,28},{24,16},{28,20},{1,9},{5... | collective-permute-start | bytes 393224 | tf_op jit(solution)/shard_map/ppermute | solution.py:77
  57.6 6.8 %collective-permute-done.20 = bf16[4,128,128]{2,1,0:T(8,128)(2,1)S(1)} collective-permute-done((bf16[4,128,128]{2,1,0:T(8,128)(2,1)S(1)}, bf16[4,128,128]{2,1,0:T(8,128)(2,1)S(1)}, u32[]{:S(2)}, u32[]{:S(2)}) %collective-permute-start.20) | collective-permute-done | bytes 131104 | tf_op jit(solution)/shard_map/ppermute | solution.py:77
  64.5 0.8 %collective-permute-start.17 = (bf16[4,128,128]{2,1,0:T(8,128)(2,1)S(1)}, bf16[4,128,128]{2,1,0:T(8,128)(2,1)S(1)}, u32[]{:S(2)}, u32[]{:S(2)}) collective-permute-start(bf16[4,128,128]{2,1,0:T(8,128)(2,1)S(1)} %add_convert_fusion.2), channel_id=1, source_target_pairs={{0,4},{4,0},{8,12},{12,8},{16,20},{20,16},{24,28},{28,24},{1,5},{5... | collective-permute-start | bytes 393224 | tf_op jit(solution)/shard_map/ppermute | solution.py:77
  65.3 3.8 %collective-permute-start.23 = (bf16[4,128,128]{2,1,0:T(8,128)(2,1)S(1)}, bf16[4,128,128]{2,1,0:T(8,128)(2,1)S(1)}, u32[]{:S(2)}, u32[]{:S(2)}) collective-permute-start(bf16[4,128,128]{2,1,0:T(8,128)(2,1)S(1)} %add_convert_fusion), channel_id=1, source_target_pairs={{0,24},{4,28},{8,16},{12,20},{16,8},{20,12},{24,0},{28,4},{1,25},{... | collective-permute-start | bytes 393224 | tf_op jit(solution)/shard_map/ppermute | solution.py:77
  69.1 1.1 %collective-permute-done.24 = bf16[144,128]{1,0:T(8,128)(2,1)S(1)} collective-permute-done((bf16[144,128]{1,0:T(8,128)(2,1)S(1)}, bf16[144,128]{1,0:T(8,128)(2,1)S(1)}, u32[]{:S(2)}, u32[]{:S(2)}) %collective-permute-start.24) | collective-permute-done | bytes 36896 | tf_op jit(solution)/shard_map/ppermute | solution.py:77
  71.4 0.7 collective-permute-done.23.refs_3_
  72.1 0.8 %shard_map.117 = f32[512,128]{1,0:T(8,128)} custom-call(f32[4,128,128]{2,1,0:T(8,128)S(1)} %get-tuple-element.54.refs_0_, bf16[4,128,128]{2,1,0:T(8,128)(2,1)S(1)} %collective-permute-done.17.refs_1_, bf16[4,128,128]{2,1,0:T(8,128)(2,1)S(1)} %collective-permute-done.18.refs_2_, bf16[4,128,128]{2,1,0:T(8,128)(2,1)S(1)} %collective-permute-done.23.refs_3_), custom_call_target="tpu_custom_call" | custom-call | tf_op jit(solution)/shard_map/pallas_call | solution.py:357
  (48 shorter events, 4.9 us)
Async XLA Ops:
  0.6 9.7 %copy-start = (bf16[512,128]{1,0:T(8,128)(2,1)S(1)}, bf16[512,128]{1,0:T(8,128)(2,1)}, u32[]{:S(2)}) copy-start(bf16[512,128]{1,0:T(8,128)(2,1)} %param.8) | copy-start | bytes 393220
  0.6 21.9 %copy-start.1 = (bf16[512,128]{1,0:T(8,128)(2,1)S(1)}, bf16[512,128]{1,0:T(8,128)(2,1)}, u32[]{:S(2)}) copy-start(bf16[512,128]{1,0:T(8,128)(2,1)} %refs_2_.1) | copy-start | bytes 393220
  0.7 11.3 %collective-permute-start.1 = (bf16[4,128,128]{2,1,0:T(8,128)(2,1)}, bf16[4,128,128]{2,1,0:T(8,128)(2,1)S(1)}, u32[]{:S(2)}, u32[]{:S(2)}) collective-permute-start(bf16[4,128,128]{2,1,0:T(8,128)(2,1)} %bitcast.8), channel_id=1, source_target_pairs={{0,24},{4,28},{8,16},{12,20},{16,8},{20,12},{24,0},{28,4},{1,25},{... | collective-permute-start | bytes 393224 | tf_op jit(solution)/shard_map/ppermute | solution.py:77
  6.4 0.7 copy-start.4
  7.1 0.7 copy-start.5
  10.3 5.0 %collective-permute-start.2 = (bf16[4,128,128]{2,1,0:T(8,128)(2,1)S(1)}, bf16[4,128,128]{2,1,0:T(8,128)(2,1)S(1)}, u32[]{:S(2)}, u32[]{:S(2)}) collective-permute-start(bf16[4,128,128]{2,1,0:T(8,128)(2,1)S(1)} %bitcast.9), channel_id=1, source_target_pairs={{0,8},{4,12},{8,0},{12,4},{16,24},{20,28},{24,16},{28,20},{1,9},{5... | collective-permute-start | bytes 393224 | tf_op jit(solution)/shard_map/ppermute | solution.py:77
  10.4 5.0 %collective-permute-start = (bf16[4,128,128]{2,1,0:T(8,128)(2,1)S(1)}, bf16[4,128,128]{2,1,0:T(8,128)(2,1)S(1)}, u32[]{:S(2)}, u32[]{:S(2)}) collective-permute-start(bf16[4,128,128]{2,1,0:T(8,128)(2,1)S(1)} %bitcast.10), channel_id=1, source_target_pairs={{0,4},{4,0},{8,12},{12,8},{16,20},{20,16},{24,28},{28,24},{1,5},{5... | collective-permute-start | bytes 393224 | tf_op jit(solution)/shard_map/ppermute | solution.py:77
  15.4 5.0 %collective-permute-start.3 = (bf16[4,128,128]{2,1,0:T(8,128)(2,1)S(1)}, bf16[4,128,128]{2,1,0:T(8,128)(2,1)S(1)}, u32[]{:S(2)}, u32[]{:S(2)}) collective-permute-start(bf16[4,128,128]{2,1,0:T(8,128)(2,1)S(1)} %collective-permute-done.1.refs_6_), channel_id=1, source_target_pairs={{0,8},{4,12},{8,0},{12,4},{16,24},{20,28},{24,16},{28,20},{1,9},{5... | collective-permute-start | bytes 393224 | tf_op jit(solution)/shard_map/ppermute | solution.py:77
  17.4 8.1 %collective-permute-start.7 = (bf16[4,128,128]{2,1,0:T(8,128)(2,1)S(1)}, bf16[4,128,128]{2,1,0:T(8,128)(2,1)S(1)}, u32[]{:S(2)}, u32[]{:S(2)}) collective-permute-start(bf16[4,128,128]{2,1,0:T(8,128)(2,1)S(1)} %collective-permute-done.1.refs_6_), channel_id=1, source_target_pairs={{0,4},{4,0},{8,12},{12,8},{16,20},{20,16},{24,28},{28,24},{1,5},{5... | collective-permute-start | bytes 393224 | tf_op jit(solution)/shard_map/ppermute | solution.py:77
  20.4 8.8 %collective-permute-start.4 = (bf16[4,128,128]{2,1,0:T(8,128)(2,1)S(1)}, bf16[4,128,128]{2,1,0:T(8,128)(2,1)S(1)}, u32[]{:S(2)}, u32[]{:S(2)}) collective-permute-start(bf16[4,128,128]{2,1,0:T(8,128)(2,1)S(1)} %collective-permute-done.refs_3_), channel_id=1, source_target_pairs={{0,8},{4,12},{8,0},{12,4},{16,24},{20,28},{24,16},{28,20},{1,9},{5... | collective-permute-start | bytes 393224 | tf_op jit(solution)/shard_map/ppermute | solution.py:77
  22.5 6.7 %collective-permute-start.5 = (bf16[512,128]{1,0:T(8,128)(2,1)S(1)}, bf16[512,128]{1,0:T(8,128)(2,1)S(1)}, u32[]{:S(2)}, u32[]{:S(2)}) collective-permute-start(bf16[512,128]{1,0:T(8,128)(2,1)S(1)} %copy-done.1), channel_id=1, source_target_pairs={{0,2},{1,3},{2,0},{3,1},{4,6},{5,7},{6,4},{7,5},{8,10},{9,11},{10,... | collective-permute-start | bytes 393224 | tf_op jit(solution)/shard_map/ppermute | solution.py:77
  24.0 5.2 %collective-permute-start.6 = (bf16[4,128,128]{2,1,0:T(8,128)(2,1)S(1)}, bf16[4,128,128]{2,1,0:T(8,128)(2,1)S(1)}, u32[]{:S(2)}, u32[]{:S(2)}) collective-permute-start(bf16[4,128,128]{2,1,0:T(8,128)(2,1)S(1)} %collective-permute-done.3.refs_5_), channel_id=1, source_target_pairs={{0,4},{4,0},{8,12},{12,8},{16,20},{20,16},{24,28},{28,24},{1,5},{5... | collective-permute-start | bytes 393224 | tf_op jit(solution)/shard_map/ppermute | solution.py:77
  29.2 11.7 %copy-start.2 = (bf16[128,128]{1,0:T(8,128)(2,1)S(1)}, bf16[128,128]{1,0:T(8,128)(2,1)}, u32[]{:S(2)}) copy-start(bf16[128,128]{1,0:T(8,128)(2,1)} %weight.1) | copy-start | bytes 98308
  29.2 11.7 %copy-start.3 = (f32[128]{0:T(128)S(1)}, f32[128]{0:T(128)}, u32[]{:S(2)}) copy-start(f32[128]{0:T(128)} %param.10) | copy-start | bytes 1540
  31.0 1.4 %collective-permute-start.8 = (bf16[4,128,128]{2,1,0:T(8,128)(2,1)S(1)}, bf16[4,128,128]{2,1,0:T(8,128)(2,1)S(1)}, u32[]{:S(2)}, u32[]{:S(2)}) collective-permute-start(bf16[4,128,128]{2,1,0:T(8,128)(2,1)S(1)} %get-tuple-element.46), channel_id=1, source_target_pairs={{0,1},{1,0},{2,3},{3,2},{4,5},{5,4},{6,7},{7,6},{8,9},{9,8},{10,11... | collective-permute-start | bytes 393224 | tf_op jit(solution)/shard_map/ppermute | solution.py:77
  31.1 1.5 %collective-permute-start.9 = (bf16[4,128,128]{2,1,0:T(8,128)(2,1)S(1)}, bf16[4,128,128]{2,1,0:T(8,128)(2,1)S(1)}, u32[]{:S(2)}, u32[]{:S(2)}) collective-permute-start(bf16[4,128,128]{2,1,0:T(8,128)(2,1)S(1)} %get-tuple-element.48), channel_id=1, source_target_pairs={{0,1},{1,0},{2,3},{3,2},{4,5},{5,4},{6,7},{7,6},{8,9},{9,8},{10,11... | collective-permute-start | bytes 393224 | tf_op jit(solution)/shard_map/ppermute | solution.py:77
  32.5 6.4 %collective-permute-start.11 = (bf16[4,128,128]{2,1,0:T(8,128)(2,1)S(1)}, bf16[4,128,128]{2,1,0:T(8,128)(2,1)S(1)}, u32[]{:S(2)}, u32[]{:S(2)}) collective-permute-start(bf16[4,128,128]{2,1,0:T(8,128)(2,1)S(1)} %add_convert_fusion.4.refs_0_), channel_id=1, source_target_pairs={{0,2},{1,3},{2,0},{3,1},{4,6},{5,7},{6,4},{7,5},{8,10},{9,11},{10,... | collective-permute-start | bytes 393224 | tf_op jit(solution)/shard_map/ppermute | solution.py:77
  32.7 8.2 %collective-permute-start.10 = (bf16[4,128,128]{2,1,0:T(8,128)(2,1)S(1)}, bf16[4,128,128]{2,1,0:T(8,128)(2,1)S(1)}, u32[]{:S(2)}, u32[]{:S(2)}) collective-permute-start(bf16[4,128,128]{2,1,0:T(8,128)(2,1)S(1)} %add_convert_fusion.3.refs_3_), channel_id=1, source_target_pairs={{0,2},{1,3},{2,0},{3,1},{4,6},{5,7},{6,4},{7,5},{8,10},{9,11},{10,... | collective-permute-start | bytes 393224 | tf_op jit(solution)/shard_map/ppermute | solution.py:77
  41.9 1.8 %collective-permute-start.13 = (bf16[4,128,128]{2,1,0:T(8,128)(2,1)S(1)}, bf16[4,128,128]{2,1,0:T(8,128)(2,1)S(1)}, u32[]{:S(2)}, u32[]{:S(2)}) collective-permute-start(bf16[4,128,128]{2,1,0:T(8,128)(2,1)S(1)} %get-tuple-element.52.refs_2_), channel_id=1, source_target_pairs={{0,1},{1,0},{2,3},{3,2},{4,5},{5,4},{6,7},{7,6},{8,9},{9,8},{10,11... | collective-permute-start | bytes 393224 | tf_op jit(solution)/shard_map/ppermute | solution.py:77
  41.9 1.8 %collective-permute-start.14 = (bf16[4,128,128]{2,1,0:T(8,128)(2,1)S(1)}, bf16[4,128,128]{2,1,0:T(8,128)(2,1)S(1)}, u32[]{:S(2)}, u32[]{:S(2)}) collective-permute-start(bf16[4,128,128]{2,1,0:T(8,128)(2,1)S(1)} %get-tuple-element.53.refs_4_), channel_id=1, source_target_pairs={{0,1},{1,0},{2,3},{3,2},{4,5},{5,4},{6,7},{7,6},{8,9},{9,8},{10,11... | collective-permute-start | bytes 393224 | tf_op jit(solution)/shard_map/ppermute | solution.py:77
  42.4 1.3 %collective-permute-start.12 = (f32[144,128]{1,0:T(8,128)S(1)}, f32[144,128]{1,0:T(8,128)S(1)}, u32[]{:S(2)}, u32[]{:S(2)}) collective-permute-start(f32[144,128]{1,0:T(8,128)S(1)} %get-tuple-element.51), channel_id=1, source_target_pairs={{0,1},{1,0},{2,3},{3,2},{4,5},{5,4},{6,7},{7,6},{8,9},{9,8},{10,11... | collective-permute-start | bytes 221192 | tf_op jit(solution)/shard_map/ppermute | solution.py:77
  46.1 5.2 %collective-permute-start.19 = (bf16[144,128]{1,0:T(8,128)(2,1)S(1)}, bf16[144,128]{1,0:T(8,128)(2,1)S(1)}, u32[]{:S(2)}, u32[]{:S(2)}) collective-permute-start(bf16[144,128]{1,0:T(8,128)(2,1)S(1)} %add.32), channel_id=1, source_target_pairs={{0,4},{4,0},{8,12},{12,8},{16,20},{20,16},{24,28},{28,24},{1,5},{5... | collective-permute-start | bytes 110600 | tf_op jit(solution)/shard_map/ppermute | solution.py:77
  46.2 5.7 %collective-permute-start.16 = (bf16[4,128,128]{2,1,0:T(8,128)(2,1)S(1)}, bf16[4,128,128]{2,1,0:T(8,128)(2,1)S(1)}, u32[]{:S(2)}, u32[]{:S(2)}) collective-permute-start(bf16[4,128,128]{2,1,0:T(8,128)(2,1)S(1)} %get-tuple-element.59), channel_id=1, source_target_pairs={{0,4},{4,0},{8,12},{12,8},{16,20},{20,16},{24,28},{28,24},{1,5},{5... | collective-permute-start | bytes 393224 | tf_op jit(solution)/shard_map/ppermute | solution.py:77
  52.0 5.3 %collective-permute-start.22 = (bf16[144,128]{1,0:T(8,128)(2,1)S(1)}, bf16[144,128]{1,0:T(8,128)(2,1)S(1)}, u32[]{:S(2)}, u32[]{:S(2)}) collective-permute-start(bf16[144,128]{1,0:T(8,128)(2,1)S(1)} %add_convert_fusion.6), channel_id=1, source_target_pairs={{0,8},{4,12},{8,0},{12,4},{16,24},{20,28},{24,16},{28,20},{1,9},{5... | collective-permute-start | bytes 110600 | tf_op jit(solution)/shard_map/ppermute | solution.py:77
  52.6 5.0 %collective-permute-start.21 = (bf16[4,128,128]{2,1,0:T(8,128)(2,1)S(1)}, bf16[4,128,128]{2,1,0:T(8,128)(2,1)S(1)}, u32[]{:S(2)}, u32[]{:S(2)}) collective-permute-start(bf16[4,128,128]{2,1,0:T(8,128)(2,1)S(1)} %get-tuple-element.68), channel_id=1, source_target_pairs={{0,4},{4,0},{8,12},{12,8},{16,20},{20,16},{24,28},{28,24},{1,5},{5... | collective-permute-start | bytes 393224 | tf_op jit(solution)/shard_map/ppermute | solution.py:77
  53.7 10.8 %collective-permute-start.15 = (bf16[4,128,128]{2,1,0:T(8,128)(2,1)S(1)}, bf16[4,128,128]{2,1,0:T(8,128)(2,1)S(1)}, u32[]{:S(2)}, u32[]{:S(2)}) collective-permute-start(bf16[4,128,128]{2,1,0:T(8,128)(2,1)S(1)} %get-tuple-element.57), channel_id=1, source_target_pairs={{0,8},{4,12},{8,0},{12,4},{16,24},{20,28},{24,16},{28,20},{1,9},{5... | collective-permute-start | bytes 393224 | tf_op jit(solution)/shard_map/ppermute | solution.py:77
  55.3 16.1 %collective-permute-start.18 = (bf16[4,128,128]{2,1,0:T(8,128)(2,1)S(1)}, bf16[4,128,128]{2,1,0:T(8,128)(2,1)S(1)}, u32[]{:S(2)}, u32[]{:S(2)}) collective-permute-start(bf16[4,128,128]{2,1,0:T(8,128)(2,1)S(1)} %get-tuple-element.62), channel_id=1, source_target_pairs={{0,8},{4,12},{8,0},{12,4},{16,24},{20,28},{24,16},{28,20},{1,9},{5... | collective-permute-start | bytes 393224 | tf_op jit(solution)/shard_map/ppermute | solution.py:77
  55.7 8.6 %collective-permute-start.20 = (bf16[4,128,128]{2,1,0:T(8,128)(2,1)S(1)}, bf16[4,128,128]{2,1,0:T(8,128)(2,1)S(1)}, u32[]{:S(2)}, u32[]{:S(2)}) collective-permute-start(bf16[4,128,128]{2,1,0:T(8,128)(2,1)S(1)} %add_convert_fusion.1), channel_id=1, source_target_pairs={{0,8},{4,12},{8,0},{12,4},{16,24},{20,28},{24,16},{28,20},{1,9},{5... | collective-permute-start | bytes 393224 | tf_op jit(solution)/shard_map/ppermute | solution.py:77
  64.4 5.9 %collective-permute-start.24 = (bf16[144,128]{1,0:T(8,128)(2,1)S(1)}, bf16[144,128]{1,0:T(8,128)(2,1)S(1)}, u32[]{:S(2)}, u32[]{:S(2)}) collective-permute-start(bf16[144,128]{1,0:T(8,128)(2,1)S(1)} %add_convert_fusion.5), channel_id=1, source_target_pairs={{0,24},{4,28},{8,16},{12,20},{16,8},{20,12},{24,0},{28,4},{1,25},{... | collective-permute-start | bytes 110600 | tf_op jit(solution)/shard_map/ppermute | solution.py:77
  64.5 6.9 %collective-permute-start.17 = (bf16[4,128,128]{2,1,0:T(8,128)(2,1)S(1)}, bf16[4,128,128]{2,1,0:T(8,128)(2,1)S(1)}, u32[]{:S(2)}, u32[]{:S(2)}) collective-permute-start(bf16[4,128,128]{2,1,0:T(8,128)(2,1)S(1)} %add_convert_fusion.2), channel_id=1, source_target_pairs={{0,4},{4,0},{8,12},{12,8},{16,20},{20,16},{24,28},{28,24},{1,5},{5... | collective-permute-start | bytes 393224 | tf_op jit(solution)/shard_map/ppermute | solution.py:77
  65.3 6.8 %collective-permute-start.23 = (bf16[4,128,128]{2,1,0:T(8,128)(2,1)S(1)}, bf16[4,128,128]{2,1,0:T(8,128)(2,1)S(1)}, u32[]{:S(2)}, u32[]{:S(2)}) collective-permute-start(bf16[4,128,128]{2,1,0:T(8,128)(2,1)S(1)} %add_convert_fusion), channel_id=1, source_target_pairs={{0,24},{4,28},{8,16},{12,20},{16,8},{20,12},{24,0},{28,4},{1,25},{... | collective-permute-start | bytes 393224 | tf_op jit(solution)/shard_map/ppermute | solution.py:77

commit v3 on v2

--- a/solution.py
+++ b/solution.py
@@ -72,19 +72,31 @@
     return depth
 
 
-def swap(x, axis, mask):
+def swap(x, axis, mask, name="swap"):
     size = lax.axis_size(axis)
-    return lax.ppermute(x, axis, [(i, i ^ mask) for i in range(size)])
+    with jax.named_scope(name):
+        return lax.ppermute(x, axis, [(i, i ^ mask) for i in range(size)])
 
 
 def after(x, *others):
     return lax.optimization_barrier((x,) + others)[0]
+
+
+class Queue:
+    def __init__(self):
+        self.last = None
+
+    def swap(self, x, axis, mask, name):
+        if self.last is not None:
+            x = after(x, self.last)
+        self.last = x
+        return swap(x, axis, mask, name)
 
 
 def spread(pieces, axis, routes):
     pieces = dict(pieces)
     for offset, parent in routes:
-        pieces[offset] = swap(pieces[parent], axis, offset ^ parent)
+        pieces[offset] = swap(pieces[parent], axis, offset ^ parent, f"rows_{offset}")
     return pieces
 
 
@@ -99,7 +111,7 @@
     terms = {d: [p] for d, p in pieces.items()}
     for offset, parent in reversed(routes):
         total = add(terms.pop(offset)).astype(jnp.bfloat16)
-        terms[parent].append(swap(total, axis, offset ^ parent))
+        terms[parent].append(swap(total, axis, offset ^ parent, f"aggregate_{offset}"))
     return terms
 
 
@@ -116,85 +128,87 @@
 
 
 FORWARD_EARLY, FORWARD_LATE, BACK_FIRST, BACK_LAST = range(4)
-LENGTHS, ROW_AT, COL_AT = 0, 4, 5
-
-
-def prep_kernel(
-    per, late, first, in_rows, in_cols, in_live, blocks,
-    table, held, rows, cols, live, sem, small_sem,
-):
+
+
+def widths(slots, row_blocks, column_blocks):
+    bits = [(n - 1).bit_length() for n in (slots, row_blocks, column_blocks)]
+    assert sum(bits) < 32
+    return bits
+
+
+def parts_of(slots):
+    return 8 if slots % 8 == 0 else 1
+
+
+def prep_kernel(per, bits, late, first, indices, blocks, table, held, sem):
     slots = blocks.shape[0]
-    copy = pltpu.make_async_copy(blocks, held, sem)
-    copy.start()
-    small = [
-        pltpu.make_async_copy(source, target, small_sem.at[n])
-        for n, (source, target) in enumerate(((in_rows, rows), (in_cols, cols), (in_live, live)))
-    ]
-    for one in small:
-        one.start()
-    for one in small:
-        one.wait()
-    row_at, col_at = lax.axis_index("row"), lax.axis_index("col")
-
-    def step(k, lengths):
-        row, col = rows[k], cols[k]
-        table[k] = row
-        table[slots + k] = col
-        in_use = (k < live[0]).astype(jnp.int32)
-        offset = lax.bitwise_xor(row_at, lax.div(col, per))
-        is_late, is_first = member(offset, late), member(offset, first)
-        flags = (1 - is_late, is_late, is_first, 1 - is_first)
-        for n, length in enumerate(lengths):
-            table[(2 + n) * slots + length] = k
-        return tuple(length + flag * in_use for length, flag in zip(lengths, flags))
-
-    lengths = lax.fori_loop(0, slots, step, (jnp.int32(0),) * 4)
+    parts = parts_of(slots)
+    copies = []
+    for n in range(parts):
+        place = pl.ds(n * (slots // parts), slots // parts)
+        copies.append(pltpu.make_async_copy(blocks.at[place], held.at[place], sem.at[n]))
+        copies[-1].start()
+    row_at = lax.axis_index("row")
+    live = indices[2 * slots]
+
+    def step(i, lengths):
+        early, late_ones, soon, last = lengths
+        for u in range(unroll):
+            k = i * unroll + u
+            row, col = indices[k], indices[slots + k]
+            entry = k + lax.shift_left(row, bits[0]) + lax.shift_left(col, bits[0] + bits[1])
+            in_use = (k < live).astype(jnp.int32)
+            offset = lax.bitwise_xor(row_at, lax.div(col, per))
+            is_late, is_first = member(offset, late), member(offset, first)
+            table[jnp.where(is_late == 1, slots - 1 - late_ones, early)] = entry
+            table[slots + jnp.where(is_first == 1, soon, slots - 1 - last)] = entry
+            early, late_ones = early + (1 - is_late) * in_use, late_ones + is_late * in_use
+            soon, last = soon + is_first * in_use, last + (1 - is_first) * in_use
+        return early, late_ones, soon, last
+
+    unroll = 4 if slots % 4 == 0 else 1
+    lengths = lax.fori_loop(0, lax.div(live + unroll - 1, unroll), step, (jnp.int32(0),) * 4)
     for n, length in enumerate(lengths):
-        table[6 * slots + n] = length
-    table[6 * slots + ROW_AT] = row_at
-    table[6 * slots + COL_AT] = col_at
-    copy.wait()
-
-
-def prep(block_rows, block_cols, tile_slot_count, blocks, per, late, first):
+        table[2 * slots + n] = length
+    for copy in copies:
+        copy.wait()
+
+
+def prep(indices, blocks, per, bits, late, first):
     slots = blocks.shape[0]
     return pl.pallas_call(
-        partial(prep_kernel, per, late, first),
+        partial(prep_kernel, per, bits, late, first),
         out_shape=[
-            jax.ShapeDtypeStruct((6 * slots + 8,), jnp.int32),
+            jax.ShapeDtypeStruct((2 * slots + 8,), jnp.int32),
             jax.ShapeDtypeStruct(blocks.shape, blocks.dtype),
         ],
-        in_specs=[HBM] * 4,
+        in_specs=[SMEM, HBM],
         out_specs=[SMEM, VMEM],
-        scratch_shapes=[
-            pltpu.SMEM((slots,), jnp.int32),
-            pltpu.SMEM((slots,), jnp.int32),
-            pltpu.SMEM((1,), jnp.int32),
-            pltpu.SemaphoreType.DMA,
-            pltpu.SemaphoreType.DMA((3,)),
-        ],
+        scratch_shapes=[pltpu.SemaphoreType.DMA((parts_of(slots),))],
         compiler_params=pltpu.CompilerParams(vmem_limit_bytes=50 << 20),
         cost_estimate=QUICK,
-    )(block_rows.reshape(slots), block_cols.reshape(slots), tile_slot_count.reshape(1), blocks)
-
-
-def sparse_kernel(which, offsets, here, there, sums, starts, *refs):
+    )(indices, blocks)
+
+
+def sparse_kernel(which, bits, offsets, here, there, sums, starts, *refs):
     transposed = which >= BACK_FIRST
-    table, held = refs[:2]
+    in_table, held = refs[:2]
     pieces, refs = refs[2 : 2 + len(offsets)], refs[2 + len(offsets) :]
     before = None
     if starts:
         before, refs = refs[0], refs[1:]
     if sums is None:
-        total, source, sem = refs
+        total, table, source, sem = refs
     else:
-        outs, (source, total, sem) = refs[: len(sums)], refs[len(sums) :]
+        outs, (total, table, source, sem) = refs[: len(sums)], refs[len(sums) :]
+    here, there = lax.axis_index(here), lax.axis_index(there)
     slots = held.shape[0]
     unroll = unroll_of(slots)
     per = pieces[0].shape[0]
-    copies = []
+    copies = [pltpu.make_async_copy(in_table, table, sem.at[len(offsets)])]
+    copies[0].start()
     for n, offset in enumerate(offsets):
-        at = lax.bitwise_xor(table[6 * slots + here], offset) * per
+        at = lax.bitwise_xor(here, offset) * per
         copies.append(
             pltpu.make_async_copy(pieces[n], source.at[pl.ds(at, per)], sem.at[n])
         )
@@ -203,7 +217,7 @@
     if sums is not None:
         out_per = outs[0].shape[0]
         places = [
-            pl.ds(lax.bitwise_xor(table[6 * slots + there], d) * out_per, out_per) for d in sums
+            pl.ds(lax.bitwise_xor(there, d) * out_per, out_per) for d in sums
         ]
     if starts:
         for place in places:
@@ -214,29 +228,30 @@
     else:
         total[...] = jnp.zeros_like(total)
     sink = total.shape[0] - 1
-    length = table[6 * slots + which]
     for copy in copies:
         copy.wait()
+    length = table[2 * slots + which]
+    idle = lax.bitwise_xor(here, offsets[0]) * per
 
     def step(i, carry):
         products, targets = [], []
         for u in range(unroll):
             n = i * unroll + u
             in_use = n < length
-            k = jnp.where(in_use, table[(2 + which) * slots + n], 0)
-            row, col = table[k], table[slots + k]
+            at = jnp.minimum(n, slots - 1)
+            if which in (FORWARD_LATE, BACK_LAST):
+                at = slots - 1 - at
+            entry = jnp.where(in_use, table[slots * transposed + at], 0)
+            k = lax.bitwise_and(entry, (1 << bits[0]) - 1)
+            row = lax.bitwise_and(lax.shift_right_logical(entry, bits[0]), (1 << bits[1]) - 1)
+            col = lax.shift_right_logical(entry, bits[0] + bits[1])
             if transposed:
-                row = jnp.where(in_use, row, lax.bitwise_xor(table[6 * slots + here], offsets[0]) * per)
-                products.append(
-                    jnp.dot(source[row], held[k], preferred_element_type=jnp.float32)
-                )
-                target = col
+                source_at, target = row, col
+                lhs, rhs = source.at[jnp.where(in_use, source_at, idle)], held.at[k]
             else:
-                col = jnp.where(in_use, col, lax.bitwise_xor(table[6 * slots + here], offsets[0]) * per)
-                products.append(
-                    jnp.dot(held[k], source[col], preferred_element_type=jnp.float32)
-                )
-                target = row
+                source_at, target = col, row
+                lhs, rhs = held.at[k], source.at[jnp.where(in_use, source_at, idle)]
+            products.append(jnp.dot(lhs[...], rhs[...], preferred_element_type=jnp.float32))
             targets.append(jnp.where(in_use, target, sink))
         for product, target in zip(products, targets):
             total[target] = total[target] + product
@@ -248,23 +263,24 @@
             out[...] = total[place].astype(out.dtype)
 
 
-def sparse(which, table, held, pieces, here, there, sources, targets, before=None, sums=None, out_per=0):
+def sparse(which, bits, table, held, pieces, here, there, sources, targets, before=None, sums=None, out_per=0):
     offsets = sorted(pieces)
     per = pieces[offsets[0]].shape[0]
     block = held.shape[1:]
     whole = jax.ShapeDtypeStruct((targets + 1,) + block, jnp.float32)
     scratch = [
+        pltpu.VMEM(whole.shape, whole.dtype),
+        pltpu.SMEM(table.shape, table.dtype),
         pltpu.VMEM((sources,) + block, jnp.bfloat16),
-        pltpu.VMEM(whole.shape, whole.dtype),
-        pltpu.SemaphoreType.DMA((len(offsets),)),
+        pltpu.SemaphoreType.DMA((len(offsets) + 1,)),
     ]
     if sums is None:
         out_shape = whole
-        scratch.pop(1)
+        scratch.pop(0)
     else:
         out_shape = [jax.ShapeDtypeStruct((out_per,) + block, sums[d]) for d in sums]
     operands = [table, held] + [pieces[d] for d in offsets]
-    in_specs = [SMEM, VMEM] + [ANY] * len(offsets)
+    in_specs = [ANY, VMEM] + [ANY] * len(offsets)
     if before is not None:
         operands.append(before)
         in_specs.append(VMEM)
@@ -274,6 +290,7 @@
         partial(
             sparse_kernel,
             which,
+            bits,
             tuple(offsets),
             here,
             there,
@@ -344,23 +361,34 @@
 
 
 def finish_kernel(*refs):
-    parts, out = refs[:-1], refs[-1]
+    mine, theirs = refs[:2]
+    parts, (out, weight_grad, bias_grad) = refs[2:-3], refs[-3:]
     for n in range(parts[0].shape[0]):
         total = parts[0][n].astype(jnp.float32)
         for part in parts[1:]:
             total = total + part[n].astype(jnp.float32)
         out[n * BS : (n + 1) * BS] = total.T
-
-
-def finish(parts):
+    grads = mine[...].astype(jnp.float32) + theirs[...].astype(jnp.float32)
+    channels = weight_grad.shape[0]
+    weight_grad[...] = grads[:channels]
+    bias_grad[...] = grads[channels : channels + 1]
+
+
+def finish(parts, mine, theirs):
     per, channels, nodes = parts[0].shape
+    units = mine.shape[1]
+    out_shape = [
+        jax.ShapeDtypeStruct(shape, jnp.float32)
+        for shape in ((per * nodes, channels), (channels, units), (1, units))
+    ]
     return pl.pallas_call(
         finish_kernel,
-        out_shape=jax.ShapeDtypeStruct((per * nodes, channels), jnp.float32),
-        in_specs=[VMEM] * len(parts),
-        out_specs=VMEM,
+        out_shape=out_shape,
+        in_specs=[VMEM] * (len(parts) + 2),
+        out_specs=[VMEM] * 3,
         compiler_params=pltpu.CompilerParams(vmem_limit_bytes=16 << 20),
-    )(*parts)
+        cost_estimate=QUICK,
+    )(mine, theirs, *parts)
 
 
 def on_device(
@@ -375,38 +403,40 @@
     on_col = tree(col_devices // 2, 2, False)
     across = col_devices - 2
     on_col = [route for route in on_col if route[0] != across]
-    late_columns = [d for d, _ in on_row[-(row_devices // 4) :]]
-    parents = [parent for _, parent in on_row]
-    first = [d for d, parent in on_row if parent and d not in parents]
-
-    table, held = prep(
-        block_rows, block_cols, tile_slot_count, blocks, per, late_columns, first
-    )
+
+    depths = {d: depth_of(d, on_row) for d, _ in on_row}
+    short = [d for d, p in on_row if p and p < inner and d >= inner]
+    chain = [max(depths, key=lambda d: (depths[d], d not in short))]
+    while chain[-1]:
+        chain.append(dict(on_row)[chain[-1]])
+    first = [d for d in depths if depths[d] == max(depths.values())]
+    late_columns = [d for d, p in on_row if depths[d] == max(depths.values()) or d in short]
+
+    bits = widths(blocks.shape[0], row_blocks, column_blocks)
+    indices = jnp.concatenate([block_rows[:, 0], block_cols[:, 0], tile_slot_count[0]])
+    table, held = prep(indices, blocks, per, bits, late_columns, first)
     pieces = {0: features.reshape(per, BS, channels)}
-    near = [route for route in on_row if not route[1]]
-    far = [route for route in on_row if route[1]]
-    top = near[0][0]
-    second = [d for d, p in far if p == top and p ^ d >= inner][0]
-    far.sort(key=lambda route: (depth_of(route[0], on_row), route[0] != second))
-    pieces |= spread({0: pieces[0]}, "row", near[:1])
-    pieces |= spread({0: after(pieces[0], table)}, "row", near[1:])
-    pieces[top] = after(pieces[top], *(pieces[d] for d, _ in near[1:]))
-    for offset, parent in far:
-        source = pieces[parent]
-        if parent in [d for d, _ in near[1:]]:
-            source = after(source, pieces[second])
-        pieces[offset] = swap(source, "row", offset ^ parent)
-    other_cotangent = swap(after(cotangent, pieces[second]), "col", across)
+    queue = Queue()
+    for offset, parent in sorted(
+        on_row,
+        key=lambda r: (
+            depths[r[0]], r[0] not in chain, (r[0] ^ r[1]) < inner
+        ),
+    ):
+        pieces[offset] = queue.swap(pieces[parent], "row", offset ^ parent, f"features_{offset}")
+        if offset == chain[-2]:
+            pieces[offset] = after(pieces[offset], table)
+    other_cotangent = queue.swap(cotangent, "col", across, "cotangent")
     early = {d: p for d, p in pieces.items() if d not in late_columns}
     late = {d: p for d, p in pieces.items() if d in late_columns}
-    late[late_columns[0]] = after(late[late_columns[0]], other_cotangent)
-    total = sparse(FORWARD_EARLY, table, held, early, ROW_AT, COL_AT, column_blocks, row_blocks)
+    total = sparse(FORWARD_EARLY, bits, table, held, early, "row", "col", column_blocks, row_blocks)
     sums = sparse(
-        FORWARD_LATE, table, held, late, ROW_AT, COL_AT, column_blocks, row_blocks, total,
+        FORWARD_LATE, bits, table, held, late, "row", "col", column_blocks, row_blocks, total,
         {d: jnp.float32 if d in (0, across) else jnp.bfloat16 for d in range(col_devices)}, per,
     )
 
     terms = collect(dict(enumerate(sums)), "col", on_col)
+    terms[0][0] = after(terms[0][0], other_cotangent)
     mine = add(terms[0]).astype(jnp.bfloat16)
     others = add(terms[across]).astype(jnp.bfloat16)
     to_mine, to_others = swap(others, "col", across), swap(mine, "col", across)
@@ -426,39 +456,36 @@
     rest = [d for d in range(row_devices) if d not in first]
     leave_first, leave_last = [
         sparse(
-            which, table, held, rows, COL_AT, ROW_AT, row_blocks, column_blocks,
+            which, bits, table, held, rows, "col", "row", row_blocks, column_blocks,
             None, {d: types[d] for d in chosen}, per,
         )
         for which, chosen in ((BACK_FIRST, first), (BACK_LAST, rest))
     ]
     sums = dict(zip(first, leave_first)) | dict(zip(rest, leave_last))
 
-    chain = [far[-1][0]]
-    while chain[-1]:
-        chain.append(dict(on_row)[chain[-1]])
     terms = {d: [p] for d, p in sums.items()}
-    came, seen = {}, []
-    for offset, parent in reversed(on_row):
+    queue = Queue()
+    top = chain[-2]
+    order = sorted(
+        on_row, key=lambda r: (-depths[r[0]], r[0] != top ^ 1, r[0] not in chain, r[0])
+    )
+    masks = [d ^ parent for d, parent in zip(chain, chain[1:])]
+    masks = masks[:1] + masks[-1:] + masks[1:-1]
+    masks += [m for m in mirror_masks(inner) if m not in masks]
+    masks += [inner * m for m in mirror_masks(row_devices // inner) if inner * m not in masks]
+    mine, theirs = grads.astype(jnp.bfloat16), None
+    for n, (offset, parent) in enumerate(order):
         total = add(terms.pop(offset)).astype(jnp.bfloat16)
-        mask = offset ^ parent
-        if offset in chain:
-            if mask not in seen:
-                seen.append(mask)
-                rounded = grads.astype(jnp.bfloat16)
-                total, rounded = lax.optimization_barrier((total, rounded))
-                grads = rounded.astype(jnp.float32) + swap(rounded, "row", mask).astype(jnp.float32)
-        elif parent == 0:
-            total = after(total, came[chain[0]])
-        else:
-            total = after(total, leave_last[0])
-        came[offset] = swap(total, "row", mask)
-        terms[parent].append(came[offset])
-    for mask in mirror_masks(inner) + [inner * m for m in mirror_masks(row_devices // inner)]:
-        if mask not in seen:
-            rounded = grads.astype(jnp.bfloat16)
-            grads = rounded.astype(jnp.float32) + swap(rounded, "row", mask).astype(jnp.float32)
-    feat_grad = finish(terms[0])
-    return hidden, feat_grad, grads[:channels], grads[channels]
+        terms[parent].append(queue.swap(total, "row", offset ^ parent, f"sums_{offset}"))
+        if n + 1 < len(order) and depths[order[n + 1][0]] == depths[offset]:
+            continue
+        for mask in masks[:1] if n + 1 < len(order) else masks:
+            if theirs is not None:
+                mine = add([mine, after(theirs, queue.last)]).astype(jnp.bfloat16)
+            theirs = queue.swap(mine, "row", mask, f"gradients_{mask}")
+        masks = masks[1:]
+    feat_grad, weight_grad, bias_grad = finish(terms[0], mine, theirs)
+    return hidden, feat_grad, weight_grad, bias_grad.reshape(-1)
 
 
 def solution(mesh):

time: 73.2 us -> 61.4 us (0.84)
  Pallas kernels: 15.3 us -> 9.47 us
  starting transfers between devices: 30.6 us -> 27.3 us
  local copies, waits for them, and re-layouts: 2.47 us -> 0.02 us
  other arithmetic: 0.24 us -> 0.98 us
    pallas_call x6, Pallas kernels: 14.3 us -> 8.46 us  [the longest x4 4.72 us: sparse(): pl.pallas_call(partial(sparse_kernel, which, bits, tuple(offsets), here,...]
    ppermute x25, starting transfers between devices: 30.6 us -> 27.3 us  [swap(): return lax.ppermute(x, axis, [(i, i ^ mask) for i in range(size)])]
    unnamed x12 -> x8, local copies, waits for them, and re-layouts: 1.32 us -> 0.02 us
    concatenate x0 -> x1, other arithmetic: none -> 0.75 us  [on_device(): jnp.concatenate([block_rows[:, 0], block_cols[:, 0], tile_slot_count[0]])]
  transfers between devices with their start and end apart: 25 -> 25, of which waited for: 13 -> 11; matrix products, arithmetic and copies ran while one was open for 2% -> 2% of each run, Pallas kernels for 13% -> 11%
where the time goes in v3:
time: 61.4 us; the launch traced here: 61.5 us
  starting transfers between devices  27.3 us (44%)
  waiting for transfers between devices  22.3 us (36%)
  Pallas kernels  9.47 us (15%)
  between operations  1.48 us (2%)
  other arithmetic  0.98 us (2%)
    ppermute x25, starting transfers between devices, swap(): return lax.ppermute(x, axis, [(i, i ^ mask) for i in range(size)])  27.3 us
    ppermute x25, waiting for transfers between devices, swap(): return lax.ppermute(x, axis, [(i, i ^ mask) for i in range(size)])  22.3 us
    pallas_call x4, Pallas kernels, sparse(): pl.pallas_call(partial(sparse_kernel, which, bits, tuple(offsets), here,...  4.72 us
    pallas_call x1, Pallas kernels, prep(): pl.pallas_call(partial(prep_kernel, per, bits, late, first), out_shape=[j...  2.88 us
  transfers between devices with their start and end apart: 25, of which 11 were waited for; matrix products, arithmetic and copies ran while one was open for 2% of the time, Pallas kernels for 11%

profile of v3, /device:TPU:0, one launch (start us, length us, event | category | flops | bytes accessed | tf_op | source)
XLA Modules:
  0.0 61.5 jit_solution(2298701352468910002)
XLA Ops:
  0.7 5.1 %collective-permute-start.1 = (bf16[4,128,128]{2,1,0:T(8,128)(2,1)}, bf16[4,128,128]{2,1,0:T(8,128)(2,1)S(1)}, u32[]{:S(2)}, u32[]{:S(2)}) collective-permute-start(bf16[4,128,128]{2,1,0:T(8,128)(2,1)} %bitcast.7), channel_id=1, source_target_pairs={{0,24},{4,28},{8,16},{12,20},{16,8},{20,12},{24,0},{28,4},{1,25},{... | collective-permute-start | bytes 393224 | tf_op jit(solution)/shard_map/features_6/ppermute | solution.py:78
  5.8 1.5 %collective-permute-start = (bf16[4,128,128]{2,1,0:T(8,128)(2,1)}, bf16[4,128,128]{2,1,0:T(8,128)(2,1)S(1)}, u32[]{:S(2)}, u32[]{:S(2)}) collective-permute-start(bf16[4,128,128]{2,1,0:T(8,128)(2,1)} %bitcast.8), channel_id=1, source_target_pairs={{0,4},{4,0},{8,12},{12,8},{16,20},{20,16},{24,28},{28,24},{1,5},{5... | collective-permute-start | bytes 393224 | tf_op jit(solution)/shard_map/features_1/ppermute | solution.py:78
  7.9 0.7 %pad_add_fusion.indices = s32[161]{0:T(256)S(1)} fusion(s32[1]{0:T(128)} %bitcast.6, s32[80]{0:T(128)} %bitcast.12, s32[80]{0:T(128)} %bitcast.13), kind=kLoop, calls=%fused_computation.7 | loop fusion | flops 322 | bytes 1288 | tf_op jit(solution)/shard_map/concatenate | solution.py:416
  8.7 2.9 %shard_map.111 = (s32[168]{0:T(256)S(1)}, bf16[80,128,128]{2,1,0:T(8,128)(2,1)S(1)}) custom-call(s32[161]{0:T(256)S(1)} %pad_add_fusion.indices, bf16[80,128,128]{2,1,0:T(8,128)(2,1)} %blocks.1), custom_call_target="tpu_custom_call" | custom-call | flops 1 | bytes 1 | tf_op jit(solution)/shard_map/pallas_call | solution.py:179
  12.0 1.7 %collective-permute-start.5 = (bf16[4,128,128]{2,1,0:T(8,128)(2,1)S(1)}, bf16[4,128,128]{2,1,0:T(8,128)(2,1)S(1)}, u32[]{:S(2)}, u32[]{:S(2)}) collective-permute-start(bf16[4,128,128]{2,1,0:T(8,128)(2,1)S(1)} %bitcast.9), channel_id=1, source_target_pairs={{0,8},{4,12},{8,0},{12,4},{16,24},{20,28},{24,16},{28,20},{1,9},{5... | collective-permute-start | bytes 393224 | tf_op jit(solution)/shard_map/features_2/ppermute | solution.py:78
  14.0 1.5 %collective-permute-start.6 = (bf16[4,128,128]{2,1,0:T(8,128)(2,1)S(1)}, bf16[4,128,128]{2,1,0:T(8,128)(2,1)S(1)}, u32[]{:S(2)}, u32[]{:S(2)}) collective-permute-start(bf16[4,128,128]{2,1,0:T(8,128)(2,1)S(1)} %collective-permute-done.1.refs_6_), channel_id=1, source_target_pairs={{0,4},{4,0},{8,12},{12,8},{16,20},{20,16},{24,28},{28,24},{1,5},{5... | collective-permute-start | bytes 393224 | tf_op jit(solution)/shard_map/features_7/ppermute | solution.py:78
  15.5 2.5 %collective-permute-done.3.refs_5_ = bf16[4,128,128]{2,1,0:T(8,128)(2,1)S(1)} collective-permute-done((bf16[4,128,128]{2,1,0:T(8,128)(2,1)S(1)}, bf16[4,128,128]{2,1,0:T(8,128)(2,1)S(1)}, u32[]{:S(2)}, u32[]{:S(2)}) %collective-permute-start.3) | collective-permute-done | bytes 131104 | tf_op jit(solution)/shard_map/features_4/ppermute | solution.py:78
  18.1 0.5 collective-permute-start.4
  18.6 1.5 %collective-permute-start.7 = (bf16[512,128]{1,0:T(8,128)(2,1)S(1)}, bf16[512,128]{1,0:T(8,128)(2,1)S(1)}, u32[]{:S(2)}, u32[]{:S(2)}) collective-permute-start(bf16[512,128]{1,0:T(8,128)(2,1)S(1)} %copy-done.1), channel_id=1, source_target_pairs={{0,2},{1,3},{2,0},{3,1},{4,6},{5,7},{6,4},{7,5},{8,10},{9,11},{10,... | collective-permute-start | bytes 393224 | tf_op jit(solution)/shard_map/cotangent/ppermute | solution.py:78
  20.5 1.4 %shard_map.112.refs_4_ = f32[17,128,128]{2,1,0:T(8,128)S(1)} custom-call(s32[168]{0:T(256)S(1)} %get-tuple-element.45.refs_0_, bf16[80,128,128]{2,1,0:T(8,128)(2,1)S(1)} %get-tuple-element.46.refs_1_, bf16[4,128,128]{2,1,0:T(8,128)(2,1)S(1)} %bitcast.10, bf16[4,128,128]{2,1,0:T(8,128)(2,1)S(1)} %collective-permute-done.refs_3_, ...), custom_call_target="tpu_custom_call" | custom-call | flops 1 | bytes 1 | tf_op jit(solution)/shard_map/pallas_call | solution.py:289
  22.0 1.1 %collective-permute-done.4.refs_3_ = bf16[4,128,128]{2,1,0:T(8,128)(2,1)S(1)} collective-permute-done((bf16[4,128,128]{2,1,0:T(8,128)(2,1)S(1)}, bf16[4,128,128]{2,1,0:T(8,128)(2,1)S(1)}, u32[]{:S(2)}, u32[]{:S(2)}) %collective-permute-start.4) | collective-permute-done | bytes 131104 | tf_op jit(solution)/shard_map/features_5/ppermute | solution.py:78
  23.0 0.9 %shard_map.113 = (f32[4,128,128]{2,1,0:T(8,128)S(1)}, bf16[4,128,128]{2,1,0:T(8,128)(2,1)S(1)}, f32[4,128,128]{2,1,0:T(8,128)S(1)}, bf16[4,128,128]{2,1,0:T(8,128)(2,1)S(1)}) custom-call(s32[168]{0:T(256)S(1)} %get-tuple-element.45.refs_0_, bf16[80,128,128]{2,1,0:T(8,128)(2,1)S(1)} %get-tuple-element.46.refs_1_, ...), custom_call_target="tpu_custom_call" | custom-call | flops 1 | bytes 1 | tf_op jit(solution)/shard_map/pallas_call | solution.py:289
  24.5 0.8 %collective-permute-done.8 = bf16[4,128,128]{2,1,0:T(8,128)(2,1)S(1)} collective-permute-done((bf16[4,128,128]{2,1,0:T(8,128)(2,1)S(1)}, bf16[4,128,128]{2,1,0:T(8,128)(2,1)S(1)}, u32[]{:S(2)}, u32[]{:S(2)}) %collective-permute-start.8) | collective-permute-done | bytes 131104 | tf_op jit(solution)/shard_map/aggregate_1/ppermute | solution.py:78
  25.4 1.6 %collective-permute-start.11 = (bf16[4,128,128]{2,1,0:T(8,128)(2,1)S(1)}, bf16[4,128,128]{2,1,0:T(8,128)(2,1)S(1)}, u32[]{:S(2)}, u32[]{:S(2)}) collective-permute-start(bf16[4,128,128]{2,1,0:T(8,128)(2,1)S(1)} %add_convert_fusion.4.refs_0_), channel_id=1, source_target_pairs={{0,2},{1,3},{2,0},{3,1},{4,6},{5,7},{6,4},{7,5},{8,10},{9,11},{10,... | collective-permute-start | bytes 393224 | tf_op jit(solution)/shard_map/swap/ppermute | solution.py:78
  27.0 0.6 collective-permute-start.10
  27.6 4.2 %collective-permute-done.11.refs_4_ = bf16[4,128,128]{2,1,0:T(8,128)(2,1)S(1)} collective-permute-done((bf16[4,128,128]{2,1,0:T(8,128)(2,1)S(1)}, bf16[4,128,128]{2,1,0:T(8,128)(2,1)S(1)}, u32[]{:S(2)}, u32[]{:S(2)}) %collective-permute-start.11) | collective-permute-done | bytes 131104 | tf_op jit(solution)/shard_map/swap/ppermute | solution.py:78
  31.8 2.0 %collective-permute-done.10.refs_1_ = bf16[4,128,128]{2,1,0:T(8,128)(2,1)S(1)} collective-permute-done((bf16[4,128,128]{2,1,0:T(8,128)(2,1)S(1)}, bf16[4,128,128]{2,1,0:T(8,128)(2,1)S(1)}, u32[]{:S(2)}, u32[]{:S(2)}) %collective-permute-start.10) | collective-permute-done | bytes 131104 | tf_op jit(solution)/shard_map/swap/ppermute | solution.py:78
  33.8 1.0 %shard_map.114 = (bf16[512,128]{1,0:T(8,128)(2,1)}, bf16[4,128,128]{2,1,0:T(8,128)(2,1)S(1)}, bf16[4,128,128]{2,1,0:T(8,128)(2,1)S(1)}, f32[144,128]{1,0:T(8,128)S(1)}) custom-call(bf16[128,128]{1,0:T(8,128)(2,1)S(1)} %copy-done.2, f32[1,128]{1,0:T(1,128)S(1)} %bitcast.11, bf16[4,128,128]{2,1,0:T(8,128)(2,1)S(1)} %add_convert_fusion.4.refs_0_, ...), custom_call_target="tpu_custom_call" | custom-call | flops 1 | bytes 1 | tf_op jit(solution)/shard_map/pallas_call | solution.py:353
  34.8 0.5 collective-permute-start.14
  35.4 1.2 %collective-permute-done.12 = f32[144,128]{1,0:T(8,128)S(1)} collective-permute-done((f32[144,128]{1,0:T(8,128)S(1)}, f32[144,128]{1,0:T(8,128)S(1)}, u32[]{:S(2)}, u32[]{:S(2)}) %collective-permute-start.12) | collective-permute-done | bytes 73760 | tf_op jit(solution)/shard_map/swap/ppermute | solution.py:78
  36.6 1.0 %shard_map.115 = bf16[4,128,128]{2,1,0:T(8,128)(2,1)S(1)} custom-call(s32[168]{0:T(256)S(1)} %get-tuple-element.45.refs_0_, bf16[80,128,128]{2,1,0:T(8,128)(2,1)S(1)} %get-tuple-element.46.refs_1_, bf16[4,128,128]{2,1,0:T(8,128)(2,1)S(1)} %get-tuple-element.63.refs_2_, bf16[4,128,128]{2,1,0:T(8,128)(2,1)S(1)} %collective-permute-done.13.refs_3_, ...), custom_call_target="tpu_custom_call" | custom-call | flops 1 | bytes 1 | tf_op jit(solution)/shard_map/pallas_call | solution.py:289
  37.7 2.5 %collective-permute-start.16 = (bf16[4,128,128]{2,1,0:T(8,128)(2,1)S(1)}, bf16[4,128,128]{2,1,0:T(8,128)(2,1)S(1)}, u32[]{:S(2)}, u32[]{:S(2)}) collective-permute-start(bf16[4,128,128]{2,1,0:T(8,128)(2,1)S(1)} %shard_map.115), channel_id=1, source_target_pairs={{0,4},{4,0},{8,12},{12,8},{16,20},{20,16},{24,28},{28,24},{1,5},{5... | collective-permute-start | bytes 393224 | tf_op jit(solution)/shard_map/sums_5/ppermute | solution.py:78
  40.2 1.4 %shard_map.116 = (f32[4,128,128]{2,1,0:T(8,128)S(1)}, bf16[4,128,128]{2,1,0:T(8,128)(2,1)S(1)}, bf16[4,128,128]{2,1,0:T(8,128)(2,1)S(1)}, bf16[4,128,128]{2,1,0:...) custom-call(s32[168]{0:T(256)S(1)} %get-tuple-element.45.refs_0_, ...), custom_call_target="tpu_custom_call" | custom-call | flops 1 | bytes 1 | tf_op jit(solution)/shard_map/pallas_call | solution.py:289
  41.6 3.7 %collective-permute-start.19 = (bf16[4,128,128]{2,1,0:T(8,128)(2,1)S(1)}, bf16[4,128,128]{2,1,0:T(8,128)(2,1)S(1)}, u32[]{:S(2)}, u32[]{:S(2)}) collective-permute-start(bf16[4,128,128]{2,1,0:T(8,128)(2,1)S(1)} %get-tuple-element.69), channel_id=1, source_target_pairs={{0,4},{4,0},{8,12},{12,8},{16,20},{20,16},{24,28},{28,24},{1,5},{5... | collective-permute-start | bytes 393224 | tf_op jit(solution)/shard_map/sums_7/ppermute | solution.py:78
  45.3 0.7 %collective-permute-start.20 = (bf16[4,128,128]{2,1,0:T(8,128)(2,1)S(1)}, bf16[4,128,128]{2,1,0:T(8,128)(2,1)S(1)}, u32[]{:S(2)}, u32[]{:S(2)}) collective-permute-start(bf16[4,128,128]{2,1,0:T(8,128)(2,1)S(1)} %add_convert_fusion.2), channel_id=1, source_target_pairs={{0,8},{4,12},{8,0},{12,4},{16,24},{20,28},{24,16},{28,20},{1,9},{5... | collective-permute-start | bytes 393224 | tf_op jit(solution)/shard_map/sums_4/ppermute | solution.py:78
  46.0 1.4 %collective-permute-start.18 = (bf16[4,128,128]{2,1,0:T(8,128)(2,1)S(1)}, bf16[4,128,128]{2,1,0:T(8,128)(2,1)S(1)}, u32[]{:S(2)}, u32[]{:S(2)}) collective-permute-start(bf16[4,128,128]{2,1,0:T(8,128)(2,1)S(1)} %get-tuple-element.71), channel_id=1, source_target_pairs={{0,8},{4,12},{8,0},{12,4},{16,24},{20,28},{24,16},{28,20},{1,9},{5... | collective-permute-start | bytes 393224 | tf_op jit(solution)/shard_map/sums_3/ppermute | solution.py:78
  47.5 1.1 %collective-permute-done.19 = bf16[4,128,128]{2,1,0:T(8,128)(2,1)S(1)} collective-permute-done((bf16[4,128,128]{2,1,0:T(8,128)(2,1)S(1)}, bf16[4,128,128]{2,1,0:T(8,128)(2,1)S(1)}, u32[]{:S(2)}, u32[]{:S(2)}) %collective-permute-start.19) | collective-permute-done | bytes 131104 | tf_op jit(solution)/shard_map/sums_7/ppermute | solution.py:78
  48.6 3.0 %collective-permute-done.20 = bf16[4,128,128]{2,1,0:T(8,128)(2,1)S(1)} collective-permute-done((bf16[4,128,128]{2,1,0:T(8,128)(2,1)S(1)}, bf16[4,128,128]{2,1,0:T(8,128)(2,1)S(1)}, u32[]{:S(2)}, u32[]{:S(2)}) %collective-permute-start.20) | collective-permute-done | bytes 131104 | tf_op jit(solution)/shard_map/sums_4/ppermute | solution.py:78
  51.8 1.9 %collective-permute-done.18 = bf16[4,128,128]{2,1,0:T(8,128)(2,1)S(1)} collective-permute-done((bf16[4,128,128]{2,1,0:T(8,128)(2,1)S(1)}, bf16[4,128,128]{2,1,0:T(8,128)(2,1)S(1)}, u32[]{:S(2)}, u32[]{:S(2)}) %collective-permute-start.18) | collective-permute-done | bytes 131104 | tf_op jit(solution)/shard_map/sums_3/ppermute | solution.py:78
  54.1 2.5 %collective-permute-start.24 = (bf16[4,128,128]{2,1,0:T(8,128)(2,1)S(1)}, bf16[4,128,128]{2,1,0:T(8,128)(2,1)S(1)}, u32[]{:S(2)}, u32[]{:S(2)}) collective-permute-start(bf16[4,128,128]{2,1,0:T(8,128)(2,1)S(1)} %get-tuple-element.79), channel_id=1, source_target_pairs={{0,8},{4,12},{8,0},{12,4},{16,24},{20,28},{24,16},{28,20},{1,9},{5... | collective-permute-start | bytes 393224 | tf_op jit(solution)/shard_map/sums_2/ppermute | solution.py:78
  56.7 3.9 %collective-permute-done.21.refs_1_ = bf16[144,128]{1,0:T(8,128)(2,1)S(1)} collective-permute-done((bf16[144,128]{1,0:T(8,128)(2,1)S(1)}, bf16[144,128]{1,0:T(8,128)(2,1)S(1)}, u32[]{:S(2)}, u32[]{:S(2)}) %collective-permute-start.21) | collective-permute-done | bytes 36896 | tf_op jit(solution)/shard_map/gradients_2/ppermute | solution.py:78
  60.7 0.9 %shard_map.117 = (f32[512,128]{1,0:T(8,128)}, f32[128,128]{1,0:T(8,128)}, f32[1,128]{1,0:T(1,128)}) custom-call(bf16[144,128]{1,0:T(8,128)(2,1)S(1)} %add_convert_fusion.5.refs_0_, bf16[144,128]{1,0:T(8,128)(2,1)S(1)} %collective-permute-done.21.refs_1_, f32[4,128,128]{2,1,0:T(8,128)S(1)} %get-tuple-element.82.refs_2_, ...), custom_call_target="tpu_custom_call" | custom-call | flops 1 | bytes 1 | tf_op jit(solution)/shard_map/pallas_call | solution.py:384
  (42 shorter events, 2.8 us)
Async XLA Ops:
  0.6 11.4 %copy-start = (bf16[512,128]{1,0:T(8,128)(2,1)S(1)}, bf16[512,128]{1,0:T(8,128)(2,1)}, u32[]{:S(2)}) copy-start(bf16[512,128]{1,0:T(8,128)(2,1)} %param.8) | copy-start | bytes 393220
  0.6 18.0 %copy-start.1 = (bf16[512,128]{1,0:T(8,128)(2,1)S(1)}, bf16[512,128]{1,0:T(8,128)(2,1)}, u32[]{:S(2)}) copy-start(bf16[512,128]{1,0:T(8,128)(2,1)} %refs_2_.1) | copy-start | bytes 393220
  0.7 10.9 %collective-permute-start.1 = (bf16[4,128,128]{2,1,0:T(8,128)(2,1)}, bf16[4,128,128]{2,1,0:T(8,128)(2,1)S(1)}, u32[]{:S(2)}, u32[]{:S(2)}) collective-permute-start(bf16[4,128,128]{2,1,0:T(8,128)(2,1)} %bitcast.7), channel_id=1, source_target_pairs={{0,24},{4,28},{8,16},{12,20},{16,8},{20,12},{24,0},{28,4},{1,25},{... | collective-permute-start | bytes 393224 | tf_op jit(solution)/shard_map/features_6/ppermute | solution.py:78
  5.8 7.9 %collective-permute-start = (bf16[4,128,128]{2,1,0:T(8,128)(2,1)}, bf16[4,128,128]{2,1,0:T(8,128)(2,1)S(1)}, u32[]{:S(2)}, u32[]{:S(2)}) collective-permute-start(bf16[4,128,128]{2,1,0:T(8,128)(2,1)} %bitcast.8), channel_id=1, source_target_pairs={{0,4},{4,0},{8,12},{12,8},{16,20},{20,16},{24,28},{28,24},{1,5},{5... | collective-permute-start | bytes 393224 | tf_op jit(solution)/shard_map/features_1/ppermute | solution.py:78
  11.6 6.5 %collective-permute-start.3 = (bf16[4,128,128]{2,1,0:T(8,128)(2,1)S(1)}, bf16[4,128,128]{2,1,0:T(8,128)(2,1)S(1)}, u32[]{:S(2)}, u32[]{:S(2)}) collective-permute-start(bf16[4,128,128]{2,1,0:T(8,128)(2,1)S(1)} %collective-permute-done.1.refs_6_), channel_id=1, source_target_pairs={{0,8},{4,12},{8,0},{12,4},{16,24},{20,28},{24,16},{28,20},{1,9},{5... | collective-permute-start | bytes 393224 | tf_op jit(solution)/shard_map/features_4/ppermute | solution.py:78
  12.0 8.5 %collective-permute-start.5 = (bf16[4,128,128]{2,1,0:T(8,128)(2,1)S(1)}, bf16[4,128,128]{2,1,0:T(8,128)(2,1)S(1)}, u32[]{:S(2)}, u32[]{:S(2)}) collective-permute-start(bf16[4,128,128]{2,1,0:T(8,128)(2,1)S(1)} %bitcast.9), channel_id=1, source_target_pairs={{0,8},{4,12},{8,0},{12,4},{16,24},{20,28},{24,16},{28,20},{1,9},{5... | collective-permute-start | bytes 393224 | tf_op jit(solution)/shard_map/features_2/ppermute | solution.py:78
  13.7 8.3 %collective-permute-start.2 = (bf16[4,128,128]{2,1,0:T(8,128)(2,1)S(1)}, bf16[4,128,128]{2,1,0:T(8,128)(2,1)S(1)}, u32[]{:S(2)}, u32[]{:S(2)}) collective-permute-start(bf16[4,128,128]{2,1,0:T(8,128)(2,1)S(1)} %collective-permute-done.refs_3_), channel_id=1, source_target_pairs={{0,8},{4,12},{8,0},{12,4},{16,24},{20,28},{24,16},{28,20},{1,9},{5... | collective-permute-start | bytes 393224 | tf_op jit(solution)/shard_map/features_3/ppermute | solution.py:78
  14.0 6.5 %collective-permute-start.6 = (bf16[4,128,128]{2,1,0:T(8,128)(2,1)S(1)}, bf16[4,128,128]{2,1,0:T(8,128)(2,1)S(1)}, u32[]{:S(2)}, u32[]{:S(2)}) collective-permute-start(bf16[4,128,128]{2,1,0:T(8,128)(2,1)S(1)} %collective-permute-done.1.refs_6_), channel_id=1, source_target_pairs={{0,4},{4,0},{8,12},{12,8},{16,20},{20,16},{24,28},{28,24},{1,5},{5... | collective-permute-start | bytes 393224 | tf_op jit(solution)/shard_map/features_7/ppermute | solution.py:78
  18.1 5.0 %collective-permute-start.4 = (bf16[4,128,128]{2,1,0:T(8,128)(2,1)S(1)}, bf16[4,128,128]{2,1,0:T(8,128)(2,1)S(1)}, u32[]{:S(2)}, u32[]{:S(2)}) collective-permute-start(bf16[4,128,128]{2,1,0:T(8,128)(2,1)S(1)} %collective-permute-done.3.refs_5_), channel_id=1, source_target_pairs={{0,4},{4,0},{8,12},{12,8},{16,20},{20,16},{24,28},{28,24},{1,5},{5... | collective-permute-start | bytes 393224 | tf_op jit(solution)/shard_map/features_5/ppermute | solution.py:78
  18.6 5.4 %collective-permute-start.7 = (bf16[512,128]{1,0:T(8,128)(2,1)S(1)}, bf16[512,128]{1,0:T(8,128)(2,1)S(1)}, u32[]{:S(2)}, u32[]{:S(2)}) collective-permute-start(bf16[512,128]{1,0:T(8,128)(2,1)S(1)} %copy-done.1), channel_id=1, source_target_pairs={{0,2},{1,3},{2,0},{3,1},{4,6},{5,7},{6,4},{7,5},{8,10},{9,11},{10,... | collective-permute-start | bytes 393224 | tf_op jit(solution)/shard_map/cotangent/ppermute | solution.py:78
  21.9 11.9 %copy-start.2 = (bf16[128,128]{1,0:T(8,128)(2,1)S(1)}, bf16[128,128]{1,0:T(8,128)(2,1)}, u32[]{:S(2)}) copy-start(bf16[128,128]{1,0:T(8,128)(2,1)} %weight.1) | copy-start | bytes 98308
  21.9 11.9 %copy-start.3 = (f32[128]{0:T(128)S(1)}, f32[128]{0:T(128)}, u32[]{:S(2)}) copy-start(f32[128]{0:T(128)} %param.10) | copy-start | bytes 1540
  23.9 1.4 %collective-permute-start.8 = (bf16[4,128,128]{2,1,0:T(8,128)(2,1)S(1)}, bf16[4,128,128]{2,1,0:T(8,128)(2,1)S(1)}, u32[]{:S(2)}, u32[]{:S(2)}) collective-permute-start(bf16[4,128,128]{2,1,0:T(8,128)(2,1)S(1)} %get-tuple-element.57), channel_id=1, source_target_pairs={{0,1},{1,0},{2,3},{3,2},{4,5},{5,4},{6,7},{7,6},{8,9},{9,8},{10,11... | collective-permute-start | bytes 393224 | tf_op jit(solution)/shard_map/aggregate_1/ppermute | solution.py:78
  24.0 2.9 %collective-permute-start.9 = (bf16[4,128,128]{2,1,0:T(8,128)(2,1)S(1)}, bf16[4,128,128]{2,1,0:T(8,128)(2,1)S(1)}, u32[]{:S(2)}, u32[]{:S(2)}) collective-permute-start(bf16[4,128,128]{2,1,0:T(8,128)(2,1)S(1)} %get-tuple-element.59), channel_id=1, source_target_pairs={{0,1},{1,0},{2,3},{3,2},{4,5},{5,4},{6,7},{7,6},{8,9},{9,8},{10,11... | collective-permute-start | bytes 393224 | tf_op jit(solution)/shard_map/aggregate_3/ppermute | solution.py:78
  25.4 6.4 %collective-permute-start.11 = (bf16[4,128,128]{2,1,0:T(8,128)(2,1)S(1)}, bf16[4,128,128]{2,1,0:T(8,128)(2,1)S(1)}, u32[]{:S(2)}, u32[]{:S(2)}) collective-permute-start(bf16[4,128,128]{2,1,0:T(8,128)(2,1)S(1)} %add_convert_fusion.4.refs_0_), channel_id=1, source_target_pairs={{0,2},{1,3},{2,0},{3,1},{4,6},{5,7},{6,4},{7,5},{8,10},{9,11},{10,... | collective-permute-start | bytes 393224 | tf_op jit(solution)/shard_map/swap/ppermute | solution.py:78
  27.0 6.8 %collective-permute-start.10 = (bf16[4,128,128]{2,1,0:T(8,128)(2,1)S(1)}, bf16[4,128,128]{2,1,0:T(8,128)(2,1)S(1)}, u32[]{:S(2)}, u32[]{:S(2)}) collective-permute-start(bf16[4,128,128]{2,1,0:T(8,128)(2,1)S(1)} %add_convert_fusion.3.refs_3_), channel_id=1, source_target_pairs={{0,2},{1,3},{2,0},{3,1},{4,6},{5,7},{6,4},{7,5},{8,10},{9,11},{10,... | collective-permute-start | bytes 393224 | tf_op jit(solution)/shard_map/swap/ppermute | solution.py:78
  34.8 1.8 %collective-permute-start.13 = (bf16[4,128,128]{2,1,0:T(8,128)(2,1)S(1)}, bf16[4,128,128]{2,1,0:T(8,128)(2,1)S(1)}, u32[]{:S(2)}, u32[]{:S(2)}) collective-permute-start(bf16[4,128,128]{2,1,0:T(8,128)(2,1)S(1)} %get-tuple-element.63.refs_2_), channel_id=1, source_target_pairs={{0,1},{1,0},{2,3},{3,2},{4,5},{5,4},{6,7},{7,6},{8,9},{9,8},{10,11... | collective-permute-start | bytes 393224 | tf_op jit(solution)/shard_map/rows_1/ppermute | solution.py:78
  34.8 1.8 %collective-permute-start.14 = (bf16[4,128,128]{2,1,0:T(8,128)(2,1)S(1)}, bf16[4,128,128]{2,1,0:T(8,128)(2,1)S(1)}, u32[]{:S(2)}, u32[]{:S(2)}) collective-permute-start(bf16[4,128,128]{2,1,0:T(8,128)(2,1)S(1)} %get-tuple-element.64.refs_4_), channel_id=1, source_target_pairs={{0,1},{1,0},{2,3},{3,2},{4,5},{5,4},{6,7},{7,6},{8,9},{9,8},{10,11... | collective-permute-start | bytes 393224 | tf_op jit(solution)/shard_map/rows_3/ppermute | solution.py:78
  35.3 1.3 %collective-permute-start.12 = (f32[144,128]{1,0:T(8,128)S(1)}, f32[144,128]{1,0:T(8,128)S(1)}, u32[]{:S(2)}, u32[]{:S(2)}) collective-permute-start(f32[144,128]{1,0:T(8,128)S(1)} %get-tuple-element.61), channel_id=1, source_target_pairs={{0,1},{1,0},{2,3},{3,2},{4,5},{5,4},{6,7},{7,6},{8,9},{9,8},{10,11... | collective-permute-start | bytes 221192 | tf_op jit(solution)/shard_map/swap/ppermute | solution.py:78
  37.7 7.6 %collective-permute-start.16 = (bf16[4,128,128]{2,1,0:T(8,128)(2,1)S(1)}, bf16[4,128,128]{2,1,0:T(8,128)(2,1)S(1)}, u32[]{:S(2)}, u32[]{:S(2)}) collective-permute-start(bf16[4,128,128]{2,1,0:T(8,128)(2,1)S(1)} %shard_map.115), channel_id=1, source_target_pairs={{0,4},{4,0},{8,12},{12,8},{16,20},{20,16},{24,28},{28,24},{1,5},{5... | collective-permute-start | bytes 393224 | tf_op jit(solution)/shard_map/sums_5/ppermute | solution.py:78
  40.1 7.3 %collective-permute-start.15 = (bf16[144,128]{1,0:T(8,128)(2,1)S(1)}, bf16[144,128]{1,0:T(8,128)(2,1)S(1)}, u32[]{:S(2)}, u32[]{:S(2)}) collective-permute-start(bf16[144,128]{1,0:T(8,128)(2,1)S(1)} %add.29), channel_id=1, source_target_pairs={{0,4},{4,0},{8,12},{12,8},{16,20},{20,16},{24,28},{28,24},{1,5},{5... | collective-permute-start | bytes 110600 | tf_op jit(solution)/shard_map/gradients_1/ppermute | solution.py:78
  41.6 7.0 %collective-permute-start.19 = (bf16[4,128,128]{2,1,0:T(8,128)(2,1)S(1)}, bf16[4,128,128]{2,1,0:T(8,128)(2,1)S(1)}, u32[]{:S(2)}, u32[]{:S(2)}) collective-permute-start(bf16[4,128,128]{2,1,0:T(8,128)(2,1)S(1)} %get-tuple-element.69), channel_id=1, source_target_pairs={{0,4},{4,0},{8,12},{12,8},{16,20},{20,16},{24,28},{28,24},{1,5},{5... | collective-permute-start | bytes 393224 | tf_op jit(solution)/shard_map/sums_7/ppermute | solution.py:78
  45.3 6.2 %collective-permute-start.20 = (bf16[4,128,128]{2,1,0:T(8,128)(2,1)S(1)}, bf16[4,128,128]{2,1,0:T(8,128)(2,1)S(1)}, u32[]{:S(2)}, u32[]{:S(2)}) collective-permute-start(bf16[4,128,128]{2,1,0:T(8,128)(2,1)S(1)} %add_convert_fusion.2), channel_id=1, source_target_pairs={{0,8},{4,12},{8,0},{12,4},{16,24},{20,28},{24,16},{28,20},{1,9},{5... | collective-permute-start | bytes 393224 | tf_op jit(solution)/shard_map/sums_4/ppermute | solution.py:78
  46.0 7.7 %collective-permute-start.18 = (bf16[4,128,128]{2,1,0:T(8,128)(2,1)S(1)}, bf16[4,128,128]{2,1,0:T(8,128)(2,1)S(1)}, u32[]{:S(2)}, u32[]{:S(2)}) collective-permute-start(bf16[4,128,128]{2,1,0:T(8,128)(2,1)S(1)} %get-tuple-element.71), channel_id=1, source_target_pairs={{0,8},{4,12},{8,0},{12,4},{16,24},{20,28},{24,16},{28,20},{1,9},{5... | collective-permute-start | bytes 393224 | tf_op jit(solution)/shard_map/sums_3/ppermute | solution.py:78
  47.5 9.2 %collective-permute-start.17 = (bf16[144,128]{1,0:T(8,128)(2,1)S(1)}, bf16[144,128]{1,0:T(8,128)(2,1)S(1)}, u32[]{:S(2)}, u32[]{:S(2)}) collective-permute-start(bf16[144,128]{1,0:T(8,128)(2,1)S(1)} %add_convert_fusion.6), channel_id=1, source_target_pairs={{0,24},{4,28},{8,16},{12,20},{16,8},{20,12},{24,0},{28,4},{1,25},{... | collective-permute-start | bytes 110600 | tf_op jit(solution)/shard_map/gradients_6/ppermute | solution.py:78
  51.6 9.0 %collective-permute-start.22 = (bf16[4,128,128]{2,1,0:T(8,128)(2,1)S(1)}, bf16[4,128,128]{2,1,0:T(8,128)(2,1)S(1)}, u32[]{:S(2)}, u32[]{:S(2)}) collective-permute-start(bf16[4,128,128]{2,1,0:T(8,128)(2,1)S(1)} %add_convert_fusion), channel_id=1, source_target_pairs={{0,24},{4,28},{8,16},{12,20},{16,8},{20,12},{24,0},{28,4},{1,25},{... | collective-permute-start | bytes 393224 | tf_op jit(solution)/shard_map/sums_6/ppermute | solution.py:78
  53.8 6.9 %collective-permute-start.23 = (bf16[4,128,128]{2,1,0:T(8,128)(2,1)S(1)}, bf16[4,128,128]{2,1,0:T(8,128)(2,1)S(1)}, u32[]{:S(2)}, u32[]{:S(2)}) collective-permute-start(bf16[4,128,128]{2,1,0:T(8,128)(2,1)S(1)} %add_convert_fusion.1), channel_id=1, source_target_pairs={{0,4},{4,0},{8,12},{12,8},{16,20},{20,16},{24,28},{28,24},{1,5},{5... | collective-permute-start | bytes 393224 | tf_op jit(solution)/shard_map/sums_1/ppermute | solution.py:78
  54.1 6.5 %collective-permute-start.24 = (bf16[4,128,128]{2,1,0:T(8,128)(2,1)S(1)}, bf16[4,128,128]{2,1,0:T(8,128)(2,1)S(1)}, u32[]{:S(2)}, u32[]{:S(2)}) collective-permute-start(bf16[4,128,128]{2,1,0:T(8,128)(2,1)S(1)} %get-tuple-element.79), channel_id=1, source_target_pairs={{0,8},{4,12},{8,0},{12,4},{16,24},{20,28},{24,16},{28,20},{1,9},{5... | collective-permute-start | bytes 393224 | tf_op jit(solution)/shard_map/sums_2/ppermute | solution.py:78
  56.6 4.0 %collective-permute-start.21 = (bf16[144,128]{1,0:T(8,128)(2,1)S(1)}, bf16[144,128]{1,0:T(8,128)(2,1)S(1)}, u32[]{:S(2)}, u32[]{:S(2)}) collective-permute-start(bf16[144,128]{1,0:T(8,128)(2,1)S(1)} %add_convert_fusion.5.refs_0_), channel_id=1, source_target_pairs={{0,8},{4,12},{8,0},{12,4},{16,24},{20,28},{24,16},{28,20},{1,9},{5... | collective-permute-start | bytes 110600 | tf_op jit(solution)/shard_map/gradients_2/ppermute | solution.py:78

commit v4 on v3

--- a/solution.py
+++ b/solution.py
@@ -306,58 +306,50 @@
     )(*operands)
 
 
-def dense_kernel(scaling, count, weight, bias, *refs):
-    parts = [refs[3 * n : 3 * n + 3] for n in range(count)]
-    hidden, *backs, grads = refs[3 * count :]
-    weight_grad = bias_grad = None
-    for n, (mine, theirs, cotangent) in enumerate(parts):
-        rows, channels = cotangent.shape[0], mine.shape[-1]
-        aggregate = mine[...].astype(jnp.float32) + theirs[...].astype(jnp.float32)
-        aggregate_b = aggregate.astype(jnp.bfloat16).reshape(rows, channels)
-        v = jnp.dot(aggregate_b, weight[...], preferred_element_type=jnp.float32) + bias[...]
-        square = v * v
-        t = jnp.tanh(C0 * (v + C1 * (v * square)))
-        half = 0.5 * (1.0 + t)
-        if n == 0:
-            hidden[...] = (v * half).astype(jnp.bfloat16)
-        slope = half + (0.5 * v) * (1.0 - t * t) * (C0 * (1.0 + (3.0 * C1) * square))
-        dpreact = cotangent[...].astype(jnp.float32) * slope
-        dpreact_b = dpreact.astype(jnp.bfloat16)
-        for m in range(rows // BS):
-            backs[n][m] = lax.dot_general(
-                weight[...],
-                dpreact_b[m * BS : (m + 1) * BS],
-                (((1,), (1,)), ((), ())),
-                preferred_element_type=jnp.float32,
-            ).astype(jnp.bfloat16)
-        weight_part = scaling * lax.dot_general(
-            aggregate_b, dpreact_b, (((0,), (0,)), ((), ())), preferred_element_type=jnp.float32
-        )
-        bias_part = scaling * jnp.sum(dpreact, axis=0, keepdims=True)
-        if n == 0:
-            weight_grad, bias_grad = weight_part, bias_part
-        else:
-            weight_grad, bias_grad = weight_grad + weight_part, bias_grad + bias_part
-    channels = weight.shape[0]
-    grads[:channels] = weight_grad
-    grads[channels:] = jnp.broadcast_to(bias_grad, (grads.shape[0] - channels, bias_grad.shape[1]))
-
-
-def dense(weight, bias, parts, scaling):
-    cotangent = parts[0][2]
+def dense_kernel(scaling, own, mine, theirs, weight, bias, cotangent, *outs):
+    rows, channels = cotangent.shape[0], mine.shape[-1]
+    back, grads = outs[-2:]
+    aggregate = mine[...].astype(jnp.float32) + theirs[...].astype(jnp.float32)
+    aggregate_b = aggregate.astype(jnp.bfloat16).reshape(rows, channels)
+    v = jnp.dot(aggregate_b, weight[...], preferred_element_type=jnp.float32) + bias[...]
+    square = v * v
+    t = jnp.tanh(C0 * (v + C1 * (v * square)))
+    half = 0.5 * (1.0 + t)
+    if own:
+        outs[0][...] = (v * half).astype(jnp.bfloat16)
+    slope = half + (0.5 * v) * (1.0 - t * t) * (C0 * (1.0 + (3.0 * C1) * square))
+    dpreact = cotangent[...].astype(jnp.float32) * slope
+    dpreact_b = dpreact.astype(jnp.bfloat16)
+    for n in range(rows // BS):
+        back[n] = lax.dot_general(
+            weight[...],
+            dpreact_b[n * BS : (n + 1) * BS],
+            (((1,), (1,)), ((), ())),
+            preferred_element_type=jnp.float32,
+        ).astype(jnp.bfloat16)
+    grads[:channels] = scaling * lax.dot_general(
+        aggregate_b, dpreact_b, (((0,), (0,)), ((), ())), preferred_element_type=jnp.float32
+    )
+    bias_grad = scaling * jnp.sum(dpreact, axis=0, keepdims=True)
+    grads[channels:] = jnp.broadcast_to(bias_grad, (grads.shape[0] - channels, grads.shape[1]))
+
+
+def dense(mine, theirs, weight, bias, cotangent, scaling, own):
     rows, (channels, units) = cotangent.shape[0], weight.shape
-    out_shape = [jax.ShapeDtypeStruct(cotangent.shape, jnp.bfloat16)]
-    out_shape += [jax.ShapeDtypeStruct((rows // BS, channels, BS), jnp.bfloat16)] * len(parts)
-    out_shape.append(jax.ShapeDtypeStruct((channels + 16, units), jnp.float32))
-    operands = [weight, bias] + [x for part in parts for x in part]
+    out_shape = [
+        jax.ShapeDtypeStruct((rows // BS, channels, BS), jnp.bfloat16),
+        jax.ShapeDtypeStruct((channels + 16, units), jnp.float32),
+    ]
+    if own:
+        out_shape.insert(0, pltpu.VMEM(cotangent.shape, jnp.bfloat16))
     return pl.pallas_call(
-        partial(dense_kernel, scaling, len(parts)),
+        partial(dense_kernel, scaling, own),
         out_shape=out_shape,
-        in_specs=[VMEM] * len(operands),
+        in_specs=[VMEM] * 5,
         out_specs=[VMEM] * len(out_shape),
-        compiler_params=pltpu.CompilerParams(vmem_limit_bytes=32 << 20),
+        compiler_params=pltpu.CompilerParams(vmem_limit_bytes=24 << 20),
         cost_estimate=QUICK,
-    )(*operands)
+    )(mine, theirs, weight, bias, cotangent)
 
 
 def finish_kernel(*refs):
@@ -400,6 +392,7 @@
     row_blocks, column_blocks = per * col_devices, per * row_devices
     inner = inner_of(row_devices)
     on_row = tree(row_devices // inner, inner, True)
+    off_row = tree(row_devices // inner, inner, False)
     on_col = tree(col_devices // 2, 2, False)
     across = col_devices - 2
     on_col = [route for route in on_col if route[0] != across]
@@ -442,16 +435,16 @@
     to_mine, to_others = swap(others, "col", across), swap(mine, "col", across)
     scaling = 1.0 / math.sqrt(own_rows * row_devices * col_devices)
     bias = bias_terms.reshape(1, -1)
-    hidden, back, other_back, grads = dense(
-        weight, bias,
-        [(mine, to_mine, cotangent), (others, to_others, other_cotangent)], scaling,
+    hidden, back, grads = dense(mine, to_mine, weight, bias, cotangent, scaling, True)
+    other_back, other_grads = dense(
+        others, to_others, weight, bias, other_cotangent, scaling, False
     )
+    grads = grads + other_grads
     grads = grads + swap(grads, "col", 1)
     for mask in mirror_masks(col_devices // 2)[1:]:
         grads = grads + swap(grads, "col", 2 * mask)
 
     rows = spread({0: back, across: other_back}, "col", on_col)
-    rows[0] = after(rows[0], grads)
     types = {d: jnp.bfloat16 if d else jnp.float32 for d in range(row_devices)}
     rest = [d for d in range(row_devices) if d not in first]
     leave_first, leave_last = [
@@ -466,18 +459,19 @@
     terms = {d: [p] for d, p in sums.items()}
     queue = Queue()
     top = chain[-2]
+    stages = {d: depth_of(d, off_row) + (d < inner) for d, _ in off_row}
     order = sorted(
-        on_row, key=lambda r: (-depths[r[0]], r[0] != top ^ 1, r[0] not in chain, r[0])
+        off_row, key=lambda r: (-stages[r[0]], r[0] != top ^ 1, r[0] not in chain, -r[0])
     )
     masks = [d ^ parent for d, parent in zip(chain, chain[1:])]
-    masks = masks[:1] + masks[-1:] + masks[1:-1]
+    masks = masks[1:] + masks[:1]
     masks += [m for m in mirror_masks(inner) if m not in masks]
     masks += [inner * m for m in mirror_masks(row_devices // inner) if inner * m not in masks]
     mine, theirs = grads.astype(jnp.bfloat16), None
     for n, (offset, parent) in enumerate(order):
         total = add(terms.pop(offset)).astype(jnp.bfloat16)
         terms[parent].append(queue.swap(total, "row", offset ^ parent, f"sums_{offset}"))
-        if n + 1 < len(order) and depths[order[n + 1][0]] == depths[offset]:
+        if n + 1 < len(order) and stages[order[n + 1][0]] == stages[offset]:
             continue
         for mask in masks[:1] if n + 1 < len(order) else masks:
             if theirs is not None:

time: 61.4 us -> 59 us (0.961)
  waiting for transfers between devices: 22.3 us -> 17.9 us
  Pallas kernels: 9.47 us -> 13.5 us
  starting transfers between devices: 27.3 us -> 24.1 us
  local copies, waits for them, and re-layouts: 0.02 us -> 0.68 us
    ppermute x25, waiting for transfers between devices: 22.3 us -> 17.9 us  [swap(): return lax.ppermute(x, axis, [(i, i ^ mask) for i in range(size)])]
    pallas_call x4, Pallas kernels: 4.72 us -> 8.7 us  [sparse(): pl.pallas_call(partial(sparse_kernel, which, bits, tuple(offsets), here,...]
    ppermute x25, starting transfers between devices: 27.3 us -> 24.1 us  [swap(): return lax.ppermute(x, axis, [(i, i ^ mask) for i in range(size)])]
    unnamed x8 -> x9, local copies, waits for them, and re-layouts: 0.02 us -> 0.68 us
  transfers between devices with their start and end apart: 25 -> 25, of which waited for: 11 -> 13; matrix products, arithmetic and copies ran while one was open for 2% -> 3% of each run, Pallas kernels for 11% -> 22%
where the time goes in v4:
time: 59 us; the launch traced here: 58.7 us
  starting transfers between devices  24.1 us (41%)
  waiting for transfers between devices  17.9 us (30%)
  Pallas kernels  13.5 us (23%)
  between operations  1.5 us (3%)
  other arithmetic  1 us (2%)
  local copies, waits for them, and re-layouts  0.68 us (1%)
    ppermute x25, starting transfers between devices, swap(): return lax.ppermute(x, axis, [(i, i ^ mask) for i in range(size)])  24.1 us
    ppermute x25, waiting for transfers between devices, swap(): return lax.ppermute(x, axis, [(i, i ^ mask) for i in range(size)])  17.9 us
    pallas_call x4, Pallas kernels, sparse(): pl.pallas_call(partial(sparse_kernel, which, bits, tuple(offsets), here,...  8.7 us
    pallas_call x1, Pallas kernels, prep(): pl.pallas_call(partial(prep_kernel, per, bits, late, first), out_shape=[j...  2.88 us
  transfers between devices with their start and end apart: 25, of which 13 were waited for; matrix products, arithmetic and copies ran while one was open for 3% of the time, Pallas kernels for 22%

profile of v4, /device:TPU:0, one launch (start us, length us, event | category | flops | bytes accessed | tf_op | source)
XLA Modules:
  0.0 58.7 jit_solution(16835813144085211568)
XLA Ops:
  0.7 5.1 %collective-permute-start.1 = (bf16[4,128,128]{2,1,0:T(8,128)(2,1)}, bf16[4,128,128]{2,1,0:T(8,128)(2,1)S(1)}, u32[]{:S(2)}, u32[]{:S(2)}) collective-permute-start(bf16[4,128,128]{2,1,0:T(8,128)(2,1)} %bitcast.7), channel_id=1, source_target_pairs={{0,24},{4,28},{8,16},{12,20},{16,8},{20,12},{24,0},{28,4},{1,25},{... | collective-permute-start | bytes 393224 | tf_op jit(solution)/shard_map/features_6/ppermute | solution.py:78
  5.8 1.5 %collective-permute-start = (bf16[4,128,128]{2,1,0:T(8,128)(2,1)}, bf16[4,128,128]{2,1,0:T(8,128)(2,1)S(1)}, u32[]{:S(2)}, u32[]{:S(2)}) collective-permute-start(bf16[4,128,128]{2,1,0:T(8,128)(2,1)} %bitcast.8), channel_id=1, source_target_pairs={{0,4},{4,0},{8,12},{12,8},{16,20},{20,16},{24,28},{28,24},{1,5},{5... | collective-permute-start | bytes 393224 | tf_op jit(solution)/shard_map/features_1/ppermute | solution.py:78
  7.9 0.7 %pad_add_fusion.indices = s32[161]{0:T(256)S(1)} fusion(s32[1]{0:T(128)} %bitcast.6, s32[80]{0:T(128)} %bitcast.13, s32[80]{0:T(128)} %bitcast.14), kind=kLoop, calls=%fused_computation.8 | loop fusion | flops 322 | bytes 1288 | tf_op jit(solution)/shard_map/concatenate | solution.py:409
  8.7 2.9 %shard_map.111 = (s32[168]{0:T(256)S(1)}, bf16[80,128,128]{2,1,0:T(8,128)(2,1)S(1)}) custom-call(s32[161]{0:T(256)S(1)} %pad_add_fusion.indices, bf16[80,128,128]{2,1,0:T(8,128)(2,1)} %blocks.1), custom_call_target="tpu_custom_call" | custom-call | flops 1 | bytes 1 | tf_op jit(solution)/shard_map/pallas_call | solution.py:179
  12.0 1.7 %collective-permute-start.5 = (bf16[4,128,128]{2,1,0:T(8,128)(2,1)S(1)}, bf16[4,128,128]{2,1,0:T(8,128)(2,1)S(1)}, u32[]{:S(2)}, u32[]{:S(2)}) collective-permute-start(bf16[4,128,128]{2,1,0:T(8,128)(2,1)S(1)} %bitcast.9), channel_id=1, source_target_pairs={{0,8},{4,12},{8,0},{12,4},{16,24},{20,28},{24,16},{28,20},{1,9},{5... | collective-permute-start | bytes 393224 | tf_op jit(solution)/shard_map/features_2/ppermute | solution.py:78
  14.0 1.5 %collective-permute-start.6 = (bf16[4,128,128]{2,1,0:T(8,128)(2,1)S(1)}, bf16[4,128,128]{2,1,0:T(8,128)(2,1)S(1)}, u32[]{:S(2)}, u32[]{:S(2)}) collective-permute-start(bf16[4,128,128]{2,1,0:T(8,128)(2,1)S(1)} %collective-permute-done.1.refs_6_), channel_id=1, source_target_pairs={{0,4},{4,0},{8,12},{12,8},{16,20},{20,16},{24,28},{28,24},{1,5},{5... | collective-permute-start | bytes 393224 | tf_op jit(solution)/shard_map/features_7/ppermute | solution.py:78
  15.5 2.5 %collective-permute-done.3.refs_5_ = bf16[4,128,128]{2,1,0:T(8,128)(2,1)S(1)} collective-permute-done((bf16[4,128,128]{2,1,0:T(8,128)(2,1)S(1)}, bf16[4,128,128]{2,1,0:T(8,128)(2,1)S(1)}, u32[]{:S(2)}, u32[]{:S(2)}) %collective-permute-start.3) | collective-permute-done | bytes 131104 | tf_op jit(solution)/shard_map/features_4/ppermute | solution.py:78
  18.6 1.5 %collective-permute-start.7 = (bf16[512,128]{1,0:T(8,128)(2,1)S(1)}, bf16[512,128]{1,0:T(8,128)(2,1)S(1)}, u32[]{:S(2)}, u32[]{:S(2)}) collective-permute-start(bf16[512,128]{1,0:T(8,128)(2,1)S(1)} %copy-done.1), channel_id=1, source_target_pairs={{0,2},{1,3},{2,0},{3,1},{4,6},{5,7},{6,4},{7,5},{8,10},{9,11},{10,... | collective-permute-start | bytes 393224 | tf_op jit(solution)/shard_map/cotangent/ppermute | solution.py:78
  20.5 3.1 %shard_map.112.refs_4_ = f32[17,128,128]{2,1,0:T(8,128)S(1)} custom-call(s32[168]{0:T(256)S(1)} %get-tuple-element.45.refs_0_, bf16[80,128,128]{2,1,0:T(8,128)(2,1)S(1)} %get-tuple-element.46.refs_1_, bf16[4,128,128]{2,1,0:T(8,128)(2,1)S(1)} %bitcast.10, bf16[4,128,128]{2,1,0:T(8,128)(2,1)S(1)} %collective-permute-done.refs_3_, ...), custom_call_target="tpu_custom_call" | custom-call | flops 1 | bytes 1 | tf_op jit(solution)/shard_map/pallas_call | solution.py:289
  23.6 1.4 %shard_map.113 = (f32[4,128,128]{2,1,0:T(8,128)S(1)}, bf16[4,128,128]{2,1,0:T(8,128)(2,1)S(1)}, f32[4,128,128]{2,1,0:T(8,128)S(1)}, bf16[4,128,128]{2,1,0:T(8,128)(2,1)S(1)}) custom-call(s32[168]{0:T(256)S(1)} %get-tuple-element.45.refs_0_, bf16[80,128,128]{2,1,0:T(8,128)(2,1)S(1)} %get-tuple-element.46.refs_1_, ...), custom_call_target="tpu_custom_call" | custom-call | flops 1 | bytes 1 | tf_op jit(solution)/shard_map/pallas_call | solution.py:289
  25.6 0.8 %collective-permute-done.8 = bf16[4,128,128]{2,1,0:T(8,128)(2,1)S(1)} collective-permute-done((bf16[4,128,128]{2,1,0:T(8,128)(2,1)S(1)}, bf16[4,128,128]{2,1,0:T(8,128)(2,1)S(1)}, u32[]{:S(2)}, u32[]{:S(2)}) %collective-permute-start.8) | collective-permute-done | bytes 131104 | tf_op jit(solution)/shard_map/aggregate_1/ppermute | solution.py:78
  27.0 1.7 %collective-permute-start.10 = (bf16[4,128,128]{2,1,0:T(8,128)(2,1)S(1)}, bf16[4,128,128]{2,1,0:T(8,128)(2,1)S(1)}, u32[]{:S(2)}, u32[]{:S(2)}) collective-permute-start(bf16[4,128,128]{2,1,0:T(8,128)(2,1)S(1)} %add_convert_fusion.3.mine), channel_id=1, source_target_pairs={{0,2},{1,3},{2,0},{3,1},{4,6},{5,7},{6,4},{7,5},{8,10},{9,11},{10,... | collective-permute-start | bytes 393224 | tf_op jit(solution)/shard_map/swap/ppermute | solution.py:78
  28.7 4.2 %collective-permute-done.11.theirs = bf16[4,128,128]{2,1,0:T(8,128)(2,1)S(1)} collective-permute-done((bf16[4,128,128]{2,1,0:T(8,128)(2,1)S(1)}, bf16[4,128,128]{2,1,0:T(8,128)(2,1)S(1)}, u32[]{:S(2)}, u32[]{:S(2)}) %collective-permute-start.11) | collective-permute-done | bytes 131104 | tf_op jit(solution)/shard_map/swap/ppermute | solution.py:78
  33.5 1.4 %collective-permute-done.10.theirs = bf16[4,128,128]{2,1,0:T(8,128)(2,1)S(1)} collective-permute-done((bf16[4,128,128]{2,1,0:T(8,128)(2,1)S(1)}, bf16[4,128,128]{2,1,0:T(8,128)(2,1)S(1)}, u32[]{:S(2)}, u32[]{:S(2)}) %collective-permute-start.10) | collective-permute-done | bytes 131104 | tf_op jit(solution)/shard_map/swap/ppermute | solution.py:78
  35.5 0.6 collective-permute-start.12
  36.1 0.8 %collective-permute-done.13.refs_3_ = bf16[4,128,128]{2,1,0:T(8,128)(2,1)S(1)} collective-permute-done((bf16[4,128,128]{2,1,0:T(8,128)(2,1)S(1)}, bf16[4,128,128]{2,1,0:T(8,128)(2,1)S(1)}, u32[]{:S(2)}, u32[]{:S(2)}) %collective-permute-start.13) | collective-permute-done | bytes 131104 | tf_op jit(solution)/shard_map/rows_1/ppermute | solution.py:78
  36.8 1.2 %shard_map.116 = bf16[4,128,128]{2,1,0:T(8,128)(2,1)S(1)} custom-call(s32[168]{0:T(256)S(1)} %get-tuple-element.45.refs_0_, bf16[80,128,128]{2,1,0:T(8,128)(2,1)S(1)} %get-tuple-element.46.refs_1_, bf16[4,128,128]{2,1,0:T(8,128)(2,1)S(1)} %get-tuple-element.63.refs_2_, bf16[4,128,128]{2,1,0:T(8,128)(2,1)S(1)} %collective-permute-done.13.refs_3_, ...), custom_call_target="tpu_custom_call" | custom-call | flops 1 | bytes 1 | tf_op jit(solution)/shard_map/pallas_call | solution.py:289
  38.2 1.1 %collective-permute-start.15 = (bf16[144,128]{1,0:T(8,128)(2,1)S(1)}, bf16[144,128]{1,0:T(8,128)(2,1)S(1)}, u32[]{:S(2)}, u32[]{:S(2)}) collective-permute-start(bf16[144,128]{1,0:T(8,128)(2,1)S(1)} %add_convert_fusion.7), channel_id=1, source_target_pairs={{0,8},{4,12},{8,0},{12,4},{16,24},{20,28},{24,16},{28,20},{1,9},{5... | collective-permute-start | bytes 110600 | tf_op jit(solution)/shard_map/gradients_2/ppermute | solution.py:78
  39.2 3.1 %shard_map.117 = (f32[4,128,128]{2,1,0:T(8,128)S(1)}, bf16[4,128,128]{2,1,0:T(8,128)(2,1)S(1)}, bf16[4,128,128]{2,1,0:T(8,128)(2,1)S(1)}, bf16[4,128,128]{2,1,0:...) custom-call(s32[168]{0:T(256)S(1)} %get-tuple-element.45.refs_0_, ...), custom_call_target="tpu_custom_call" | custom-call | flops 1 | bytes 1 | tf_op jit(solution)/shard_map/pallas_call | solution.py:289
  42.5 1.2 %collective-permute-done.16 = bf16[4,128,128]{2,1,0:T(8,128)(2,1)S(1)} collective-permute-done((bf16[4,128,128]{2,1,0:T(8,128)(2,1)S(1)}, bf16[4,128,128]{2,1,0:T(8,128)(2,1)S(1)}, u32[]{:S(2)}, u32[]{:S(2)}) %collective-permute-start.16) | collective-permute-done | bytes 131104 | tf_op jit(solution)/shard_map/sums_5/ppermute | solution.py:78
  43.7 0.6 %collective-permute-start.20 = (bf16[4,128,128]{2,1,0:T(8,128)(2,1)S(1)}, bf16[4,128,128]{2,1,0:T(8,128)(2,1)S(1)}, u32[]{:S(2)}, u32[]{:S(2)}) collective-permute-start(bf16[4,128,128]{2,1,0:T(8,128)(2,1)S(1)} %add_convert_fusion.2), channel_id=1, source_target_pairs={{0,8},{4,12},{8,0},{12,4},{16,24},{20,28},{24,16},{28,20},{1,9},{5... | collective-permute-start | bytes 393224 | tf_op jit(solution)/shard_map/sums_4/ppermute | solution.py:78
  44.6 1.8 %collective-permute-start.22 = (bf16[4,128,128]{2,1,0:T(8,128)(2,1)S(1)}, bf16[4,128,128]{2,1,0:T(8,128)(2,1)S(1)}, u32[]{:S(2)}, u32[]{:S(2)}) collective-permute-start(bf16[4,128,128]{2,1,0:T(8,128)(2,1)S(1)} %get-tuple-element.73), channel_id=1, source_target_pairs={{0,4},{4,0},{8,12},{12,8},{16,20},{20,16},{24,28},{28,24},{1,5},{5... | collective-permute-start | bytes 393224 | tf_op jit(solution)/shard_map/sums_1/ppermute | solution.py:78
  46.4 0.8 %collective-permute-start.17 = (bf16[144,128]{1,0:T(8,128)(2,1)S(1)}, bf16[144,128]{1,0:T(8,128)(2,1)S(1)}, u32[]{:S(2)}, u32[]{:S(2)}) collective-permute-start(bf16[144,128]{1,0:T(8,128)(2,1)S(1)} %add_convert_fusion.6), channel_id=1, source_target_pairs={{0,24},{4,28},{8,16},{12,20},{16,8},{20,12},{24,0},{28,4},{1,25},{... | collective-permute-start | bytes 110600 | tf_op jit(solution)/shard_map/gradients_6/ppermute | solution.py:78
  47.1 1.3 %collective-permute-done.19 = bf16[4,128,128]{2,1,0:T(8,128)(2,1)S(1)} collective-permute-done((bf16[4,128,128]{2,1,0:T(8,128)(2,1)S(1)}, bf16[4,128,128]{2,1,0:T(8,128)(2,1)S(1)}, u32[]{:S(2)}, u32[]{:S(2)}) %collective-permute-start.19) | collective-permute-done | bytes 131104 | tf_op jit(solution)/shard_map/sums_7/ppermute | solution.py:78
  48.8 1.6 %collective-permute-start.23 = (bf16[4,128,128]{2,1,0:T(8,128)(2,1)S(1)}, bf16[4,128,128]{2,1,0:T(8,128)(2,1)S(1)}, u32[]{:S(2)}, u32[]{:S(2)}) collective-permute-start(bf16[4,128,128]{2,1,0:T(8,128)(2,1)S(1)} %add_convert_fusion), channel_id=1, source_target_pairs={{0,24},{4,28},{8,16},{12,20},{16,8},{20,12},{24,0},{28,4},{1,25},{... | collective-permute-start | bytes 393224 | tf_op jit(solution)/shard_map/sums_6/ppermute | solution.py:78
  50.4 0.9 %collective-permute-done.18 = bf16[4,128,128]{2,1,0:T(8,128)(2,1)S(1)} collective-permute-done((bf16[4,128,128]{2,1,0:T(8,128)(2,1)S(1)}, bf16[4,128,128]{2,1,0:T(8,128)(2,1)S(1)}, u32[]{:S(2)}, u32[]{:S(2)}) %collective-permute-start.18) | collective-permute-done | bytes 131104 | tf_op jit(solution)/shard_map/sums_3/ppermute | solution.py:78
  51.3 1.0 %collective-permute-start.24 = (bf16[4,128,128]{2,1,0:T(8,128)(2,1)S(1)}, bf16[4,128,128]{2,1,0:T(8,128)(2,1)S(1)}, u32[]{:S(2)}, u32[]{:S(2)}) collective-permute-start(bf16[4,128,128]{2,1,0:T(8,128)(2,1)S(1)} %add_convert_fusion.1), channel_id=1, source_target_pairs={{0,8},{4,12},{8,0},{12,4},{16,24},{20,28},{24,16},{28,20},{1,9},{5... | collective-permute-start | bytes 393224 | tf_op jit(solution)/shard_map/sums_2/ppermute | solution.py:78
  52.8 0.8 %collective-permute-start.21 = (bf16[144,128]{1,0:T(8,128)(2,1)S(1)}, bf16[144,128]{1,0:T(8,128)(2,1)S(1)}, u32[]{:S(2)}, u32[]{:S(2)}) collective-permute-start(bf16[144,128]{1,0:T(8,128)(2,1)S(1)} %add_convert_fusion.5.refs_0_), channel_id=1, source_target_pairs={{0,4},{4,0},{8,12},{12,8},{16,20},{20,16},{24,28},{28,24},{1,5},{5... | collective-permute-start | bytes 110600 | tf_op jit(solution)/shard_map/gradients_1/ppermute | solution.py:78
  53.6 0.7 %copy.12 = bf16[512,128]{1,0:T(8,128)(2,1)} copy(bf16[512,128]{1,0:T(8,128)(2,1)S(1)} %get-tuple-element.86) | data formatting | bytes 262144
  54.3 2.6 %collective-permute-done.21.refs_1_ = bf16[144,128]{1,0:T(8,128)(2,1)S(1)} collective-permute-done((bf16[144,128]{1,0:T(8,128)(2,1)S(1)}, bf16[144,128]{1,0:T(8,128)(2,1)S(1)}, u32[]{:S(2)}, u32[]{:S(2)}) %collective-permute-start.21) | collective-permute-done | bytes 36896 | tf_op jit(solution)/shard_map/gradients_1/ppermute | solution.py:78
  56.8 1.0 %collective-permute-done.24.refs_5_ = bf16[4,128,128]{2,1,0:T(8,128)(2,1)S(1)} collective-permute-done((bf16[4,128,128]{2,1,0:T(8,128)(2,1)S(1)}, bf16[4,128,128]{2,1,0:T(8,128)(2,1)S(1)}, u32[]{:S(2)}, u32[]{:S(2)}) %collective-permute-start.24) | collective-permute-done | bytes 131104 | tf_op jit(solution)/shard_map/sums_2/ppermute | solution.py:78
  57.8 0.9 %shard_map.118 = (f32[512,128]{1,0:T(8,128)}, f32[128,128]{1,0:T(8,128)}, f32[1,128]{1,0:T(1,128)}) custom-call(bf16[144,128]{1,0:T(8,128)(2,1)S(1)} %add_convert_fusion.5.refs_0_, bf16[144,128]{1,0:T(8,128)(2,1)S(1)} %collective-permute-done.21.refs_1_, f32[4,128,128]{2,1,0:T(8,128)S(1)} %get-tuple-element.82.refs_2_, ...), custom_call_target="tpu_custom_call" | custom-call | flops 1 | bytes 1 | tf_op jit(solution)/shard_map/pallas_call | solution.py:376
  (45 shorter events, 5.5 us)
Async XLA Ops:
  0.6 11.4 %copy-start = (bf16[512,128]{1,0:T(8,128)(2,1)S(1)}, bf16[512,128]{1,0:T(8,128)(2,1)}, u32[]{:S(2)}) copy-start(bf16[512,128]{1,0:T(8,128)(2,1)} %param.8) | copy-start | bytes 393220
  0.6 18.0 %copy-start.1 = (bf16[512,128]{1,0:T(8,128)(2,1)S(1)}, bf16[512,128]{1,0:T(8,128)(2,1)}, u32[]{:S(2)}) copy-start(bf16[512,128]{1,0:T(8,128)(2,1)} %cotangent.1) | copy-start | bytes 393220
  0.7 10.9 %collective-permute-start.1 = (bf16[4,128,128]{2,1,0:T(8,128)(2,1)}, bf16[4,128,128]{2,1,0:T(8,128)(2,1)S(1)}, u32[]{:S(2)}, u32[]{:S(2)}) collective-permute-start(bf16[4,128,128]{2,1,0:T(8,128)(2,1)} %bitcast.7), channel_id=1, source_target_pairs={{0,24},{4,28},{8,16},{12,20},{16,8},{20,12},{24,0},{28,4},{1,25},{... | collective-permute-start | bytes 393224 | tf_op jit(solution)/shard_map/features_6/ppermute | solution.py:78
  5.8 7.9 %collective-permute-start = (bf16[4,128,128]{2,1,0:T(8,128)(2,1)}, bf16[4,128,128]{2,1,0:T(8,128)(2,1)S(1)}, u32[]{:S(2)}, u32[]{:S(2)}) collective-permute-start(bf16[4,128,128]{2,1,0:T(8,128)(2,1)} %bitcast.8), channel_id=1, source_target_pairs={{0,4},{4,0},{8,12},{12,8},{16,20},{20,16},{24,28},{28,24},{1,5},{5... | collective-permute-start | bytes 393224 | tf_op jit(solution)/shard_map/features_1/ppermute | solution.py:78
  11.6 6.5 %collective-permute-start.3 = (bf16[4,128,128]{2,1,0:T(8,128)(2,1)S(1)}, bf16[4,128,128]{2,1,0:T(8,128)(2,1)S(1)}, u32[]{:S(2)}, u32[]{:S(2)}) collective-permute-start(bf16[4,128,128]{2,1,0:T(8,128)(2,1)S(1)} %collective-permute-done.1.refs_6_), channel_id=1, source_target_pairs={{0,8},{4,12},{8,0},{12,4},{16,24},{20,28},{24,16},{28,20},{1,9},{5... | collective-permute-start | bytes 393224 | tf_op jit(solution)/shard_map/features_4/ppermute | solution.py:78
  12.0 8.5 %collective-permute-start.5 = (bf16[4,128,128]{2,1,0:T(8,128)(2,1)S(1)}, bf16[4,128,128]{2,1,0:T(8,128)(2,1)S(1)}, u32[]{:S(2)}, u32[]{:S(2)}) collective-permute-start(bf16[4,128,128]{2,1,0:T(8,128)(2,1)S(1)} %bitcast.9), channel_id=1, source_target_pairs={{0,8},{4,12},{8,0},{12,4},{16,24},{20,28},{24,16},{28,20},{1,9},{5... | collective-permute-start | bytes 393224 | tf_op jit(solution)/shard_map/features_2/ppermute | solution.py:78
  13.7 10.0 %collective-permute-start.2 = (bf16[4,128,128]{2,1,0:T(8,128)(2,1)S(1)}, bf16[4,128,128]{2,1,0:T(8,128)(2,1)S(1)}, u32[]{:S(2)}, u32[]{:S(2)}) collective-permute-start(bf16[4,128,128]{2,1,0:T(8,128)(2,1)S(1)} %collective-permute-done.refs_3_), channel_id=1, source_target_pairs={{0,8},{4,12},{8,0},{12,4},{16,24},{20,28},{24,16},{28,20},{1,9},{5... | collective-permute-start | bytes 393224 | tf_op jit(solution)/shard_map/features_3/ppermute | solution.py:78
  14.0 6.5 %collective-permute-start.6 = (bf16[4,128,128]{2,1,0:T(8,128)(2,1)S(1)}, bf16[4,128,128]{2,1,0:T(8,128)(2,1)S(1)}, u32[]{:S(2)}, u32[]{:S(2)}) collective-permute-start(bf16[4,128,128]{2,1,0:T(8,128)(2,1)S(1)} %collective-permute-done.1.refs_6_), channel_id=1, source_target_pairs={{0,4},{4,0},{8,12},{12,8},{16,20},{20,16},{24,28},{28,24},{1,5},{5... | collective-permute-start | bytes 393224 | tf_op jit(solution)/shard_map/features_7/ppermute | solution.py:78
  18.1 5.6 %collective-permute-start.4 = (bf16[4,128,128]{2,1,0:T(8,128)(2,1)S(1)}, bf16[4,128,128]{2,1,0:T(8,128)(2,1)S(1)}, u32[]{:S(2)}, u32[]{:S(2)}) collective-permute-start(bf16[4,128,128]{2,1,0:T(8,128)(2,1)S(1)} %collective-permute-done.3.refs_5_), channel_id=1, source_target_pairs={{0,4},{4,0},{8,12},{12,8},{16,20},{20,16},{24,28},{28,24},{1,5},{5... | collective-permute-start | bytes 393224 | tf_op jit(solution)/shard_map/features_5/ppermute | solution.py:78
  18.6 6.5 %collective-permute-start.7 = (bf16[512,128]{1,0:T(8,128)(2,1)S(1)}, bf16[512,128]{1,0:T(8,128)(2,1)S(1)}, u32[]{:S(2)}, u32[]{:S(2)}) collective-permute-start(bf16[512,128]{1,0:T(8,128)(2,1)S(1)} %copy-done.1), channel_id=1, source_target_pairs={{0,2},{1,3},{2,0},{3,1},{4,6},{5,7},{6,4},{7,5},{8,10},{9,11},{10,... | collective-permute-start | bytes 393224 | tf_op jit(solution)/shard_map/cotangent/ppermute | solution.py:78
  23.6 9.3 %copy-start.2 = (bf16[128,128]{1,0:T(8,128)(2,1)S(1)}, bf16[128,128]{1,0:T(8,128)(2,1)}, u32[]{:S(2)}) copy-start(bf16[128,128]{1,0:T(8,128)(2,1)} %weight.3) | copy-start | bytes 98308
  23.6 9.3 %copy-start.3 = (f32[128]{0:T(128)S(1)}, f32[128]{0:T(128)}, u32[]{:S(2)}) copy-start(f32[128]{0:T(128)} %param.10) | copy-start | bytes 1540
  25.0 1.4 %collective-permute-start.8 = (bf16[4,128,128]{2,1,0:T(8,128)(2,1)S(1)}, bf16[4,128,128]{2,1,0:T(8,128)(2,1)S(1)}, u32[]{:S(2)}, u32[]{:S(2)}) collective-permute-start(bf16[4,128,128]{2,1,0:T(8,128)(2,1)S(1)} %get-tuple-element.57), channel_id=1, source_target_pairs={{0,1},{1,0},{2,3},{3,2},{4,5},{5,4},{6,7},{7,6},{8,9},{9,8},{10,11... | collective-permute-start | bytes 393224 | tf_op jit(solution)/shard_map/aggregate_1/ppermute | solution.py:78
  25.1 1.9 %collective-permute-start.9 = (bf16[4,128,128]{2,1,0:T(8,128)(2,1)S(1)}, bf16[4,128,128]{2,1,0:T(8,128)(2,1)S(1)}, u32[]{:S(2)}, u32[]{:S(2)}) collective-permute-start(bf16[4,128,128]{2,1,0:T(8,128)(2,1)S(1)} %get-tuple-element.59), channel_id=1, source_target_pairs={{0,1},{1,0},{2,3},{3,2},{4,5},{5,4},{6,7},{7,6},{8,9},{9,8},{10,11... | collective-permute-start | bytes 393224 | tf_op jit(solution)/shard_map/aggregate_3/ppermute | solution.py:78
  26.5 6.4 %collective-permute-start.11 = (bf16[4,128,128]{2,1,0:T(8,128)(2,1)S(1)}, bf16[4,128,128]{2,1,0:T(8,128)(2,1)S(1)}, u32[]{:S(2)}, u32[]{:S(2)}) collective-permute-start(bf16[4,128,128]{2,1,0:T(8,128)(2,1)S(1)} %add_convert_fusion.4.mine), channel_id=1, source_target_pairs={{0,2},{1,3},{2,0},{3,1},{4,6},{5,7},{6,4},{7,5},{8,10},{9,11},{10,... | collective-permute-start | bytes 393224 | tf_op jit(solution)/shard_map/swap/ppermute | solution.py:78
  27.0 7.9 %collective-permute-start.10 = (bf16[4,128,128]{2,1,0:T(8,128)(2,1)S(1)}, bf16[4,128,128]{2,1,0:T(8,128)(2,1)S(1)}, u32[]{:S(2)}, u32[]{:S(2)}) collective-permute-start(bf16[4,128,128]{2,1,0:T(8,128)(2,1)S(1)} %add_convert_fusion.3.mine), channel_id=1, source_target_pairs={{0,2},{1,3},{2,0},{3,1},{4,6},{5,7},{6,4},{7,5},{8,10},{9,11},{10,... | collective-permute-start | bytes 393224 | tf_op jit(solution)/shard_map/swap/ppermute | solution.py:78
  33.4 2.7 %collective-permute-start.14 = (bf16[4,128,128]{2,1,0:T(8,128)(2,1)S(1)}, bf16[4,128,128]{2,1,0:T(8,128)(2,1)S(1)}, u32[]{:S(2)}, u32[]{:S(2)}) collective-permute-start(bf16[4,128,128]{2,1,0:T(8,128)(2,1)S(1)} %get-tuple-element.64.refs_4_), channel_id=1, source_target_pairs={{0,1},{1,0},{2,3},{3,2},{4,5},{5,4},{6,7},{7,6},{8,9},{9,8},{10,11... | collective-permute-start | bytes 393224 | tf_op jit(solution)/shard_map/rows_3/ppermute | solution.py:78
  35.4 1.4 %collective-permute-start.13 = (bf16[4,128,128]{2,1,0:T(8,128)(2,1)S(1)}, bf16[4,128,128]{2,1,0:T(8,128)(2,1)S(1)}, u32[]{:S(2)}, u32[]{:S(2)}) collective-permute-start(bf16[4,128,128]{2,1,0:T(8,128)(2,1)S(1)} %get-tuple-element.63.refs_2_), channel_id=1, source_target_pairs={{0,1},{1,0},{2,3},{3,2},{4,5},{5,4},{6,7},{7,6},{8,9},{9,8},{10,11... | collective-permute-start | bytes 393224 | tf_op jit(solution)/shard_map/rows_1/ppermute | solution.py:78
  35.5 2.6 %collective-permute-start.12 = (f32[144,128]{1,0:T(8,128)S(1)}, f32[144,128]{1,0:T(8,128)S(1)}, u32[]{:S(2)}, u32[]{:S(2)}) collective-permute-start(f32[144,128]{1,0:T(8,128)S(1)} %add.32), channel_id=1, source_target_pairs={{0,1},{1,0},{2,3},{3,2},{4,5},{5,4},{6,7},{7,6},{8,9},{9,8},{10,11... | collective-permute-start | bytes 221192 | tf_op jit(solution)/shard_map/swap/ppermute | solution.py:78
  38.1 5.6 %collective-permute-start.16 = (bf16[4,128,128]{2,1,0:T(8,128)(2,1)S(1)}, bf16[4,128,128]{2,1,0:T(8,128)(2,1)S(1)}, u32[]{:S(2)}, u32[]{:S(2)}) collective-permute-start(bf16[4,128,128]{2,1,0:T(8,128)(2,1)S(1)} %shard_map.116), channel_id=1, source_target_pairs={{0,4},{4,0},{8,12},{12,8},{16,20},{20,16},{24,28},{28,24},{1,5},{5... | collective-permute-start | bytes 393224 | tf_op jit(solution)/shard_map/sums_5/ppermute | solution.py:78
  38.2 8.2 %collective-permute-start.15 = (bf16[144,128]{1,0:T(8,128)(2,1)S(1)}, bf16[144,128]{1,0:T(8,128)(2,1)S(1)}, u32[]{:S(2)}, u32[]{:S(2)}) collective-permute-start(bf16[144,128]{1,0:T(8,128)(2,1)S(1)} %add_convert_fusion.7), channel_id=1, source_target_pairs={{0,8},{4,12},{8,0},{12,4},{16,24},{20,28},{24,16},{28,20},{1,9},{5... | collective-permute-start | bytes 110600 | tf_op jit(solution)/shard_map/gradients_2/ppermute | solution.py:78
  42.3 6.2 %collective-permute-start.19 = (bf16[4,128,128]{2,1,0:T(8,128)(2,1)S(1)}, bf16[4,128,128]{2,1,0:T(8,128)(2,1)S(1)}, u32[]{:S(2)}, u32[]{:S(2)}) collective-permute-start(bf16[4,128,128]{2,1,0:T(8,128)(2,1)S(1)} %get-tuple-element.70), channel_id=1, source_target_pairs={{0,4},{4,0},{8,12},{12,8},{16,20},{20,16},{24,28},{28,24},{1,5},{5... | collective-permute-start | bytes 393224 | tf_op jit(solution)/shard_map/sums_7/ppermute | solution.py:78
  43.7 5.0 %collective-permute-start.20 = (bf16[4,128,128]{2,1,0:T(8,128)(2,1)S(1)}, bf16[4,128,128]{2,1,0:T(8,128)(2,1)S(1)}, u32[]{:S(2)}, u32[]{:S(2)}) collective-permute-start(bf16[4,128,128]{2,1,0:T(8,128)(2,1)S(1)} %add_convert_fusion.2), channel_id=1, source_target_pairs={{0,8},{4,12},{8,0},{12,4},{16,24},{20,28},{24,16},{28,20},{1,9},{5... | collective-permute-start | bytes 393224 | tf_op jit(solution)/shard_map/sums_4/ppermute | solution.py:78
  44.3 7.0 %collective-permute-start.18 = (bf16[4,128,128]{2,1,0:T(8,128)(2,1)S(1)}, bf16[4,128,128]{2,1,0:T(8,128)(2,1)S(1)}, u32[]{:S(2)}, u32[]{:S(2)}) collective-permute-start(bf16[4,128,128]{2,1,0:T(8,128)(2,1)S(1)} %get-tuple-element.72), channel_id=1, source_target_pairs={{0,4},{4,0},{8,12},{12,8},{16,20},{20,16},{24,28},{28,24},{1,5},{5... | collective-permute-start | bytes 393224 | tf_op jit(solution)/shard_map/sums_3/ppermute | solution.py:78
  44.6 9.7 %collective-permute-start.22 = (bf16[4,128,128]{2,1,0:T(8,128)(2,1)S(1)}, bf16[4,128,128]{2,1,0:T(8,128)(2,1)S(1)}, u32[]{:S(2)}, u32[]{:S(2)}) collective-permute-start(bf16[4,128,128]{2,1,0:T(8,128)(2,1)S(1)} %get-tuple-element.73), channel_id=1, source_target_pairs={{0,4},{4,0},{8,12},{12,8},{16,20},{20,16},{24,28},{28,24},{1,5},{5... | collective-permute-start | bytes 393224 | tf_op jit(solution)/shard_map/sums_1/ppermute | solution.py:78
  46.4 6.4 %collective-permute-start.17 = (bf16[144,128]{1,0:T(8,128)(2,1)S(1)}, bf16[144,128]{1,0:T(8,128)(2,1)S(1)}, u32[]{:S(2)}, u32[]{:S(2)}) collective-permute-start(bf16[144,128]{1,0:T(8,128)(2,1)S(1)} %add_convert_fusion.6), channel_id=1, source_target_pairs={{0,24},{4,28},{8,16},{12,20},{16,8},{20,12},{24,0},{28,4},{1,25},{... | collective-permute-start | bytes 110600 | tf_op jit(solution)/shard_map/gradients_6/ppermute | solution.py:78
  48.8 9.0 %collective-permute-start.23 = (bf16[4,128,128]{2,1,0:T(8,128)(2,1)S(1)}, bf16[4,128,128]{2,1,0:T(8,128)(2,1)S(1)}, u32[]{:S(2)}, u32[]{:S(2)}) collective-permute-start(bf16[4,128,128]{2,1,0:T(8,128)(2,1)S(1)} %add_convert_fusion), channel_id=1, source_target_pairs={{0,24},{4,28},{8,16},{12,20},{16,8},{20,12},{24,0},{28,4},{1,25},{... | collective-permute-start | bytes 393224 | tf_op jit(solution)/shard_map/sums_6/ppermute | solution.py:78
  51.3 6.5 %collective-permute-start.24 = (bf16[4,128,128]{2,1,0:T(8,128)(2,1)S(1)}, bf16[4,128,128]{2,1,0:T(8,128)(2,1)S(1)}, u32[]{:S(2)}, u32[]{:S(2)}) collective-permute-start(bf16[4,128,128]{2,1,0:T(8,128)(2,1)S(1)} %add_convert_fusion.1), channel_id=1, source_target_pairs={{0,8},{4,12},{8,0},{12,4},{16,24},{20,28},{24,16},{28,20},{1,9},{5... | collective-permute-start | bytes 393224 | tf_op jit(solution)/shard_map/sums_2/ppermute | solution.py:78
  52.8 4.0 %collective-permute-start.21 = (bf16[144,128]{1,0:T(8,128)(2,1)S(1)}, bf16[144,128]{1,0:T(8,128)(2,1)S(1)}, u32[]{:S(2)}, u32[]{:S(2)}) collective-permute-start(bf16[144,128]{1,0:T(8,128)(2,1)S(1)} %add_convert_fusion.5.refs_0_), channel_id=1, source_target_pairs={{0,4},{4,0},{8,12},{12,8},{16,20},{20,16},{24,28},{28,24},{1,5},{5... | collective-permute-start | bytes 110600 | tf_op jit(solution)/shard_map/gradients_1/ppermute | solution.py:78

commit v5 on v4

--- a/solution.py
+++ b/solution.py
@@ -1,5 +1,7 @@
 from functools import partial
+import functools
 import math
+import operator
 
 import jax
 import jax.numpy as jnp
@@ -36,25 +38,16 @@
     return steps
 
 
-def tree(outer, inner, shortcut):
-    assert outer & (outer - 1) == 0 and inner & (inner - 1) == 0
-    outer_masks, inner_masks = mirror_masks(outer), mirror_masks(inner)
+def tree(outer, inner):
     found = []
     for o in range(outer):
-        o_steps = steps_to(o, outer_masks)
         for i in range(inner):
-            i_steps = steps_to(i, inner_masks)
-            if o == 0 and i == 0:
-                continue
-            short = bool(i) and shortcut and o == 1
-            if i and not short:
-                parent = (o, i ^ i_steps[-1])
-            else:
-                parent = (o ^ o_steps[-1], i)
-            depth = len(o_steps) + len(i_steps)
-            found.append((depth, short, -o, i, parent))
-    found.sort()
-    return [(-o * inner + i, parent[0] * inner + parent[1]) for _, _, o, i, parent in found]
+            o_steps, i_steps = steps_to(o, mirror_masks(outer)), steps_to(i, mirror_masks(inner))
+            if i:
+                found.append((len(o_steps) + len(i_steps), o * inner + i, o * inner + (i ^ i_steps[-1])))
+            elif o:
+                found.append((len(o_steps), o * inner, (o ^ o_steps[-1]) * inner))
+    return [(offset, parent) for _, offset, parent in sorted(found)]
 
 
 def inner_of(size):
@@ -64,12 +57,14 @@
     return inner
 
 
-def depth_of(offset, routes):
-    parents = dict(routes)
-    depth = 0
-    while offset:
-        offset, depth = parents[offset], depth + 1
-    return depth
+def offset_of(code, steps):
+    chosen = [masks for n, masks in enumerate(steps) if code >> n & 1]
+    return tuple(functools.reduce(operator.xor, masks) for masks in zip(*chosen, strict=True)) or (0, 0)
+
+
+def last_step(code):
+    step = code.bit_length() - 1
+    return code ^ 1 << step, step
 
 
 def swap(x, axis, mask, name="swap"):
@@ -78,6 +73,13 @@
         return lax.ppermute(x, axis, [(i, i ^ mask) for i in range(size)])
 
 
+def row_swap(x, masks, name="swap"):
+    rows, cols = lax.axis_size("row"), lax.axis_size("col")
+    pairs = [(i * cols + j, (i ^ masks[j % 2]) * cols + j) for i in range(rows) for j in range(cols)]
+    with jax.named_scope(name):
+        return lax.ppermute(x, ("row", "col"), pairs)
+
+
 def after(x, *others):
     return lax.optimization_barrier((x,) + others)[0]
 
@@ -86,11 +88,11 @@
     def __init__(self):
         self.last = None
 
-    def swap(self, x, axis, mask, name):
+    def tie(self, x):
         if self.last is not None:
             x = after(x, self.last)
         self.last = x
-        return swap(x, axis, mask, name)
+        return x
 
 
 def spread(pieces, axis, routes):
@@ -122,9 +124,18 @@
     return 1
 
 
+def core_at():
+    return lax.rem(lax.axis_index("col"), 2)
+
+
+def by_core(pair):
+    return pair[0] if pair[0] == pair[1] else jnp.where(core_at() == 0, pair[0], pair[1])
+
+
 def member(offset, chosen):
-    mask = np.uint32(sum(1 << d for d in chosen)).astype(np.int32)
-    return lax.bitwise_and(lax.shift_right_logical(jnp.int32(mask), offset), 1)
+    masks = [np.uint32(sum(1 << pair[core] for pair in chosen)).astype(np.int32) for core in (0, 1)]
+    mask = jnp.where(core_at() == 0, jnp.int32(masks[0]), jnp.int32(masks[1]))
+    return lax.bitwise_and(lax.shift_right_logical(mask, offset), 1)
 
 
 FORWARD_EARLY, FORWARD_LATE, BACK_FIRST, BACK_LAST = range(4)
@@ -137,7 +148,7 @@
 
 
 def parts_of(slots):
-    return 8 if slots % 8 == 0 else 1
+    return 2 if slots % 2 == 0 else 1
 
 
 def prep_kernel(per, bits, late, first, indices, blocks, table, held, sem):
@@ -208,7 +219,7 @@
     copies = [pltpu.make_async_copy(in_table, table, sem.at[len(offsets)])]
     copies[0].start()
     for n, offset in enumerate(offsets):
-        at = lax.bitwise_xor(here, offset) * per
+        at = lax.bitwise_xor(here, by_core(offset)) * per
         copies.append(
             pltpu.make_async_copy(pieces[n], source.at[pl.ds(at, per)], sem.at[n])
         )
@@ -217,7 +228,7 @@
     if sums is not None:
         out_per = outs[0].shape[0]
         places = [
-            pl.ds(lax.bitwise_xor(there, d) * out_per, out_per) for d in sums
+            pl.ds(lax.bitwise_xor(there, by_core(d)) * out_per, out_per) for d in sums
         ]
     if starts:
         for place in places:
@@ -231,7 +242,7 @@
     for copy in copies:
         copy.wait()
     length = table[2 * slots + which]
-    idle = lax.bitwise_xor(here, offsets[0]) * per
+    idle = lax.bitwise_xor(here, by_core(offsets[0])) * per
 
     def step(i, carry):
         products, targets = [], []
@@ -391,41 +402,38 @@
     per = own_rows // BS
     row_blocks, column_blocks = per * col_devices, per * row_devices
     inner = inner_of(row_devices)
-    on_row = tree(row_devices // inner, inner, True)
-    off_row = tree(row_devices // inner, inner, False)
-    on_col = tree(col_devices // 2, 2, False)
+    on_col = tree(col_devices // 2, 2)
     across = col_devices - 2
     on_col = [route for route in on_col if route[0] != across]
 
-    depths = {d: depth_of(d, on_row) for d, _ in on_row}
-    short = [d for d, p in on_row if p and p < inner and d >= inner]
-    chain = [max(depths, key=lambda d: (depths[d], d not in short))]
-    while chain[-1]:
-        chain.append(dict(on_row)[chain[-1]])
-    first = [d for d in depths if depths[d] == max(depths.values())]
-    late_columns = [d for d, p in on_row if depths[d] == max(depths.values()) or d in short]
-
+    outer_steps = [inner * mask for mask in mirror_masks(row_devices // inner)]
+    inner_steps = mirror_masks(inner)
+    there = list(zip(outer_steps + inner_steps, outer_steps[:-1] + inner_steps + outer_steps[-1:]))
+    back_steps = [(mask, mask) for mask in outer_steps + inner_steps]
+    count = len(there)
+    assert 1 << count == row_devices
+    codes = sorted(range(1, row_devices), key=lambda code: (code.bit_count(), code))
+    late_codes = codes[-(row_devices // 4) :]
+    first_codes = codes[-1:]
+    late_columns = [offset_of(code, there) for code in late_codes]
+    first = [offset_of(code, back_steps) for code in first_codes]
     bits = widths(blocks.shape[0], row_blocks, column_blocks)
-    indices = jnp.concatenate([block_rows[:, 0], block_cols[:, 0], tile_slot_count[0]])
+    indices = jnp.concatenate([block_rows, block_cols, tile_slot_count], axis=0)[:, 0]
     table, held = prep(indices, blocks, per, bits, late_columns, first)
     pieces = {0: features.reshape(per, BS, channels)}
     queue = Queue()
-    for offset, parent in sorted(
-        on_row,
-        key=lambda r: (
-            depths[r[0]], r[0] not in chain, (r[0] ^ r[1]) < inner
-        ),
-    ):
-        pieces[offset] = queue.swap(pieces[parent], "row", offset ^ parent, f"features_{offset}")
-        if offset == chain[-2]:
-            pieces[offset] = after(pieces[offset], table)
-    other_cotangent = queue.swap(cotangent, "col", across, "cotangent")
-    early = {d: p for d, p in pieces.items() if d not in late_columns}
-    late = {d: p for d, p in pieces.items() if d in late_columns}
+    for code in codes:
+        parent, step = last_step(code)
+        pieces[code] = row_swap(queue.tie(pieces[parent]), there[step], f"features_{code}")
+        if code == 1:
+            pieces[code] = after(pieces[code], table)
+    other_cotangent = swap(queue.tie(cotangent), "col", across, "cotangent")
+    early = {offset_of(c, there): p for c, p in pieces.items() if c not in late_codes}
+    late = {offset_of(c, there): p for c, p in pieces.items() if c in late_codes}
     total = sparse(FORWARD_EARLY, bits, table, held, early, "row", "col", column_blocks, row_blocks)
     sums = sparse(
         FORWARD_LATE, bits, table, held, late, "row", "col", column_blocks, row_blocks, total,
-        {d: jnp.float32 if d in (0, across) else jnp.bfloat16 for d in range(col_devices)}, per,
+        {(d, d): jnp.float32 if d in (0, across) else jnp.bfloat16 for d in range(col_devices)}, per,
     )
 
     terms = collect(dict(enumerate(sums)), "col", on_col)
@@ -445,39 +453,39 @@
         grads = grads + swap(grads, "col", 2 * mask)
 
     rows = spread({0: back, across: other_back}, "col", on_col)
-    types = {d: jnp.bfloat16 if d else jnp.float32 for d in range(row_devices)}
-    rest = [d for d in range(row_devices) if d not in first]
+    types = {code: jnp.bfloat16 if code else jnp.float32 for code in range(row_devices)}
+    rest = [code for code in range(row_devices) if code not in first_codes]
+    rows = {(d, d): p for d, p in rows.items()}
     leave_first, leave_last = [
         sparse(
             which, bits, table, held, rows, "col", "row", row_blocks, column_blocks,
-            None, {d: types[d] for d in chosen}, per,
+            None, {offset_of(c, back_steps): types[c] for c in chosen}, per,
         )
-        for which, chosen in ((BACK_FIRST, first), (BACK_LAST, rest))
+        for which, chosen in ((BACK_FIRST, first_codes), (BACK_LAST, rest))
     ]
-    sums = dict(zip(first, leave_first)) | dict(zip(rest, leave_last))
-
-    terms = {d: [p] for d, p in sums.items()}
+    sums = dict(zip(first_codes, leave_first)) | dict(zip(rest, leave_last))
+    whole_way = [(1 << n) - 1 for n in range(1, count + 1)]
+    outer_codes = (1 << len(outer_steps)) - 1
+    stages = {code: code.bit_count() + (code & outer_codes == 0) for code in codes}
+    order = sorted(
+        codes, key=lambda code: (-stages[code], code != 1 + (1 << count - 1), code not in whole_way, -code)
+    )
+    grad_steps = list(range(count - 2, -1, -1)) + [count - 1]
+    terms = {code: [p] for code, p in sums.items()}
     queue = Queue()
-    top = chain[-2]
-    stages = {d: depth_of(d, off_row) + (d < inner) for d, _ in off_row}
-    order = sorted(
-        off_row, key=lambda r: (-stages[r[0]], r[0] != top ^ 1, r[0] not in chain, -r[0])
-    )
-    masks = [d ^ parent for d, parent in zip(chain, chain[1:])]
-    masks = masks[1:] + masks[:1]
-    masks += [m for m in mirror_masks(inner) if m not in masks]
-    masks += [inner * m for m in mirror_masks(row_devices // inner) if inner * m not in masks]
     mine, theirs = grads.astype(jnp.bfloat16), None
-    for n, (offset, parent) in enumerate(order):
-        total = add(terms.pop(offset)).astype(jnp.bfloat16)
-        terms[parent].append(queue.swap(total, "row", offset ^ parent, f"sums_{offset}"))
-        if n + 1 < len(order) and stages[order[n + 1][0]] == stages[offset]:
+    for n, code in enumerate(order):
+        parent, step = last_step(code)
+        total = add(terms.pop(code)).astype(jnp.bfloat16)
+        terms[parent].append(row_swap(queue.tie(total), back_steps[step], f"sums_{code}"))
+        ends = n + 1 == len(order)
+        if not ends and stages[order[n + 1]] == stages[code]:
             continue
-        for mask in masks[:1] if n + 1 < len(order) else masks:
+        for step in grad_steps if ends else grad_steps[:1]:
             if theirs is not None:
                 mine = add([mine, after(theirs, queue.last)]).astype(jnp.bfloat16)
-            theirs = queue.swap(mine, "row", mask, f"gradients_{mask}")
-        masks = masks[1:]
+            theirs = row_swap(queue.tie(mine), back_steps[step], f"gradients_{step}")
+        grad_steps = grad_steps[1:]
     feat_grad, weight_grad, bias_grad = finish(terms[0], mine, theirs)
     return hidden, feat_grad, weight_grad, bias_grad.reshape(-1)
 

time: 59 us -> 58.6 us (level)
  waiting for transfers between devices: 17.9 us -> 15 us
  starting transfers between devices: 24.1 us -> 26.7 us
    ppermute x0 -> x17, starting transfers between devices: none -> 21.8 us  [row_swap(): return lax.ppermute(x, ('row', 'col'), pairs)]
    ppermute x25 -> x8, starting transfers between devices: 24.1 us -> 4.86 us  [swap(): return lax.ppermute(x, axis, [(i, i ^ mask) for i in range(size)])]
    ppermute x25 -> x8, waiting for transfers between devices: 17.9 us -> 7.29 us  [swap(): return lax.ppermute(x, axis, [(i, i ^ mask) for i in range(size)])]
    ppermute x0 -> x17, waiting for transfers between devices: none -> 7.73 us  [row_swap(): return lax.ppermute(x, ('row', 'col'), pairs)]
  transfers between devices with their start and end apart: 25 -> 25, of which waited for: 13 -> 11; matrix products, arithmetic and copies ran while one was open for 3% -> 3% of each run, Pallas kernels for 22% -> 22%
where the time goes in v5:
time: 58.6 us; the launch traced here: 58.3 us
  starting transfers between devices  26.7 us (46%)
  waiting for transfers between devices  15 us (26%)
  Pallas kernels  13.5 us (23%)
  between operations  1.52 us (3%)
  other arithmetic  1 us (2%)
  local copies, waits for them, and re-layouts  0.68 us (1%)
    ppermute x17, starting transfers between devices, row_swap(): return lax.ppermute(x, ('row', 'col'), pairs)  21.8 us
    pallas_call x4, Pallas kernels, sparse(): pl.pallas_call(partial(sparse_kernel, which, bits, tuple(offsets), here,...  8.71 us
    ppermute x17, waiting for transfers between devices, row_swap(): return lax.ppermute(x, ('row', 'col'), pairs)  7.73 us
    ppermute x8, waiting for transfers between devices, swap(): return lax.ppermute(x, axis, [(i, i ^ mask) for i in range(size)])  7.29 us
    ppermute x8, starting transfers between devices, swap(): return lax.ppermute(x, axis, [(i, i ^ mask) for i in range(size)])  4.86 us
    pallas_call x1, Pallas kernels, prep(): pl.pallas_call(partial(prep_kernel, per, bits, late, first), out_shape=[j...  2.88 us
  transfers between devices with their start and end apart: 25, of which 11 were waited for; matrix products, arithmetic and copies ran while one was open for 3% of the time, Pallas kernels for 22%

profile of v5, /device:TPU:0, one launch (start us, length us, event | category | flops | bytes accessed | tf_op | source)
XLA Modules:
  0.0 58.3 jit_solution(3669840255273096986)
XLA Ops:
  0.7 5.1 %collective-permute-start.1 = (bf16[4,128,128]{2,1,0:T(8,128)(2,1)}, bf16[4,128,128]{2,1,0:T(8,128)(2,1)S(1)}, u32[]{:S(2)}, u32[]{:S(2)}) collective-permute-start(bf16[4,128,128]{2,1,0:T(8,128)(2,1)} %bitcast.6), channel_id=1, source_target_pairs={{0,24},{1,25},{2,26},{3,27},{4,28},{5,29},{6,30},{7,31},{8,16},{9,... | collective-permute-start | bytes 393224 | tf_op jit(solution)/shard_map/features_1/ppermute | solution.py:80
  6.4 0.7 %pad_add_fusion = s32[161,1]{0,1:T(1,128)S(1)} fusion(s32[1,1]{0,1:T(1,128)} %bitcast.5, s32[80,1]{0,1:T(1,128)} %param.13, s32[80,1]{0,1:T(1,128)} %param.12), kind=kLoop, calls=%fused_computation.8 | loop fusion | flops 322 | bytes 1288 | tf_op jit(solution)/shard_map/concatenate | solution.py:421
  7.2 2.9 %shard_map.111 = (s32[168]{0:T(256)S(1)}, bf16[80,128,128]{2,1,0:T(8,128)(2,1)S(1)}) custom-call(s32[161]{0:T(256)S(1)} %bitcast.10, bf16[80,128,128]{2,1,0:T(8,128)(2,1)} %blocks.1), custom_call_target="tpu_custom_call" | custom-call | flops 1 | bytes 1 | tf_op jit(solution)/shard_map/pallas_call | solution.py:190
  10.1 2.1 %collective-permute-start.3 = (bf16[4,128,128]{2,1,0:T(8,128)(2,1)S(1)}, bf16[4,128,128]{2,1,0:T(8,128)(2,1)S(1)}, u32[]{:S(2)}, u32[]{:S(2)}) collective-permute-start(bf16[4,128,128]{2,1,0:T(8,128)(2,1)S(1)} %collective-permute-done.1.refs_6_), channel_id=1, source_target_pairs={{0,8},{1,5},{2,10},{3,7},{4,12},{5,1},{6,14},{7,3},{8,0},{9,13},{1... | collective-permute-start | bytes 393224 | tf_op jit(solution)/shard_map/features_3/ppermute | solution.py:80
  12.2 1.5 %collective-permute-start.5 = (bf16[4,128,128]{2,1,0:T(8,128)(2,1)S(1)}, bf16[4,128,128]{2,1,0:T(8,128)(2,1)S(1)}, u32[]{:S(2)}, u32[]{:S(2)}) collective-permute-start(bf16[4,128,128]{2,1,0:T(8,128)(2,1)S(1)} %bitcast.8), channel_id=1, source_target_pairs={{0,4},{1,9},{2,6},{3,11},{4,0},{5,13},{6,2},{7,15},{8,12},{9,1},{1... | collective-permute-start | bytes 393224 | tf_op jit(solution)/shard_map/features_4/ppermute | solution.py:80
  13.6 0.5 collective-permute-start.6
  14.2 1.5 %collective-permute-start.2 = (bf16[4,128,128]{2,1,0:T(8,128)(2,1)S(1)}, bf16[4,128,128]{2,1,0:T(8,128)(2,1)S(1)}, u32[]{:S(2)}, u32[]{:S(2)}) collective-permute-start(bf16[4,128,128]{2,1,0:T(8,128)(2,1)S(1)} %collective-permute-done.refs_4_), channel_id=1, source_target_pairs={{0,4},{1,9},{2,6},{3,11},{4,0},{5,13},{6,2},{7,15},{8,12},{9,1},{1... | collective-permute-start | bytes 393224 | tf_op jit(solution)/shard_map/features_6/ppermute | solution.py:80
  15.7 0.8 %collective-permute-done.3.refs_5_ = bf16[4,128,128]{2,1,0:T(8,128)(2,1)S(1)} collective-permute-done((bf16[4,128,128]{2,1,0:T(8,128)(2,1)S(1)}, bf16[4,128,128]{2,1,0:T(8,128)(2,1)S(1)}, u32[]{:S(2)}, u32[]{:S(2)}) %collective-permute-start.3) | collective-permute-done | bytes 131104 | tf_op jit(solution)/shard_map/features_3/ppermute | solution.py:80
  16.5 1.5 %collective-permute-start.4 = (bf16[4,128,128]{2,1,0:T(8,128)(2,1)S(1)}, bf16[4,128,128]{2,1,0:T(8,128)(2,1)S(1)}, u32[]{:S(2)}, u32[]{:S(2)}) collective-permute-start(bf16[4,128,128]{2,1,0:T(8,128)(2,1)S(1)} %collective-permute-done.3.refs_5_), channel_id=1, source_target_pairs={{0,4},{1,9},{2,6},{3,11},{4,0},{5,13},{6,2},{7,15},{8,12},{9,1},{1... | collective-permute-start | bytes 393224 | tf_op jit(solution)/shard_map/features_7/ppermute | solution.py:80
  18.0 1.5 %collective-permute-start.7 = (bf16[512,128]{1,0:T(8,128)(2,1)S(1)}, bf16[512,128]{1,0:T(8,128)(2,1)S(1)}, u32[]{:S(2)}, u32[]{:S(2)}) collective-permute-start(bf16[512,128]{1,0:T(8,128)(2,1)S(1)} %copy-done.1), channel_id=1, source_target_pairs={{0,2},{1,3},{2,0},{3,1},{4,6},{5,7},{6,4},{7,5},{8,10},{9,11},{10,... | collective-permute-start | bytes 393224 | tf_op jit(solution)/shard_map/cotangent/ppermute | solution.py:73
  19.5 2.8 %shard_map.112.refs_4_ = f32[17,128,128]{2,1,0:T(8,128)S(1)} custom-call(s32[168]{0:T(256)S(1)} %get-tuple-element.45.refs_0_, bf16[80,128,128]{2,1,0:T(8,128)(2,1)S(1)} %get-tuple-element.46.refs_1_, bf16[4,128,128]{2,1,0:T(8,128)(2,1)S(1)} %bitcast.9, bf16[4,128,128]{2,1,0:T(8,128)(2,1)S(1)} %collective-permute-done.5.refs_3_, ...), custom_call_target="tpu_custom_call" | custom-call | flops 1 | bytes 1 | tf_op jit(solution)/shard_map/pallas_call | solution.py:300
  22.4 1.6 %shard_map.113 = (f32[4,128,128]{2,1,0:T(8,128)S(1)}, bf16[4,128,128]{2,1,0:T(8,128)(2,1)S(1)}, f32[4,128,128]{2,1,0:T(8,128)S(1)}, bf16[4,128,128]{2,1,0:T(8,128)(2,1)S(1)}) custom-call(s32[168]{0:T(256)S(1)} %get-tuple-element.45.refs_0_, bf16[80,128,128]{2,1,0:T(8,128)(2,1)S(1)} %get-tuple-element.46.refs_1_, ...), custom_call_target="tpu_custom_call" | custom-call | flops 1 | bytes 1 | tf_op jit(solution)/shard_map/pallas_call | solution.py:300
  24.6 0.8 %collective-permute-done.8 = bf16[4,128,128]{2,1,0:T(8,128)(2,1)S(1)} collective-permute-done((bf16[4,128,128]{2,1,0:T(8,128)(2,1)S(1)}, bf16[4,128,128]{2,1,0:T(8,128)(2,1)S(1)}, u32[]{:S(2)}, u32[]{:S(2)}) %collective-permute-start.8) | collective-permute-done | bytes 131104 | tf_op jit(solution)/shard_map/aggregate_1/ppermute | solution.py:73
  25.6 2.0 %collective-permute-start.10 = (bf16[4,128,128]{2,1,0:T(8,128)(2,1)S(1)}, bf16[4,128,128]{2,1,0:T(8,128)(2,1)S(1)}, u32[]{:S(2)}, u32[]{:S(2)}) collective-permute-start(bf16[4,128,128]{2,1,0:T(8,128)(2,1)S(1)} %add_convert_fusion.3.mine), channel_id=1, source_target_pairs={{0,2},{1,3},{2,0},{3,1},{4,6},{5,7},{6,4},{7,5},{8,10},{9,11},{10,... | collective-permute-start | bytes 393224 | tf_op jit(solution)/shard_map/swap/ppermute | solution.py:73
  27.6 4.2 %collective-permute-done.11.theirs = bf16[4,128,128]{2,1,0:T(8,128)(2,1)S(1)} collective-permute-done((bf16[4,128,128]{2,1,0:T(8,128)(2,1)S(1)}, bf16[4,128,128]{2,1,0:T(8,128)(2,1)S(1)}, u32[]{:S(2)}, u32[]{:S(2)}) %collective-permute-start.11) | collective-permute-done | bytes 131104 | tf_op jit(solution)/shard_map/swap/ppermute | solution.py:73
  31.8 0.5 shard_map.115
  32.4 1.4 %collective-permute-done.10.theirs = bf16[4,128,128]{2,1,0:T(8,128)(2,1)S(1)} collective-permute-done((bf16[4,128,128]{2,1,0:T(8,128)(2,1)S(1)}, bf16[4,128,128]{2,1,0:T(8,128)(2,1)S(1)}, u32[]{:S(2)}, u32[]{:S(2)}) %collective-permute-start.10) | collective-permute-done | bytes 131104 | tf_op jit(solution)/shard_map/swap/ppermute | solution.py:73
  33.9 0.5 shard_map.114
  34.5 0.6 collective-permute-start.12
  35.0 0.8 %collective-permute-done.13.refs_3_ = bf16[4,128,128]{2,1,0:T(8,128)(2,1)S(1)} collective-permute-done((bf16[4,128,128]{2,1,0:T(8,128)(2,1)S(1)}, bf16[4,128,128]{2,1,0:T(8,128)(2,1)S(1)}, u32[]{:S(2)}, u32[]{:S(2)}) %collective-permute-start.13) | collective-permute-done | bytes 131104 | tf_op jit(solution)/shard_map/rows_1/ppermute | solution.py:73
  35.8 1.2 %shard_map.116 = bf16[4,128,128]{2,1,0:T(8,128)(2,1)S(1)} custom-call(s32[168]{0:T(256)S(1)} %get-tuple-element.45.refs_0_, bf16[80,128,128]{2,1,0:T(8,128)(2,1)S(1)} %get-tuple-element.46.refs_1_, bf16[4,128,128]{2,1,0:T(8,128)(2,1)S(1)} %get-tuple-element.63.refs_2_, bf16[4,128,128]{2,1,0:T(8,128)(2,1)S(1)} %collective-permute-done.13.refs_3_, ...), custom_call_target="tpu_custom_call" | custom-call | flops 1 | bytes 1 | tf_op jit(solution)/shard_map/pallas_call | solution.py:300
  37.1 2.1 %collective-permute-start.15 = (bf16[144,128]{1,0:T(8,128)(2,1)S(1)}, bf16[144,128]{1,0:T(8,128)(2,1)S(1)}, u32[]{:S(2)}, u32[]{:S(2)}) collective-permute-start(bf16[144,128]{1,0:T(8,128)(2,1)S(1)} %add_convert_fusion.7), channel_id=1, source_target_pairs={{0,8},{1,9},{2,10},{3,11},{4,12},{5,13},{6,14},{7,15},{8,0},{9,1},... | collective-permute-start | bytes 110600 | tf_op jit(solution)/shard_map/gradients_1/ppermute | solution.py:80
  39.3 3.1 %shard_map.117 = (f32[4,128,128]{2,1,0:T(8,128)S(1)}, bf16[4,128,128]{2,1,0:T(8,128)(2,1)S(1)}, bf16[4,128,128]{2,1,0:T(8,128)(2,1)S(1)}, bf16[4,128,128]{2,1,0:...) custom-call(s32[168]{0:T(256)S(1)} %get-tuple-element.45.refs_0_, ...), custom_call_target="tpu_custom_call" | custom-call | flops 1 | bytes 1 | tf_op jit(solution)/shard_map/pallas_call | solution.py:300
  42.8 2.2 %collective-permute-start.20 = (bf16[4,128,128]{2,1,0:T(8,128)(2,1)S(1)}, bf16[4,128,128]{2,1,0:T(8,128)(2,1)S(1)}, u32[]{:S(2)}, u32[]{:S(2)}) collective-permute-start(bf16[4,128,128]{2,1,0:T(8,128)(2,1)S(1)} %add_convert_fusion.2), channel_id=1, source_target_pairs={{0,8},{1,9},{2,10},{3,11},{4,12},{5,13},{6,14},{7,15},{8,0},{9,1},... | collective-permute-start | bytes 393224 | tf_op jit(solution)/shard_map/sums_3/ppermute | solution.py:80
  45.0 2.0 %collective-permute-start.22 = (bf16[4,128,128]{2,1,0:T(8,128)(2,1)S(1)}, bf16[4,128,128]{2,1,0:T(8,128)(2,1)S(1)}, u32[]{:S(2)}, u32[]{:S(2)}) collective-permute-start(bf16[4,128,128]{2,1,0:T(8,128)(2,1)S(1)} %get-tuple-element.73), channel_id=1, source_target_pairs={{0,4},{1,5},{2,6},{3,7},{4,0},{5,1},{6,2},{7,3},{8,12},{9,13},{10,... | collective-permute-start | bytes 393224 | tf_op jit(solution)/shard_map/sums_4/ppermute | solution.py:80
  47.4 1.4 %collective-permute-done.19 = bf16[4,128,128]{2,1,0:T(8,128)(2,1)S(1)} collective-permute-done((bf16[4,128,128]{2,1,0:T(8,128)(2,1)S(1)}, bf16[4,128,128]{2,1,0:T(8,128)(2,1)S(1)}, u32[]{:S(2)}, u32[]{:S(2)}) %collective-permute-start.19) | collective-permute-done | bytes 131104 | tf_op jit(solution)/shard_map/sums_5/ppermute | solution.py:80
  48.9 2.2 %collective-permute-start.23 = (bf16[4,128,128]{2,1,0:T(8,128)(2,1)S(1)}, bf16[4,128,128]{2,1,0:T(8,128)(2,1)S(1)}, u32[]{:S(2)}, u32[]{:S(2)}) collective-permute-start(bf16[4,128,128]{2,1,0:T(8,128)(2,1)S(1)} %add_convert_fusion), channel_id=1, source_target_pairs={{0,24},{1,25},{2,26},{3,27},{4,28},{5,29},{6,30},{7,31},{8,16},{9,... | collective-permute-start | bytes 393224 | tf_op jit(solution)/shard_map/sums_1/ppermute | solution.py:80
  51.1 0.6 collective-permute-done.18
  51.8 1.6 %collective-permute-done.17 = bf16[144,128]{1,0:T(8,128)(2,1)S(1)} collective-permute-done((bf16[144,128]{1,0:T(8,128)(2,1)S(1)}, bf16[144,128]{1,0:T(8,128)(2,1)S(1)}, u32[]{:S(2)}, u32[]{:S(2)}) %collective-permute-start.17) | collective-permute-done | bytes 36896 | tf_op jit(solution)/shard_map/gradients_0/ppermute | solution.py:80
  53.5 0.7 %copy.13 = bf16[512,128]{1,0:T(8,128)(2,1)} copy(bf16[512,128]{1,0:T(8,128)(2,1)S(1)} %get-tuple-element.86) | data formatting | bytes 262144
  54.1 3.2 %collective-permute-done.21.refs_1_ = bf16[144,128]{1,0:T(8,128)(2,1)S(1)} collective-permute-done((bf16[144,128]{1,0:T(8,128)(2,1)S(1)}, bf16[144,128]{1,0:T(8,128)(2,1)S(1)}, u32[]{:S(2)}, u32[]{:S(2)}) %collective-permute-start.21) | collective-permute-done | bytes 36896 | tf_op jit(solution)/shard_map/gradients_2/ppermute | solution.py:80
  57.5 0.9 %shard_map.118 = (f32[512,128]{1,0:T(8,128)}, f32[128,128]{1,0:T(8,128)}, f32[1,128]{1,0:T(1,128)}) custom-call(bf16[144,128]{1,0:T(8,128)(2,1)S(1)} %add_convert_fusion.5.refs_0_, bf16[144,128]{1,0:T(8,128)(2,1)S(1)} %collective-permute-done.21.refs_1_, f32[4,128,128]{2,1,0:T(8,128)S(1)} %get-tuple-element.82.refs_2_, ...), custom_call_target="tpu_custom_call" | custom-call | flops 1 | bytes 1 | tf_op jit(solution)/shard_map/pallas_call | solution.py:387
  (45 shorter events, 2.3 us)
Async XLA Ops:
  0.6 11.5 %copy-start = (bf16[512,128]{1,0:T(8,128)(2,1)S(1)}, bf16[512,128]{1,0:T(8,128)(2,1)}, u32[]{:S(2)}) copy-start(bf16[512,128]{1,0:T(8,128)(2,1)} %param.8) | copy-start | bytes 393220
  0.6 17.3 %copy-start.1 = (bf16[512,128]{1,0:T(8,128)(2,1)S(1)}, bf16[512,128]{1,0:T(8,128)(2,1)}, u32[]{:S(2)}) copy-start(bf16[512,128]{1,0:T(8,128)(2,1)} %cotangent.1) | copy-start | bytes 393220
  0.7 9.4 %collective-permute-start.1 = (bf16[4,128,128]{2,1,0:T(8,128)(2,1)}, bf16[4,128,128]{2,1,0:T(8,128)(2,1)S(1)}, u32[]{:S(2)}, u32[]{:S(2)}) collective-permute-start(bf16[4,128,128]{2,1,0:T(8,128)(2,1)} %bitcast.6), channel_id=1, source_target_pairs={{0,24},{1,25},{2,26},{3,27},{4,28},{5,29},{6,30},{7,31},{8,16},{9,... | collective-permute-start | bytes 393224 | tf_op jit(solution)/shard_map/features_1/ppermute | solution.py:80
  5.8 8.4 %collective-permute-start = (bf16[4,128,128]{2,1,0:T(8,128)(2,1)}, bf16[4,128,128]{2,1,0:T(8,128)(2,1)S(1)}, u32[]{:S(2)}, u32[]{:S(2)}) collective-permute-start(bf16[4,128,128]{2,1,0:T(8,128)(2,1)} %bitcast.7), channel_id=1, source_target_pairs={{0,8},{1,5},{2,10},{3,7},{4,12},{5,1},{6,14},{7,3},{8,0},{9,13},{1... | collective-permute-start | bytes 393224 | tf_op jit(solution)/shard_map/features_2/ppermute | solution.py:80
  10.1 6.4 %collective-permute-start.3 = (bf16[4,128,128]{2,1,0:T(8,128)(2,1)S(1)}, bf16[4,128,128]{2,1,0:T(8,128)(2,1)S(1)}, u32[]{:S(2)}, u32[]{:S(2)}) collective-permute-start(bf16[4,128,128]{2,1,0:T(8,128)(2,1)S(1)} %collective-permute-done.1.refs_6_), channel_id=1, source_target_pairs={{0,8},{1,5},{2,10},{3,7},{4,12},{5,1},{6,14},{7,3},{8,0},{9,13},{1... | collective-permute-start | bytes 393224 | tf_op jit(solution)/shard_map/features_3/ppermute | solution.py:80
  12.2 7.3 %collective-permute-start.5 = (bf16[4,128,128]{2,1,0:T(8,128)(2,1)S(1)}, bf16[4,128,128]{2,1,0:T(8,128)(2,1)S(1)}, u32[]{:S(2)}, u32[]{:S(2)}) collective-permute-start(bf16[4,128,128]{2,1,0:T(8,128)(2,1)S(1)} %bitcast.8), channel_id=1, source_target_pairs={{0,4},{1,9},{2,6},{3,11},{4,0},{5,13},{6,2},{7,15},{8,12},{9,1},{1... | collective-permute-start | bytes 393224 | tf_op jit(solution)/shard_map/features_4/ppermute | solution.py:80
  13.6 5.8 %collective-permute-start.6 = (bf16[4,128,128]{2,1,0:T(8,128)(2,1)S(1)}, bf16[4,128,128]{2,1,0:T(8,128)(2,1)S(1)}, u32[]{:S(2)}, u32[]{:S(2)}) collective-permute-start(bf16[4,128,128]{2,1,0:T(8,128)(2,1)S(1)} %collective-permute-done.1.refs_6_), channel_id=1, source_target_pairs={{0,4},{1,9},{2,6},{3,11},{4,0},{5,13},{6,2},{7,15},{8,12},{9,1},{1... | collective-permute-start | bytes 393224 | tf_op jit(solution)/shard_map/features_5/ppermute | solution.py:80
  14.2 8.2 %collective-permute-start.2 = (bf16[4,128,128]{2,1,0:T(8,128)(2,1)S(1)}, bf16[4,128,128]{2,1,0:T(8,128)(2,1)S(1)}, u32[]{:S(2)}, u32[]{:S(2)}) collective-permute-start(bf16[4,128,128]{2,1,0:T(8,128)(2,1)S(1)} %collective-permute-done.refs_4_), channel_id=1, source_target_pairs={{0,4},{1,9},{2,6},{3,11},{4,0},{5,13},{6,2},{7,15},{8,12},{9,1},{1... | collective-permute-start | bytes 393224 | tf_op jit(solution)/shard_map/features_6/ppermute | solution.py:80
  16.5 5.9 %collective-permute-start.4 = (bf16[4,128,128]{2,1,0:T(8,128)(2,1)S(1)}, bf16[4,128,128]{2,1,0:T(8,128)(2,1)S(1)}, u32[]{:S(2)}, u32[]{:S(2)}) collective-permute-start(bf16[4,128,128]{2,1,0:T(8,128)(2,1)S(1)} %collective-permute-done.3.refs_5_), channel_id=1, source_target_pairs={{0,4},{1,9},{2,6},{3,11},{4,0},{5,13},{6,2},{7,15},{8,12},{9,1},{1... | collective-permute-start | bytes 393224 | tf_op jit(solution)/shard_map/features_7/ppermute | solution.py:80
  18.0 6.1 %collective-permute-start.7 = (bf16[512,128]{1,0:T(8,128)(2,1)S(1)}, bf16[512,128]{1,0:T(8,128)(2,1)S(1)}, u32[]{:S(2)}, u32[]{:S(2)}) collective-permute-start(bf16[512,128]{1,0:T(8,128)(2,1)S(1)} %copy-done.1), channel_id=1, source_target_pairs={{0,2},{1,3},{2,0},{3,1},{4,6},{5,7},{6,4},{7,5},{8,10},{9,11},{10,... | collective-permute-start | bytes 393224 | tf_op jit(solution)/shard_map/cotangent/ppermute | solution.py:73
  22.3 9.5 %copy-start.2 = (bf16[128,128]{1,0:T(8,128)(2,1)S(1)}, bf16[128,128]{1,0:T(8,128)(2,1)}, u32[]{:S(2)}) copy-start(bf16[128,128]{1,0:T(8,128)(2,1)} %weight.3) | copy-start | bytes 98308
  22.3 9.5 %copy-start.3 = (f32[128]{0:T(128)S(1)}, f32[128]{0:T(128)}, u32[]{:S(2)}) copy-start(f32[128]{0:T(128)} %param.10) | copy-start | bytes 1540
  24.0 1.4 %collective-permute-start.8 = (bf16[4,128,128]{2,1,0:T(8,128)(2,1)S(1)}, bf16[4,128,128]{2,1,0:T(8,128)(2,1)S(1)}, u32[]{:S(2)}, u32[]{:S(2)}) collective-permute-start(bf16[4,128,128]{2,1,0:T(8,128)(2,1)S(1)} %get-tuple-element.57), channel_id=1, source_target_pairs={{0,1},{1,0},{2,3},{3,2},{4,5},{5,4},{6,7},{7,6},{8,9},{9,8},{10,11... | collective-permute-start | bytes 393224 | tf_op jit(solution)/shard_map/aggregate_1/ppermute | solution.py:73
  24.1 1.5 %collective-permute-start.9 = (bf16[4,128,128]{2,1,0:T(8,128)(2,1)S(1)}, bf16[4,128,128]{2,1,0:T(8,128)(2,1)S(1)}, u32[]{:S(2)}, u32[]{:S(2)}) collective-permute-start(bf16[4,128,128]{2,1,0:T(8,128)(2,1)S(1)} %get-tuple-element.59), channel_id=1, source_target_pairs={{0,1},{1,0},{2,3},{3,2},{4,5},{5,4},{6,7},{7,6},{8,9},{9,8},{10,11... | collective-permute-start | bytes 393224 | tf_op jit(solution)/shard_map/aggregate_3/ppermute | solution.py:73
  25.4 6.4 %collective-permute-start.11 = (bf16[4,128,128]{2,1,0:T(8,128)(2,1)S(1)}, bf16[4,128,128]{2,1,0:T(8,128)(2,1)S(1)}, u32[]{:S(2)}, u32[]{:S(2)}) collective-permute-start(bf16[4,128,128]{2,1,0:T(8,128)(2,1)S(1)} %add_convert_fusion.4.mine), channel_id=1, source_target_pairs={{0,2},{1,3},{2,0},{3,1},{4,6},{5,7},{6,4},{7,5},{8,10},{9,11},{10,... | collective-permute-start | bytes 393224 | tf_op jit(solution)/shard_map/swap/ppermute | solution.py:73
  25.6 8.2 %collective-permute-start.10 = (bf16[4,128,128]{2,1,0:T(8,128)(2,1)S(1)}, bf16[4,128,128]{2,1,0:T(8,128)(2,1)S(1)}, u32[]{:S(2)}, u32[]{:S(2)}) collective-permute-start(bf16[4,128,128]{2,1,0:T(8,128)(2,1)S(1)} %add_convert_fusion.3.mine), channel_id=1, source_target_pairs={{0,2},{1,3},{2,0},{3,1},{4,6},{5,7},{6,4},{7,5},{8,10},{9,11},{10,... | collective-permute-start | bytes 393224 | tf_op jit(solution)/shard_map/swap/ppermute | solution.py:73
  32.4 2.7 %collective-permute-start.14 = (bf16[4,128,128]{2,1,0:T(8,128)(2,1)S(1)}, bf16[4,128,128]{2,1,0:T(8,128)(2,1)S(1)}, u32[]{:S(2)}, u32[]{:S(2)}) collective-permute-start(bf16[4,128,128]{2,1,0:T(8,128)(2,1)S(1)} %get-tuple-element.64.refs_4_), channel_id=1, source_target_pairs={{0,1},{1,0},{2,3},{3,2},{4,5},{5,4},{6,7},{7,6},{8,9},{9,8},{10,11... | collective-permute-start | bytes 393224 | tf_op jit(solution)/shard_map/rows_3/ppermute | solution.py:73
  34.4 1.4 %collective-permute-start.13 = (bf16[4,128,128]{2,1,0:T(8,128)(2,1)S(1)}, bf16[4,128,128]{2,1,0:T(8,128)(2,1)S(1)}, u32[]{:S(2)}, u32[]{:S(2)}) collective-permute-start(bf16[4,128,128]{2,1,0:T(8,128)(2,1)S(1)} %get-tuple-element.63.refs_2_), channel_id=1, source_target_pairs={{0,1},{1,0},{2,3},{3,2},{4,5},{5,4},{6,7},{7,6},{8,9},{9,8},{10,11... | collective-permute-start | bytes 393224 | tf_op jit(solution)/shard_map/rows_1/ppermute | solution.py:73
  34.5 2.6 %collective-permute-start.12 = (f32[144,128]{1,0:T(8,128)S(1)}, f32[144,128]{1,0:T(8,128)S(1)}, u32[]{:S(2)}, u32[]{:S(2)}) collective-permute-start(f32[144,128]{1,0:T(8,128)S(1)} %add.32), channel_id=1, source_target_pairs={{0,1},{1,0},{2,3},{3,2},{4,5},{5,4},{6,7},{7,6},{8,9},{9,8},{10,11... | collective-permute-start | bytes 221192 | tf_op jit(solution)/shard_map/swap/ppermute | solution.py:73
  37.0 5.7 %collective-permute-start.16 = (bf16[4,128,128]{2,1,0:T(8,128)(2,1)S(1)}, bf16[4,128,128]{2,1,0:T(8,128)(2,1)S(1)}, u32[]{:S(2)}, u32[]{:S(2)}) collective-permute-start(bf16[4,128,128]{2,1,0:T(8,128)(2,1)S(1)} %shard_map.116), channel_id=1, source_target_pairs={{0,4},{1,5},{2,6},{3,7},{4,0},{5,1},{6,2},{7,3},{8,12},{9,13},{10,... | collective-permute-start | bytes 393224 | tf_op jit(solution)/shard_map/sums_7/ppermute | solution.py:80
  37.1 9.9 %collective-permute-start.15 = (bf16[144,128]{1,0:T(8,128)(2,1)S(1)}, bf16[144,128]{1,0:T(8,128)(2,1)S(1)}, u32[]{:S(2)}, u32[]{:S(2)}) collective-permute-start(bf16[144,128]{1,0:T(8,128)(2,1)S(1)} %add_convert_fusion.7), channel_id=1, source_target_pairs={{0,8},{1,9},{2,10},{3,11},{4,12},{5,13},{6,14},{7,15},{8,0},{9,1},... | collective-permute-start | bytes 110600 | tf_op jit(solution)/shard_map/gradients_1/ppermute | solution.py:80
  42.3 6.5 %collective-permute-start.19 = (bf16[4,128,128]{2,1,0:T(8,128)(2,1)S(1)}, bf16[4,128,128]{2,1,0:T(8,128)(2,1)S(1)}, u32[]{:S(2)}, u32[]{:S(2)}) collective-permute-start(bf16[4,128,128]{2,1,0:T(8,128)(2,1)S(1)} %get-tuple-element.70), channel_id=1, source_target_pairs={{0,4},{1,5},{2,6},{3,7},{4,0},{5,1},{6,2},{7,3},{8,12},{9,13},{10,... | collective-permute-start | bytes 393224 | tf_op jit(solution)/shard_map/sums_5/ppermute | solution.py:80
  42.8 6.0 %collective-permute-start.20 = (bf16[4,128,128]{2,1,0:T(8,128)(2,1)S(1)}, bf16[4,128,128]{2,1,0:T(8,128)(2,1)S(1)}, u32[]{:S(2)}, u32[]{:S(2)}) collective-permute-start(bf16[4,128,128]{2,1,0:T(8,128)(2,1)S(1)} %add_convert_fusion.2), channel_id=1, source_target_pairs={{0,8},{1,9},{2,10},{3,11},{4,12},{5,13},{6,14},{7,15},{8,0},{9,1},... | collective-permute-start | bytes 393224 | tf_op jit(solution)/shard_map/sums_3/ppermute | solution.py:80
  45.0 6.6 %collective-permute-start.18 = (bf16[4,128,128]{2,1,0:T(8,128)(2,1)S(1)}, bf16[4,128,128]{2,1,0:T(8,128)(2,1)S(1)}, u32[]{:S(2)}, u32[]{:S(2)}) collective-permute-start(bf16[4,128,128]{2,1,0:T(8,128)(2,1)S(1)} %get-tuple-element.72), channel_id=1, source_target_pairs={{0,4},{1,5},{2,6},{3,7},{4,0},{5,1},{6,2},{7,3},{8,12},{9,13},{10,... | collective-permute-start | bytes 393224 | tf_op jit(solution)/shard_map/sums_6/ppermute | solution.py:80
  45.0 9.1 %collective-permute-start.22 = (bf16[4,128,128]{2,1,0:T(8,128)(2,1)S(1)}, bf16[4,128,128]{2,1,0:T(8,128)(2,1)S(1)}, u32[]{:S(2)}, u32[]{:S(2)}) collective-permute-start(bf16[4,128,128]{2,1,0:T(8,128)(2,1)S(1)} %get-tuple-element.73), channel_id=1, source_target_pairs={{0,4},{1,5},{2,6},{3,7},{4,0},{5,1},{6,2},{7,3},{8,12},{9,13},{10,... | collective-permute-start | bytes 393224 | tf_op jit(solution)/shard_map/sums_4/ppermute | solution.py:80
  47.1 6.3 %collective-permute-start.17 = (bf16[144,128]{1,0:T(8,128)(2,1)S(1)}, bf16[144,128]{1,0:T(8,128)(2,1)S(1)}, u32[]{:S(2)}, u32[]{:S(2)}) collective-permute-start(bf16[144,128]{1,0:T(8,128)(2,1)S(1)} %add_convert_fusion.6), channel_id=1, source_target_pairs={{0,24},{1,25},{2,26},{3,27},{4,28},{5,29},{6,30},{7,31},{8,16},{9,... | collective-permute-start | bytes 110600 | tf_op jit(solution)/shard_map/gradients_0/ppermute | solution.py:80
  48.9 8.6 %collective-permute-start.23 = (bf16[4,128,128]{2,1,0:T(8,128)(2,1)S(1)}, bf16[4,128,128]{2,1,0:T(8,128)(2,1)S(1)}, u32[]{:S(2)}, u32[]{:S(2)}) collective-permute-start(bf16[4,128,128]{2,1,0:T(8,128)(2,1)S(1)} %add_convert_fusion), channel_id=1, source_target_pairs={{0,24},{1,25},{2,26},{3,27},{4,28},{5,29},{6,30},{7,31},{8,16},{9,... | collective-permute-start | bytes 393224 | tf_op jit(solution)/shard_map/sums_1/ppermute | solution.py:80
  51.7 5.8 %collective-permute-start.24 = (bf16[4,128,128]{2,1,0:T(8,128)(2,1)S(1)}, bf16[4,128,128]{2,1,0:T(8,128)(2,1)S(1)}, u32[]{:S(2)}, u32[]{:S(2)}) collective-permute-start(bf16[4,128,128]{2,1,0:T(8,128)(2,1)S(1)} %add_convert_fusion.1), channel_id=1, source_target_pairs={{0,8},{1,9},{2,10},{3,11},{4,12},{5,13},{6,14},{7,15},{8,0},{9,1},... | collective-permute-start | bytes 393224 | tf_op jit(solution)/shard_map/sums_2/ppermute | solution.py:80
  53.4 4.0 %collective-permute-start.21 = (bf16[144,128]{1,0:T(8,128)(2,1)S(1)}, bf16[144,128]{1,0:T(8,128)(2,1)S(1)}, u32[]{:S(2)}, u32[]{:S(2)}) collective-permute-start(bf16[144,128]{1,0:T(8,128)(2,1)S(1)} %add_convert_fusion.5.refs_0_), channel_id=1, source_target_pairs={{0,4},{1,5},{2,6},{3,7},{4,0},{5,1},{6,2},{7,3},{8,12},{9,13},{10,... | collective-permute-start | bytes 110600 | tf_op jit(solution)/shard_map/gradients_2/ppermute | solution.py:80

commit v6 on v5

--- a/solution.py
+++ b/solution.py
@@ -151,22 +151,32 @@
     return 2 if slots % 2 == 0 else 1
 
 
-def prep_kernel(per, bits, late, first, indices, blocks, table, held, sem):
+def prep_kernel(
+    per, bits, late, first, in_rows, in_cols, live_slots, blocks, table, held, rows, cols, sem, small_sem
+):
     slots = blocks.shape[0]
+    small = [
+        pltpu.make_async_copy(source, target, small_sem.at[n])
+        for n, (source, target) in enumerate(((in_rows, rows), (in_cols, cols)))
+    ]
+    for copy in small:
+        copy.start()
     parts = parts_of(slots)
     copies = []
     for n in range(parts):
         place = pl.ds(n * (slots // parts), slots // parts)
         copies.append(pltpu.make_async_copy(blocks.at[place], held.at[place], sem.at[n]))
         copies[-1].start()
+    for copy in small:
+        copy.wait()
     row_at = lax.axis_index("row")
-    live = indices[2 * slots]
+    live = live_slots[0, 0]
 
     def step(i, lengths):
         early, late_ones, soon, last = lengths
         for u in range(unroll):
             k = i * unroll + u
-            row, col = indices[k], indices[slots + k]
+            row, col = rows[k], cols[k]
             entry = k + lax.shift_left(row, bits[0]) + lax.shift_left(col, bits[0] + bits[1])
             in_use = (k < live).astype(jnp.int32)
             offset = lax.bitwise_xor(row_at, lax.div(col, per))
@@ -185,20 +195,28 @@
         copy.wait()
 
 
-def prep(indices, blocks, per, bits, late, first):
+def prep(block_rows, block_cols, tile_slot_count, blocks, per, bits, late, first):
     slots = blocks.shape[0]
+    in_hbm = partial(pltpu.with_memory_space_constraint, memory_space=pltpu.HBM)
     return pl.pallas_call(
         partial(prep_kernel, per, bits, late, first),
         out_shape=[
             jax.ShapeDtypeStruct((2 * slots + 8,), jnp.int32),
             jax.ShapeDtypeStruct(blocks.shape, blocks.dtype),
         ],
-        in_specs=[SMEM, HBM],
+        in_specs=[HBM, HBM, SMEM, HBM],
         out_specs=[SMEM, VMEM],
-        scratch_shapes=[pltpu.SemaphoreType.DMA((parts_of(slots),))],
+        scratch_shapes=[
+            pltpu.SMEM((slots,), jnp.int32),
+            pltpu.SMEM((slots,), jnp.int32),
+            pltpu.SemaphoreType.DMA((parts_of(slots),)),
+            pltpu.SemaphoreType.DMA((2,)),
+        ],
         compiler_params=pltpu.CompilerParams(vmem_limit_bytes=50 << 20),
         cost_estimate=QUICK,
-    )(indices, blocks)
+    )(
+        in_hbm(block_rows.reshape(slots)), in_hbm(block_cols.reshape(slots)), tile_slot_count, in_hbm(blocks)
+    )
 
 
 def sparse_kernel(which, bits, offsets, here, there, sums, starts, *refs):
@@ -418,8 +436,9 @@
     late_columns = [offset_of(code, there) for code in late_codes]
     first = [offset_of(code, back_steps) for code in first_codes]
     bits = widths(blocks.shape[0], row_blocks, column_blocks)
-    indices = jnp.concatenate([block_rows, block_cols, tile_slot_count], axis=0)[:, 0]
-    table, held = prep(indices, blocks, per, bits, late_columns, first)
+    table, held = prep(
+        block_rows, block_cols, tile_slot_count, blocks, per, bits, late_columns, first
+    )
     pieces = {0: features.reshape(per, BS, channels)}
     queue = Queue()
     for code in codes:

time: 58.6 us -> 58.5 us (level); the launches traced: 58.3 us -> 58.9 us
  starting transfers between devices: 26.7 us -> 33.1 us
  Pallas kernels: 13.5 us -> 9.43 us
  waiting for transfers between devices: 15 us -> 14 us
  other arithmetic: 1 us -> 0.25 us
    ppermute x17, starting transfers between devices: 21.8 us -> 28.6 us  [row_swap(): return lax.ppermute(x, ('row', 'col'), pairs)]
    pallas_call x4, Pallas kernels: 8.71 us -> 5.17 us  [sparse(): pl.pallas_call(partial(sparse_kernel, which, bits, tuple(offsets), here,...]
    ppermute x17, waiting for transfers between devices: 7.73 us -> 6.32 us  [row_swap(): return lax.ppermute(x, ('row', 'col'), pairs)]
    concatenate x1 -> x0, other arithmetic: 0.75 us -> none  [on_device(): jnp.concatenate([block_rows, block_cols, tile_slot_count], axis=0)[:, 0]]
  transfers between devices with their start and end apart: 25 -> 25, of which waited for: 11 -> 10; matrix products, arithmetic and copies ran while one was open for 3% -> 2% of each run, Pallas kernels for 22% -> 15%
where the time goes in v6:
time: 58.5 us; the launch traced here: 58.9 us
  starting transfers between devices  33.1 us (57%)
  waiting for transfers between devices  14 us (24%)
  Pallas kernels  9.43 us (16%)
  between operations  1.47 us (3%)
  local copies, waits for them, and re-layouts  0.68 us (1%)
    ppermute x17, starting transfers between devices, row_swap(): return lax.ppermute(x, ('row', 'col'), pairs)  28.6 us
    ppermute x8, waiting for transfers between devices, swap(): return lax.ppermute(x, axis, [(i, i ^ mask) for i in range(size)])  7.71 us
    ppermute x17, waiting for transfers between devices, row_swap(): return lax.ppermute(x, ('row', 'col'), pairs)  6.32 us
    pallas_call x4, Pallas kernels, sparse(): pl.pallas_call(partial(sparse_kernel, which, bits, tuple(offsets), here,...  5.17 us
    ppermute x8, starting transfers between devices, swap(): return lax.ppermute(x, axis, [(i, i ^ mask) for i in range(size)])  4.45 us
    pallas_call x1, Pallas kernels, prep(): pl.pallas_call(partial(prep_kernel, per, bits, late, first), out_shape=[j...  2.35 us
  transfers between devices with their start and end apart: 25, of which 10 were waited for; matrix products, arithmetic and copies ran while one was open for 2% of the time, Pallas kernels for 15%

profile of v6, /device:TPU:0, one launch (start us, length us, event | category | flops | bytes accessed | tf_op | source)
XLA Modules:
  0.0 58.9 jit_solution(10082095550312250461)
XLA Ops:
  0.7 5.1 %collective-permute-start.1 = (bf16[4,128,128]{2,1,0:T(8,128)(2,1)}, bf16[4,128,128]{2,1,0:T(8,128)(2,1)S(1)}, u32[]{:S(2)}, u32[]{:S(2)}) collective-permute-start(bf16[4,128,128]{2,1,0:T(8,128)(2,1)} %bitcast.5), channel_id=1, source_target_pairs={{0,24},{1,25},{2,26},{3,27},{4,28},{5,29},{6,30},{7,31},{8,16},{9,... | collective-permute-start | bytes 393224 | tf_op jit(solution)/shard_map/features_1/ppermute | solution.py:80
  6.4 2.3 %shard_map.111 = (s32[168]{0:T(256)S(1)}, bf16[80,128,128]{2,1,0:T(8,128)(2,1)S(1)}) custom-call(s32[80]{0:T(128)} %bitcast.11, s32[80]{0:T(128)} %bitcast.12, s32[1,1]{1,0:T(1,128)S(6)} %copy.13.live_slots, bf16[80,128,128]{2,1,0:T(8,128)(2,1)} %blocks.1), custom_call_target="tpu_custom_call" | custom-call | flops 1 | bytes 1 | tf_op jit(solution)/shard_map/pallas_call | solution.py:201
  8.8 0.8 %collective-permute-done.1.refs_6_ = bf16[4,128,128]{2,1,0:T(8,128)(2,1)S(1)} collective-permute-done((bf16[4,128,128]{2,1,0:T(8,128)(2,1)}, bf16[4,128,128]{2,1,0:T(8,128)(2,1)S(1)}, u32[]{:S(2)}, u32[]{:S(2)}) %collective-permute-start.1) | collective-permute-done | bytes 131104 | tf_op jit(solution)/shard_map/features_1/ppermute | solution.py:80
  9.6 2.4 %collective-permute-start.3 = (bf16[4,128,128]{2,1,0:T(8,128)(2,1)S(1)}, bf16[4,128,128]{2,1,0:T(8,128)(2,1)S(1)}, u32[]{:S(2)}, u32[]{:S(2)}) collective-permute-start(bf16[4,128,128]{2,1,0:T(8,128)(2,1)S(1)} %collective-permute-done.1.refs_6_), channel_id=1, source_target_pairs={{0,8},{1,5},{2,10},{3,7},{4,12},{5,1},{6,14},{7,3},{8,0},{9,13},{1... | collective-permute-start | bytes 393224 | tf_op jit(solution)/shard_map/features_3/ppermute | solution.py:80
  12.0 1.5 %collective-permute-start.5 = (bf16[4,128,128]{2,1,0:T(8,128)(2,1)S(1)}, bf16[4,128,128]{2,1,0:T(8,128)(2,1)S(1)}, u32[]{:S(2)}, u32[]{:S(2)}) collective-permute-start(bf16[4,128,128]{2,1,0:T(8,128)(2,1)S(1)} %bitcast.7), channel_id=1, source_target_pairs={{0,4},{1,9},{2,6},{3,11},{4,0},{5,13},{6,2},{7,15},{8,12},{9,1},{1... | collective-permute-start | bytes 393224 | tf_op jit(solution)/shard_map/features_4/ppermute | solution.py:80
  13.5 0.6 collective-permute-start.6
  14.1 1.5 %collective-permute-start.2 = (bf16[4,128,128]{2,1,0:T(8,128)(2,1)S(1)}, bf16[4,128,128]{2,1,0:T(8,128)(2,1)S(1)}, u32[]{:S(2)}, u32[]{:S(2)}) collective-permute-start(bf16[4,128,128]{2,1,0:T(8,128)(2,1)S(1)} %collective-permute-done.refs_4_), channel_id=1, source_target_pairs={{0,4},{1,9},{2,6},{3,11},{4,0},{5,13},{6,2},{7,15},{8,12},{9,1},{1... | collective-permute-start | bytes 393224 | tf_op jit(solution)/shard_map/features_6/ppermute | solution.py:80
  15.5 0.8 %collective-permute-done.3.refs_5_ = bf16[4,128,128]{2,1,0:T(8,128)(2,1)S(1)} collective-permute-done((bf16[4,128,128]{2,1,0:T(8,128)(2,1)S(1)}, bf16[4,128,128]{2,1,0:T(8,128)(2,1)S(1)}, u32[]{:S(2)}, u32[]{:S(2)}) %collective-permute-start.3) | collective-permute-done | bytes 131104 | tf_op jit(solution)/shard_map/features_3/ppermute | solution.py:80
  16.3 1.5 %collective-permute-start.4 = (bf16[4,128,128]{2,1,0:T(8,128)(2,1)S(1)}, bf16[4,128,128]{2,1,0:T(8,128)(2,1)S(1)}, u32[]{:S(2)}, u32[]{:S(2)}) collective-permute-start(bf16[4,128,128]{2,1,0:T(8,128)(2,1)S(1)} %collective-permute-done.3.refs_5_), channel_id=1, source_target_pairs={{0,4},{1,9},{2,6},{3,11},{4,0},{5,13},{6,2},{7,15},{8,12},{9,1},{1... | collective-permute-start | bytes 393224 | tf_op jit(solution)/shard_map/features_7/ppermute | solution.py:80
  17.8 1.5 %collective-permute-start.7 = (bf16[512,128]{1,0:T(8,128)(2,1)S(1)}, bf16[512,128]{1,0:T(8,128)(2,1)S(1)}, u32[]{:S(2)}, u32[]{:S(2)}) collective-permute-start(bf16[512,128]{1,0:T(8,128)(2,1)S(1)} %copy-done.1), channel_id=1, source_target_pairs={{0,2},{1,3},{2,0},{3,1},{4,6},{5,7},{6,4},{7,5},{8,10},{9,11},{10,... | collective-permute-start | bytes 393224 | tf_op jit(solution)/shard_map/cotangent/ppermute | solution.py:73
  19.3 1.7 %shard_map.112.refs_4_ = f32[17,128,128]{2,1,0:T(8,128)S(1)} custom-call(s32[168]{0:T(256)S(1)} %get-tuple-element.45.refs_0_, bf16[80,128,128]{2,1,0:T(8,128)(2,1)S(1)} %get-tuple-element.46.refs_1_, bf16[4,128,128]{2,1,0:T(8,128)(2,1)S(1)} %bitcast.8, bf16[4,128,128]{2,1,0:T(8,128)(2,1)S(1)} %collective-permute-done.5.refs_3_, ...), custom_call_target="tpu_custom_call" | custom-call | flops 1 | bytes 1 | tf_op jit(solution)/shard_map/pallas_call | solution.py:318
  21.3 0.9 %shard_map.113 = (f32[4,128,128]{2,1,0:T(8,128)S(1)}, bf16[4,128,128]{2,1,0:T(8,128)(2,1)S(1)}, f32[4,128,128]{2,1,0:T(8,128)S(1)}, bf16[4,128,128]{2,1,0:T(8,128)(2,1)S(1)}) custom-call(s32[168]{0:T(256)S(1)} %get-tuple-element.45.refs_0_, bf16[80,128,128]{2,1,0:T(8,128)(2,1)S(1)} %get-tuple-element.46.refs_1_, ...), custom_call_target="tpu_custom_call" | custom-call | flops 1 | bytes 1 | tf_op jit(solution)/shard_map/pallas_call | solution.py:318
  22.8 0.8 %collective-permute-done.8 = bf16[4,128,128]{2,1,0:T(8,128)(2,1)S(1)} collective-permute-done((bf16[4,128,128]{2,1,0:T(8,128)(2,1)S(1)}, bf16[4,128,128]{2,1,0:T(8,128)(2,1)S(1)}, u32[]{:S(2)}, u32[]{:S(2)}) %collective-permute-start.8) | collective-permute-done | bytes 131104 | tf_op jit(solution)/shard_map/aggregate_1/ppermute | solution.py:73
  23.7 1.6 %collective-permute-start.11 = (bf16[4,128,128]{2,1,0:T(8,128)(2,1)S(1)}, bf16[4,128,128]{2,1,0:T(8,128)(2,1)S(1)}, u32[]{:S(2)}, u32[]{:S(2)}) collective-permute-start(bf16[4,128,128]{2,1,0:T(8,128)(2,1)S(1)} %add_convert_fusion.4.mine), channel_id=1, source_target_pairs={{0,2},{1,3},{2,0},{3,1},{4,6},{5,7},{6,4},{7,5},{8,10},{9,11},{10,... | collective-permute-start | bytes 393224 | tf_op jit(solution)/shard_map/swap/ppermute | solution.py:73
  25.3 0.6 collective-permute-start.10
  25.9 4.2 %collective-permute-done.11.theirs = bf16[4,128,128]{2,1,0:T(8,128)(2,1)S(1)} collective-permute-done((bf16[4,128,128]{2,1,0:T(8,128)(2,1)S(1)}, bf16[4,128,128]{2,1,0:T(8,128)(2,1)S(1)}, u32[]{:S(2)}, u32[]{:S(2)}) %collective-permute-start.11) | collective-permute-done | bytes 131104 | tf_op jit(solution)/shard_map/swap/ppermute | solution.py:73
  30.7 1.4 %collective-permute-done.10.theirs = bf16[4,128,128]{2,1,0:T(8,128)(2,1)S(1)} collective-permute-done((bf16[4,128,128]{2,1,0:T(8,128)(2,1)S(1)}, bf16[4,128,128]{2,1,0:T(8,128)(2,1)S(1)}, u32[]{:S(2)}, u32[]{:S(2)}) %collective-permute-start.10) | collective-permute-done | bytes 131104 | tf_op jit(solution)/shard_map/swap/ppermute | solution.py:73
  33.3 0.8 %collective-permute-done.13.refs_3_ = bf16[4,128,128]{2,1,0:T(8,128)(2,1)S(1)} collective-permute-done((bf16[4,128,128]{2,1,0:T(8,128)(2,1)S(1)}, bf16[4,128,128]{2,1,0:T(8,128)(2,1)S(1)}, u32[]{:S(2)}, u32[]{:S(2)}) %collective-permute-start.13) | collective-permute-done | bytes 131104 | tf_op jit(solution)/shard_map/rows_1/ppermute | solution.py:73
  34.0 1.0 %shard_map.116 = bf16[4,128,128]{2,1,0:T(8,128)(2,1)S(1)} custom-call(s32[168]{0:T(256)S(1)} %get-tuple-element.45.refs_0_, bf16[80,128,128]{2,1,0:T(8,128)(2,1)S(1)} %get-tuple-element.46.refs_1_, bf16[4,128,128]{2,1,0:T(8,128)(2,1)S(1)} %get-tuple-element.63.refs_2_, bf16[4,128,128]{2,1,0:T(8,128)(2,1)S(1)} %collective-permute-done.13.refs_3_, ...), custom_call_target="tpu_custom_call" | custom-call | flops 1 | bytes 1 | tf_op jit(solution)/shard_map/pallas_call | solution.py:318
  35.0 2.3 %collective-permute-start.16 = (bf16[4,128,128]{2,1,0:T(8,128)(2,1)S(1)}, bf16[4,128,128]{2,1,0:T(8,128)(2,1)S(1)}, u32[]{:S(2)}, u32[]{:S(2)}) collective-permute-start(bf16[4,128,128]{2,1,0:T(8,128)(2,1)S(1)} %shard_map.116), channel_id=1, source_target_pairs={{0,4},{1,5},{2,6},{3,7},{4,0},{5,1},{6,2},{7,3},{8,12},{9,13},{10,... | collective-permute-start | bytes 393224 | tf_op jit(solution)/shard_map/sums_7/ppermute | solution.py:80
  37.3 2.1 %collective-permute-start.15 = (bf16[144,128]{1,0:T(8,128)(2,1)S(1)}, bf16[144,128]{1,0:T(8,128)(2,1)S(1)}, u32[]{:S(2)}, u32[]{:S(2)}) collective-permute-start(bf16[144,128]{1,0:T(8,128)(2,1)S(1)} %add_convert_fusion.7), channel_id=1, source_target_pairs={{0,8},{1,9},{2,10},{3,11},{4,12},{5,13},{6,14},{7,15},{8,0},{9,1},... | collective-permute-start | bytes 110600 | tf_op jit(solution)/shard_map/gradients_1/ppermute | solution.py:80
  39.4 1.6 %shard_map.117 = (f32[4,128,128]{2,1,0:T(8,128)S(1)}, bf16[4,128,128]{2,1,0:T(8,128)(2,1)S(1)}, bf16[4,128,128]{2,1,0:T(8,128)(2,1)S(1)}, bf16[4,128,128]{2,1,0:...) custom-call(s32[168]{0:T(256)S(1)} %get-tuple-element.45.refs_0_, ...), custom_call_target="tpu_custom_call" | custom-call | flops 1 | bytes 1 | tf_op jit(solution)/shard_map/pallas_call | solution.py:318
  41.0 2.1 %collective-permute-start.19 = (bf16[4,128,128]{2,1,0:T(8,128)(2,1)S(1)}, bf16[4,128,128]{2,1,0:T(8,128)(2,1)S(1)}, u32[]{:S(2)}, u32[]{:S(2)}) collective-permute-start(bf16[4,128,128]{2,1,0:T(8,128)(2,1)S(1)} %get-tuple-element.70), channel_id=1, source_target_pairs={{0,4},{1,5},{2,6},{3,7},{4,0},{5,1},{6,2},{7,3},{8,12},{9,13},{10,... | collective-permute-start | bytes 393224 | tf_op jit(solution)/shard_map/sums_5/ppermute | solution.py:80
  43.3 1.6 %collective-permute-start.18 = (bf16[4,128,128]{2,1,0:T(8,128)(2,1)S(1)}, bf16[4,128,128]{2,1,0:T(8,128)(2,1)S(1)}, u32[]{:S(2)}, u32[]{:S(2)}) collective-permute-start(bf16[4,128,128]{2,1,0:T(8,128)(2,1)S(1)} %get-tuple-element.72), channel_id=1, source_target_pairs={{0,4},{1,5},{2,6},{3,7},{4,0},{5,1},{6,2},{7,3},{8,12},{9,13},{10,... | collective-permute-start | bytes 393224 | tf_op jit(solution)/shard_map/sums_6/ppermute | solution.py:80
  45.4 4.1 %collective-permute-start.17 = (bf16[144,128]{1,0:T(8,128)(2,1)S(1)}, bf16[144,128]{1,0:T(8,128)(2,1)S(1)}, u32[]{:S(2)}, u32[]{:S(2)}) collective-permute-start(bf16[144,128]{1,0:T(8,128)(2,1)S(1)} %add_convert_fusion.6), channel_id=1, source_target_pairs={{0,24},{1,25},{2,26},{3,27},{4,28},{5,29},{6,30},{7,31},{8,16},{9,... | collective-permute-start | bytes 110600 | tf_op jit(solution)/shard_map/gradients_0/ppermute | solution.py:80
  49.5 0.9 %collective-permute-start.23 = (bf16[4,128,128]{2,1,0:T(8,128)(2,1)S(1)}, bf16[4,128,128]{2,1,0:T(8,128)(2,1)S(1)}, u32[]{:S(2)}, u32[]{:S(2)}) collective-permute-start(bf16[4,128,128]{2,1,0:T(8,128)(2,1)S(1)} %add_convert_fusion), channel_id=1, source_target_pairs={{0,24},{1,25},{2,26},{3,27},{4,28},{5,29},{6,30},{7,31},{8,16},{9,... | collective-permute-start | bytes 393224 | tf_op jit(solution)/shard_map/sums_1/ppermute | solution.py:80
  50.5 1.2 %collective-permute-start.24 = (bf16[4,128,128]{2,1,0:T(8,128)(2,1)S(1)}, bf16[4,128,128]{2,1,0:T(8,128)(2,1)S(1)}, u32[]{:S(2)}, u32[]{:S(2)}) collective-permute-start(bf16[4,128,128]{2,1,0:T(8,128)(2,1)S(1)} %add_convert_fusion.1), channel_id=1, source_target_pairs={{0,8},{1,9},{2,10},{3,11},{4,12},{5,13},{6,14},{7,15},{8,0},{9,1},... | collective-permute-start | bytes 393224 | tf_op jit(solution)/shard_map/sums_2/ppermute | solution.py:80
  51.7 1.3 %collective-permute-start.21 = (bf16[144,128]{1,0:T(8,128)(2,1)S(1)}, bf16[144,128]{1,0:T(8,128)(2,1)S(1)}, u32[]{:S(2)}, u32[]{:S(2)}) collective-permute-start(bf16[144,128]{1,0:T(8,128)(2,1)S(1)} %add_convert_fusion.5.refs_0_), channel_id=1, source_target_pairs={{0,4},{1,5},{2,6},{3,7},{4,0},{5,1},{6,2},{7,3},{8,12},{9,13},{10,... | collective-permute-start | bytes 110600 | tf_op jit(solution)/shard_map/gradients_2/ppermute | solution.py:80
  53.0 0.7 %copy.12 = bf16[512,128]{1,0:T(8,128)(2,1)} copy(bf16[512,128]{1,0:T(8,128)(2,1)S(1)} %get-tuple-element.86) | data formatting | bytes 262144
  53.7 2.1 %collective-permute-done.21.refs_1_ = bf16[144,128]{1,0:T(8,128)(2,1)S(1)} collective-permute-done((bf16[144,128]{1,0:T(8,128)(2,1)S(1)}, bf16[144,128]{1,0:T(8,128)(2,1)S(1)}, u32[]{:S(2)}, u32[]{:S(2)}) %collective-permute-start.21) | collective-permute-done | bytes 36896 | tf_op jit(solution)/shard_map/gradients_2/ppermute | solution.py:80
  55.7 2.3 %collective-permute-done.24.refs_5_ = bf16[4,128,128]{2,1,0:T(8,128)(2,1)S(1)} collective-permute-done((bf16[4,128,128]{2,1,0:T(8,128)(2,1)S(1)}, bf16[4,128,128]{2,1,0:T(8,128)(2,1)S(1)}, u32[]{:S(2)}, u32[]{:S(2)}) %collective-permute-start.24) | collective-permute-done | bytes 131104 | tf_op jit(solution)/shard_map/sums_2/ppermute | solution.py:80
  58.0 0.9 %shard_map.118 = (f32[512,128]{1,0:T(8,128)}, f32[128,128]{1,0:T(8,128)}, f32[1,128]{1,0:T(1,128)}) custom-call(bf16[144,128]{1,0:T(8,128)(2,1)S(1)} %add_convert_fusion.5.refs_0_, bf16[144,128]{1,0:T(8,128)(2,1)S(1)} %collective-permute-done.21.refs_1_, f32[4,128,128]{2,1,0:T(8,128)S(1)} %get-tuple-element.82.refs_2_, ...), custom_call_target="tpu_custom_call" | custom-call | flops 1 | bytes 1 | tf_op jit(solution)/shard_map/pallas_call | solution.py:405
  (44 shorter events, 3.5 us)
Async XLA Ops:
  0.6 11.4 %copy-start = (bf16[512,128]{1,0:T(8,128)(2,1)S(1)}, bf16[512,128]{1,0:T(8,128)(2,1)}, u32[]{:S(2)}) copy-start(bf16[512,128]{1,0:T(8,128)(2,1)} %param.8) | copy-start | bytes 393220
  0.6 17.2 %copy-start.1 = (bf16[512,128]{1,0:T(8,128)(2,1)S(1)}, bf16[512,128]{1,0:T(8,128)(2,1)}, u32[]{:S(2)}) copy-start(bf16[512,128]{1,0:T(8,128)(2,1)} %cotangent.1) | copy-start | bytes 393220
  0.7 8.9 %collective-permute-start.1 = (bf16[4,128,128]{2,1,0:T(8,128)(2,1)}, bf16[4,128,128]{2,1,0:T(8,128)(2,1)S(1)}, u32[]{:S(2)}, u32[]{:S(2)}) collective-permute-start(bf16[4,128,128]{2,1,0:T(8,128)(2,1)} %bitcast.5), channel_id=1, source_target_pairs={{0,24},{1,25},{2,26},{3,27},{4,28},{5,29},{6,30},{7,31},{8,16},{9,... | collective-permute-start | bytes 393224 | tf_op jit(solution)/shard_map/features_1/ppermute | solution.py:80
  5.8 8.3 %collective-permute-start = (bf16[4,128,128]{2,1,0:T(8,128)(2,1)}, bf16[4,128,128]{2,1,0:T(8,128)(2,1)S(1)}, u32[]{:S(2)}, u32[]{:S(2)}) collective-permute-start(bf16[4,128,128]{2,1,0:T(8,128)(2,1)} %bitcast.6), channel_id=1, source_target_pairs={{0,8},{1,5},{2,10},{3,7},{4,12},{5,1},{6,14},{7,3},{8,0},{9,13},{1... | collective-permute-start | bytes 393224 | tf_op jit(solution)/shard_map/features_2/ppermute | solution.py:80
  9.6 6.8 %collective-permute-start.3 = (bf16[4,128,128]{2,1,0:T(8,128)(2,1)S(1)}, bf16[4,128,128]{2,1,0:T(8,128)(2,1)S(1)}, u32[]{:S(2)}, u32[]{:S(2)}) collective-permute-start(bf16[4,128,128]{2,1,0:T(8,128)(2,1)S(1)} %collective-permute-done.1.refs_6_), channel_id=1, source_target_pairs={{0,8},{1,5},{2,10},{3,7},{4,12},{5,1},{6,14},{7,3},{8,0},{9,13},{1... | collective-permute-start | bytes 393224 | tf_op jit(solution)/shard_map/features_3/ppermute | solution.py:80
  12.0 7.3 %collective-permute-start.5 = (bf16[4,128,128]{2,1,0:T(8,128)(2,1)S(1)}, bf16[4,128,128]{2,1,0:T(8,128)(2,1)S(1)}, u32[]{:S(2)}, u32[]{:S(2)}) collective-permute-start(bf16[4,128,128]{2,1,0:T(8,128)(2,1)S(1)} %bitcast.7), channel_id=1, source_target_pairs={{0,4},{1,9},{2,6},{3,11},{4,0},{5,13},{6,2},{7,15},{8,12},{9,1},{1... | collective-permute-start | bytes 393224 | tf_op jit(solution)/shard_map/features_4/ppermute | solution.py:80
  13.5 5.8 %collective-permute-start.6 = (bf16[4,128,128]{2,1,0:T(8,128)(2,1)S(1)}, bf16[4,128,128]{2,1,0:T(8,128)(2,1)S(1)}, u32[]{:S(2)}, u32[]{:S(2)}) collective-permute-start(bf16[4,128,128]{2,1,0:T(8,128)(2,1)S(1)} %collective-permute-done.1.refs_6_), channel_id=1, source_target_pairs={{0,4},{1,9},{2,6},{3,11},{4,0},{5,13},{6,2},{7,15},{8,12},{9,1},{1... | collective-permute-start | bytes 393224 | tf_op jit(solution)/shard_map/features_5/ppermute | solution.py:80
  14.1 7.0 %collective-permute-start.2 = (bf16[4,128,128]{2,1,0:T(8,128)(2,1)S(1)}, bf16[4,128,128]{2,1,0:T(8,128)(2,1)S(1)}, u32[]{:S(2)}, u32[]{:S(2)}) collective-permute-start(bf16[4,128,128]{2,1,0:T(8,128)(2,1)S(1)} %collective-permute-done.refs_4_), channel_id=1, source_target_pairs={{0,4},{1,9},{2,6},{3,11},{4,0},{5,13},{6,2},{7,15},{8,12},{9,1},{1... | collective-permute-start | bytes 393224 | tf_op jit(solution)/shard_map/features_6/ppermute | solution.py:80
  16.3 5.0 %collective-permute-start.4 = (bf16[4,128,128]{2,1,0:T(8,128)(2,1)S(1)}, bf16[4,128,128]{2,1,0:T(8,128)(2,1)S(1)}, u32[]{:S(2)}, u32[]{:S(2)}) collective-permute-start(bf16[4,128,128]{2,1,0:T(8,128)(2,1)S(1)} %collective-permute-done.3.refs_5_), channel_id=1, source_target_pairs={{0,4},{1,9},{2,6},{3,11},{4,0},{5,13},{6,2},{7,15},{8,12},{9,1},{1... | collective-permute-start | bytes 393224 | tf_op jit(solution)/shard_map/features_7/ppermute | solution.py:80
  17.8 5.0 %collective-permute-start.7 = (bf16[512,128]{1,0:T(8,128)(2,1)S(1)}, bf16[512,128]{1,0:T(8,128)(2,1)S(1)}, u32[]{:S(2)}, u32[]{:S(2)}) collective-permute-start(bf16[512,128]{1,0:T(8,128)(2,1)S(1)} %copy-done.1), channel_id=1, source_target_pairs={{0,2},{1,3},{2,0},{3,1},{4,6},{5,7},{6,4},{7,5},{8,10},{9,11},{10,... | collective-permute-start | bytes 393224 | tf_op jit(solution)/shard_map/cotangent/ppermute | solution.py:73
  21.0 9.1 %copy-start.2 = (bf16[128,128]{1,0:T(8,128)(2,1)S(1)}, bf16[128,128]{1,0:T(8,128)(2,1)}, u32[]{:S(2)}) copy-start(bf16[128,128]{1,0:T(8,128)(2,1)} %weight.3) | copy-start | bytes 98308
  21.0 9.1 %copy-start.3 = (f32[128]{0:T(128)S(1)}, f32[128]{0:T(128)}, u32[]{:S(2)}) copy-start(f32[128]{0:T(128)} %param.10) | copy-start | bytes 1540
  22.2 1.4 %collective-permute-start.8 = (bf16[4,128,128]{2,1,0:T(8,128)(2,1)S(1)}, bf16[4,128,128]{2,1,0:T(8,128)(2,1)S(1)}, u32[]{:S(2)}, u32[]{:S(2)}) collective-permute-start(bf16[4,128,128]{2,1,0:T(8,128)(2,1)S(1)} %get-tuple-element.57), channel_id=1, source_target_pairs={{0,1},{1,0},{2,3},{3,2},{4,5},{5,4},{6,7},{7,6},{8,9},{9,8},{10,11... | collective-permute-start | bytes 393224 | tf_op jit(solution)/shard_map/aggregate_1/ppermute | solution.py:73
  22.8 2.5 %collective-permute-start.9 = (bf16[4,128,128]{2,1,0:T(8,128)(2,1)S(1)}, bf16[4,128,128]{2,1,0:T(8,128)(2,1)S(1)}, u32[]{:S(2)}, u32[]{:S(2)}) collective-permute-start(bf16[4,128,128]{2,1,0:T(8,128)(2,1)S(1)} %get-tuple-element.59), channel_id=1, source_target_pairs={{0,1},{1,0},{2,3},{3,2},{4,5},{5,4},{6,7},{7,6},{8,9},{9,8},{10,11... | collective-permute-start | bytes 393224 | tf_op jit(solution)/shard_map/aggregate_3/ppermute | solution.py:73
  23.7 6.4 %collective-permute-start.11 = (bf16[4,128,128]{2,1,0:T(8,128)(2,1)S(1)}, bf16[4,128,128]{2,1,0:T(8,128)(2,1)S(1)}, u32[]{:S(2)}, u32[]{:S(2)}) collective-permute-start(bf16[4,128,128]{2,1,0:T(8,128)(2,1)S(1)} %add_convert_fusion.4.mine), channel_id=1, source_target_pairs={{0,2},{1,3},{2,0},{3,1},{4,6},{5,7},{6,4},{7,5},{8,10},{9,11},{10,... | collective-permute-start | bytes 393224 | tf_op jit(solution)/shard_map/swap/ppermute | solution.py:73
  25.3 6.8 %collective-permute-start.10 = (bf16[4,128,128]{2,1,0:T(8,128)(2,1)S(1)}, bf16[4,128,128]{2,1,0:T(8,128)(2,1)S(1)}, u32[]{:S(2)}, u32[]{:S(2)}) collective-permute-start(bf16[4,128,128]{2,1,0:T(8,128)(2,1)S(1)} %add_convert_fusion.3.mine), channel_id=1, source_target_pairs={{0,2},{1,3},{2,0},{3,1},{4,6},{5,7},{6,4},{7,5},{8,10},{9,11},{10,... | collective-permute-start | bytes 393224 | tf_op jit(solution)/shard_map/swap/ppermute | solution.py:73
  30.6 2.7 %collective-permute-start.14 = (bf16[4,128,128]{2,1,0:T(8,128)(2,1)S(1)}, bf16[4,128,128]{2,1,0:T(8,128)(2,1)S(1)}, u32[]{:S(2)}, u32[]{:S(2)}) collective-permute-start(bf16[4,128,128]{2,1,0:T(8,128)(2,1)S(1)} %get-tuple-element.64.refs_4_), channel_id=1, source_target_pairs={{0,1},{1,0},{2,3},{3,2},{4,5},{5,4},{6,7},{7,6},{8,9},{9,8},{10,11... | collective-permute-start | bytes 393224 | tf_op jit(solution)/shard_map/rows_3/ppermute | solution.py:73
  32.6 1.4 %collective-permute-start.13 = (bf16[4,128,128]{2,1,0:T(8,128)(2,1)S(1)}, bf16[4,128,128]{2,1,0:T(8,128)(2,1)S(1)}, u32[]{:S(2)}, u32[]{:S(2)}) collective-permute-start(bf16[4,128,128]{2,1,0:T(8,128)(2,1)S(1)} %get-tuple-element.63.refs_2_), channel_id=1, source_target_pairs={{0,1},{1,0},{2,3},{3,2},{4,5},{5,4},{6,7},{7,6},{8,9},{9,8},{10,11... | collective-permute-start | bytes 393224 | tf_op jit(solution)/shard_map/rows_1/ppermute | solution.py:73
  32.7 4.6 %collective-permute-start.12 = (f32[144,128]{1,0:T(8,128)S(1)}, f32[144,128]{1,0:T(8,128)S(1)}, u32[]{:S(2)}, u32[]{:S(2)}) collective-permute-start(f32[144,128]{1,0:T(8,128)S(1)} %add.32), channel_id=1, source_target_pairs={{0,1},{1,0},{2,3},{3,2},{4,5},{5,4},{6,7},{7,6},{8,9},{9,8},{10,11... | collective-permute-start | bytes 221192 | tf_op jit(solution)/shard_map/swap/ppermute | solution.py:73
  35.0 8.1 %collective-permute-start.16 = (bf16[4,128,128]{2,1,0:T(8,128)(2,1)S(1)}, bf16[4,128,128]{2,1,0:T(8,128)(2,1)S(1)}, u32[]{:S(2)}, u32[]{:S(2)}) collective-permute-start(bf16[4,128,128]{2,1,0:T(8,128)(2,1)S(1)} %shard_map.116), channel_id=1, source_target_pairs={{0,4},{1,5},{2,6},{3,7},{4,0},{5,1},{6,2},{7,3},{8,12},{9,13},{10,... | collective-permute-start | bytes 393224 | tf_op jit(solution)/shard_map/sums_7/ppermute | solution.py:80
  37.3 8.0 %collective-permute-start.15 = (bf16[144,128]{1,0:T(8,128)(2,1)S(1)}, bf16[144,128]{1,0:T(8,128)(2,1)S(1)}, u32[]{:S(2)}, u32[]{:S(2)}) collective-permute-start(bf16[144,128]{1,0:T(8,128)(2,1)S(1)} %add_convert_fusion.7), channel_id=1, source_target_pairs={{0,8},{1,9},{2,10},{3,11},{4,12},{5,13},{6,14},{7,15},{8,0},{9,1},... | collective-permute-start | bytes 110600 | tf_op jit(solution)/shard_map/gradients_1/ppermute | solution.py:80
  41.0 8.5 %collective-permute-start.19 = (bf16[4,128,128]{2,1,0:T(8,128)(2,1)S(1)}, bf16[4,128,128]{2,1,0:T(8,128)(2,1)S(1)}, u32[]{:S(2)}, u32[]{:S(2)}) collective-permute-start(bf16[4,128,128]{2,1,0:T(8,128)(2,1)S(1)} %get-tuple-element.70), channel_id=1, source_target_pairs={{0,4},{1,5},{2,6},{3,7},{4,0},{5,1},{6,2},{7,3},{8,12},{9,13},{10,... | collective-permute-start | bytes 393224 | tf_op jit(solution)/shard_map/sums_5/ppermute | solution.py:80
  43.2 6.3 %collective-permute-start.20 = (bf16[4,128,128]{2,1,0:T(8,128)(2,1)S(1)}, bf16[4,128,128]{2,1,0:T(8,128)(2,1)S(1)}, u32[]{:S(2)}, u32[]{:S(2)}) collective-permute-start(bf16[4,128,128]{2,1,0:T(8,128)(2,1)S(1)} %add_convert_fusion.2), channel_id=1, source_target_pairs={{0,8},{1,9},{2,10},{3,11},{4,12},{5,13},{6,14},{7,15},{8,0},{9,1},... | collective-permute-start | bytes 393224 | tf_op jit(solution)/shard_map/sums_3/ppermute | solution.py:80
  43.3 7.1 %collective-permute-start.18 = (bf16[4,128,128]{2,1,0:T(8,128)(2,1)S(1)}, bf16[4,128,128]{2,1,0:T(8,128)(2,1)S(1)}, u32[]{:S(2)}, u32[]{:S(2)}) collective-permute-start(bf16[4,128,128]{2,1,0:T(8,128)(2,1)S(1)} %get-tuple-element.72), channel_id=1, source_target_pairs={{0,4},{1,5},{2,6},{3,7},{4,0},{5,1},{6,2},{7,3},{8,12},{9,13},{10,... | collective-permute-start | bytes 393224 | tf_op jit(solution)/shard_map/sums_6/ppermute | solution.py:80
  44.9 8.7 %collective-permute-start.22 = (bf16[4,128,128]{2,1,0:T(8,128)(2,1)S(1)}, bf16[4,128,128]{2,1,0:T(8,128)(2,1)S(1)}, u32[]{:S(2)}, u32[]{:S(2)}) collective-permute-start(bf16[4,128,128]{2,1,0:T(8,128)(2,1)S(1)} %get-tuple-element.73), channel_id=1, source_target_pairs={{0,4},{1,5},{2,6},{3,7},{4,0},{5,1},{6,2},{7,3},{8,12},{9,13},{10,... | collective-permute-start | bytes 393224 | tf_op jit(solution)/shard_map/sums_4/ppermute | solution.py:80
  45.4 6.3 %collective-permute-start.17 = (bf16[144,128]{1,0:T(8,128)(2,1)S(1)}, bf16[144,128]{1,0:T(8,128)(2,1)S(1)}, u32[]{:S(2)}, u32[]{:S(2)}) collective-permute-start(bf16[144,128]{1,0:T(8,128)(2,1)S(1)} %add_convert_fusion.6), channel_id=1, source_target_pairs={{0,24},{1,25},{2,26},{3,27},{4,28},{5,29},{6,30},{7,31},{8,16},{9,... | collective-permute-start | bytes 110600 | tf_op jit(solution)/shard_map/gradients_0/ppermute | solution.py:80
  49.5 8.5 %collective-permute-start.23 = (bf16[4,128,128]{2,1,0:T(8,128)(2,1)S(1)}, bf16[4,128,128]{2,1,0:T(8,128)(2,1)S(1)}, u32[]{:S(2)}, u32[]{:S(2)}) collective-permute-start(bf16[4,128,128]{2,1,0:T(8,128)(2,1)S(1)} %add_convert_fusion), channel_id=1, source_target_pairs={{0,24},{1,25},{2,26},{3,27},{4,28},{5,29},{6,30},{7,31},{8,16},{9,... | collective-permute-start | bytes 393224 | tf_op jit(solution)/shard_map/sums_1/ppermute | solution.py:80
  50.5 7.6 %collective-permute-start.24 = (bf16[4,128,128]{2,1,0:T(8,128)(2,1)S(1)}, bf16[4,128,128]{2,1,0:T(8,128)(2,1)S(1)}, u32[]{:S(2)}, u32[]{:S(2)}) collective-permute-start(bf16[4,128,128]{2,1,0:T(8,128)(2,1)S(1)} %add_convert_fusion.1), channel_id=1, source_target_pairs={{0,8},{1,9},{2,10},{3,11},{4,12},{5,13},{6,14},{7,15},{8,0},{9,1},... | collective-permute-start | bytes 393224 | tf_op jit(solution)/shard_map/sums_2/ppermute | solution.py:80
  51.7 4.0 %collective-permute-start.21 = (bf16[144,128]{1,0:T(8,128)(2,1)S(1)}, bf16[144,128]{1,0:T(8,128)(2,1)S(1)}, u32[]{:S(2)}, u32[]{:S(2)}) collective-permute-start(bf16[144,128]{1,0:T(8,128)(2,1)S(1)} %add_convert_fusion.5.refs_0_), channel_id=1, source_target_pairs={{0,4},{1,5},{2,6},{3,7},{4,0},{5,1},{6,2},{7,3},{8,12},{9,13},{10,... | collective-permute-start | bytes 110600 | tf_op jit(solution)/shard_map/gradients_2/ppermute | solution.py:80

commit v7 on v5

--- a/solution.py
+++ b/solution.py
@@ -427,7 +427,8 @@
         pieces[code] = row_swap(queue.tie(pieces[parent]), there[step], f"features_{code}")
         if code == 1:
             pieces[code] = after(pieces[code], table)
-    other_cotangent = swap(queue.tie(cotangent), "col", across, "cotangent")
+        if code == 1 << len(outer_steps) - 1:
+            other_cotangent = swap(queue.tie(cotangent), "col", across, "cotangent")
     early = {offset_of(c, there): p for c, p in pieces.items() if c not in late_codes}
     late = {offset_of(c, there): p for c, p in pieces.items() if c in late_codes}
     total = sparse(FORWARD_EARLY, bits, table, held, early, "row", "col", column_blocks, row_blocks)

time: 58.6 us -> 58.5 us (level)
  starting transfers between devices: 26.7 us -> 30.2 us
  Pallas kernels: 13.5 us -> 11.1 us
  waiting for transfers between devices: 15 us -> 13.8 us
    ppermute x17, starting transfers between devices: 21.8 us -> 25.3 us  [row_swap(): return lax.ppermute(x, ('row', 'col'), pairs)]
    pallas_call x4, Pallas kernels: 8.71 us -> 6.36 us  [sparse(): pl.pallas_call(partial(sparse_kernel, which, bits, tuple(offsets), here,...]
    ppermute x17, waiting for transfers between devices: 7.73 us -> 6.62 us  [row_swap(): return lax.ppermute(x, ('row', 'col'), pairs)]
  transfers between devices with their start and end apart: 25 -> 25, of which waited for: 11 -> 11; matrix products, arithmetic and copies ran while one was open for 3% -> 3% of each run, Pallas kernels for 22% -> 18%
where the time goes in v7:
time: 58.5 us; the launch traced here: 58.4 us
  starting transfers between devices  30.2 us (52%)
  waiting for transfers between devices  13.8 us (24%)
  Pallas kernels  11.1 us (19%)
  between operations  1.48 us (3%)
  other arithmetic  1 us (2%)
  local copies, waits for them, and re-layouts  0.68 us (1%)
    ppermute x17, starting transfers between devices, row_swap(): return lax.ppermute(x, ('row', 'col'), pairs)  25.3 us
    ppermute x8, waiting for transfers between devices, swap(): return lax.ppermute(x, axis, [(i, i ^ mask) for i in range(size)])  7.22 us
    ppermute x17, waiting for transfers between devices, row_swap(): return lax.ppermute(x, ('row', 'col'), pairs)  6.62 us
    pallas_call x4, Pallas kernels, sparse(): pl.pallas_call(partial(sparse_kernel, which, bits, tuple(offsets), here,...  6.36 us
    ppermute x8, starting transfers between devices, swap(): return lax.ppermute(x, axis, [(i, i ^ mask) for i in range(size)])  4.94 us
    pallas_call x1, Pallas kernels, prep(): pl.pallas_call(partial(prep_kernel, per, bits, late, first), out_shape=[j...  2.88 us
  transfers between devices with their start and end apart: 25, of which 11 were waited for; matrix products, arithmetic and copies ran while one was open for 3% of the time, Pallas kernels for 18%

profile of v7, /device:TPU:0, one launch (start us, length us, event | category | flops | bytes accessed | tf_op | source)
XLA Modules:
  0.0 58.4 jit_solution(12839842663577412931)
XLA Ops:
  0.7 5.1 %collective-permute-start.1 = (bf16[4,128,128]{2,1,0:T(8,128)(2,1)}, bf16[4,128,128]{2,1,0:T(8,128)(2,1)S(1)}, u32[]{:S(2)}, u32[]{:S(2)}) collective-permute-start(bf16[4,128,128]{2,1,0:T(8,128)(2,1)} %bitcast.6), channel_id=1, source_target_pairs={{0,24},{1,25},{2,26},{3,27},{4,28},{5,29},{6,30},{7,31},{8,16},{9,... | collective-permute-start | bytes 393224 | tf_op jit(solution)/shard_map/features_1/ppermute | solution.py:80
  6.4 0.7 %pad_add_fusion = s32[161,1]{0,1:T(1,128)S(1)} fusion(s32[1,1]{0,1:T(1,128)} %bitcast.5, s32[80,1]{0,1:T(1,128)} %param.13, s32[80,1]{0,1:T(1,128)} %param.12), kind=kLoop, calls=%fused_computation.8 | loop fusion | flops 322 | bytes 1288 | tf_op jit(solution)/shard_map/concatenate | solution.py:421
  7.2 2.9 %shard_map.111 = (s32[168]{0:T(256)S(1)}, bf16[80,128,128]{2,1,0:T(8,128)(2,1)S(1)}) custom-call(s32[161]{0:T(256)S(1)} %bitcast.10, bf16[80,128,128]{2,1,0:T(8,128)(2,1)} %blocks.1), custom_call_target="tpu_custom_call" | custom-call | flops 1 | bytes 1 | tf_op jit(solution)/shard_map/pallas_call | solution.py:190
  10.1 2.1 %collective-permute-start.3 = (bf16[4,128,128]{2,1,0:T(8,128)(2,1)S(1)}, bf16[4,128,128]{2,1,0:T(8,128)(2,1)S(1)}, u32[]{:S(2)}, u32[]{:S(2)}) collective-permute-start(bf16[4,128,128]{2,1,0:T(8,128)(2,1)S(1)} %collective-permute-done.1.refs_6_), channel_id=1, source_target_pairs={{0,8},{1,5},{2,10},{3,7},{4,12},{5,1},{6,14},{7,3},{8,0},{9,13},{1... | collective-permute-start | bytes 393224 | tf_op jit(solution)/shard_map/features_3/ppermute | solution.py:80
  12.2 1.5 %collective-permute-start.5 = (bf16[4,128,128]{2,1,0:T(8,128)(2,1)S(1)}, bf16[4,128,128]{2,1,0:T(8,128)(2,1)S(1)}, u32[]{:S(2)}, u32[]{:S(2)}) collective-permute-start(bf16[4,128,128]{2,1,0:T(8,128)(2,1)S(1)} %bitcast.8), channel_id=1, source_target_pairs={{0,4},{1,9},{2,6},{3,11},{4,0},{5,13},{6,2},{7,15},{8,12},{9,1},{1... | collective-permute-start | bytes 393224 | tf_op jit(solution)/shard_map/features_4/ppermute | solution.py:80
  14.2 1.5 %collective-permute-start.2 = (bf16[4,128,128]{2,1,0:T(8,128)(2,1)S(1)}, bf16[4,128,128]{2,1,0:T(8,128)(2,1)S(1)}, u32[]{:S(2)}, u32[]{:S(2)}) collective-permute-start(bf16[4,128,128]{2,1,0:T(8,128)(2,1)S(1)} %collective-permute-done.refs_4_), channel_id=1, source_target_pairs={{0,4},{1,9},{2,6},{3,11},{4,0},{5,13},{6,2},{7,15},{8,12},{9,1},{1... | collective-permute-start | bytes 393224 | tf_op jit(solution)/shard_map/features_6/ppermute | solution.py:80
  15.7 0.8 %collective-permute-done.3.refs_5_ = bf16[4,128,128]{2,1,0:T(8,128)(2,1)S(1)} collective-permute-done((bf16[4,128,128]{2,1,0:T(8,128)(2,1)S(1)}, bf16[4,128,128]{2,1,0:T(8,128)(2,1)S(1)}, u32[]{:S(2)}, u32[]{:S(2)}) %collective-permute-start.3) | collective-permute-done | bytes 131104 | tf_op jit(solution)/shard_map/features_3/ppermute | solution.py:80
  16.5 1.5 %collective-permute-start.4 = (bf16[4,128,128]{2,1,0:T(8,128)(2,1)S(1)}, bf16[4,128,128]{2,1,0:T(8,128)(2,1)S(1)}, u32[]{:S(2)}, u32[]{:S(2)}) collective-permute-start(bf16[4,128,128]{2,1,0:T(8,128)(2,1)S(1)} %collective-permute-done.3.refs_5_), channel_id=1, source_target_pairs={{0,4},{1,9},{2,6},{3,11},{4,0},{5,13},{6,2},{7,15},{8,12},{9,1},{1... | collective-permute-start | bytes 393224 | tf_op jit(solution)/shard_map/features_7/ppermute | solution.py:80
  18.0 1.5 %collective-permute-start.7 = (bf16[512,128]{1,0:T(8,128)(2,1)S(1)}, bf16[512,128]{1,0:T(8,128)(2,1)S(1)}, u32[]{:S(2)}, u32[]{:S(2)}) collective-permute-start(bf16[512,128]{1,0:T(8,128)(2,1)S(1)} %copy-done.1), channel_id=1, source_target_pairs={{0,2},{1,3},{2,0},{3,1},{4,6},{5,7},{6,4},{7,5},{8,10},{9,11},{10,... | collective-permute-start | bytes 393224 | tf_op jit(solution)/shard_map/cotangent/ppermute | solution.py:73
  19.5 2.1 %shard_map.112.refs_4_ = f32[17,128,128]{2,1,0:T(8,128)S(1)} custom-call(s32[168]{0:T(256)S(1)} %get-tuple-element.45.refs_0_, bf16[80,128,128]{2,1,0:T(8,128)(2,1)S(1)} %get-tuple-element.46.refs_1_, bf16[4,128,128]{2,1,0:T(8,128)(2,1)S(1)} %bitcast.9, bf16[4,128,128]{2,1,0:T(8,128)(2,1)S(1)} %collective-permute-done.5.refs_3_, ...), custom_call_target="tpu_custom_call" | custom-call | flops 1 | bytes 1 | tf_op jit(solution)/shard_map/pallas_call | solution.py:300
  21.7 1.1 %shard_map.113 = (f32[4,128,128]{2,1,0:T(8,128)S(1)}, bf16[4,128,128]{2,1,0:T(8,128)(2,1)S(1)}, f32[4,128,128]{2,1,0:T(8,128)S(1)}, bf16[4,128,128]{2,1,0:T(8,128)(2,1)S(1)}) custom-call(s32[168]{0:T(256)S(1)} %get-tuple-element.45.refs_0_, bf16[80,128,128]{2,1,0:T(8,128)(2,1)S(1)} %get-tuple-element.46.refs_1_, ...), custom_call_target="tpu_custom_call" | custom-call | flops 1 | bytes 1 | tf_op jit(solution)/shard_map/pallas_call | solution.py:300
  23.4 0.8 %collective-permute-done.8 = bf16[4,128,128]{2,1,0:T(8,128)(2,1)S(1)} collective-permute-done((bf16[4,128,128]{2,1,0:T(8,128)(2,1)S(1)}, bf16[4,128,128]{2,1,0:T(8,128)(2,1)S(1)}, u32[]{:S(2)}, u32[]{:S(2)}) %collective-permute-start.8) | collective-permute-done | bytes 131104 | tf_op jit(solution)/shard_map/aggregate_1/ppermute | solution.py:73
  24.3 1.1 %collective-permute-start.11 = (bf16[4,128,128]{2,1,0:T(8,128)(2,1)S(1)}, bf16[4,128,128]{2,1,0:T(8,128)(2,1)S(1)}, u32[]{:S(2)}, u32[]{:S(2)}) collective-permute-start(bf16[4,128,128]{2,1,0:T(8,128)(2,1)S(1)} %add_convert_fusion.4.mine), channel_id=1, source_target_pairs={{0,2},{1,3},{2,0},{3,1},{4,6},{5,7},{6,4},{7,5},{8,10},{9,11},{10,... | collective-permute-start | bytes 393224 | tf_op jit(solution)/shard_map/swap/ppermute | solution.py:73
  25.4 1.1 %collective-permute-start.10 = (bf16[4,128,128]{2,1,0:T(8,128)(2,1)S(1)}, bf16[4,128,128]{2,1,0:T(8,128)(2,1)S(1)}, u32[]{:S(2)}, u32[]{:S(2)}) collective-permute-start(bf16[4,128,128]{2,1,0:T(8,128)(2,1)S(1)} %add_convert_fusion.3.mine), channel_id=1, source_target_pairs={{0,2},{1,3},{2,0},{3,1},{4,6},{5,7},{6,4},{7,5},{8,10},{9,11},{10,... | collective-permute-start | bytes 393224 | tf_op jit(solution)/shard_map/swap/ppermute | solution.py:73
  26.4 4.2 %collective-permute-done.11.theirs = bf16[4,128,128]{2,1,0:T(8,128)(2,1)S(1)} collective-permute-done((bf16[4,128,128]{2,1,0:T(8,128)(2,1)S(1)}, bf16[4,128,128]{2,1,0:T(8,128)(2,1)S(1)}, u32[]{:S(2)}, u32[]{:S(2)}) %collective-permute-start.11) | collective-permute-done | bytes 131104 | tf_op jit(solution)/shard_map/swap/ppermute | solution.py:73
  31.3 1.4 %collective-permute-done.10.theirs = bf16[4,128,128]{2,1,0:T(8,128)(2,1)S(1)} collective-permute-done((bf16[4,128,128]{2,1,0:T(8,128)(2,1)S(1)}, bf16[4,128,128]{2,1,0:T(8,128)(2,1)S(1)}, u32[]{:S(2)}, u32[]{:S(2)}) %collective-permute-start.10) | collective-permute-done | bytes 131104 | tf_op jit(solution)/shard_map/swap/ppermute | solution.py:73
  33.9 0.8 %collective-permute-done.13.refs_3_ = bf16[4,128,128]{2,1,0:T(8,128)(2,1)S(1)} collective-permute-done((bf16[4,128,128]{2,1,0:T(8,128)(2,1)S(1)}, bf16[4,128,128]{2,1,0:T(8,128)(2,1)S(1)}, u32[]{:S(2)}, u32[]{:S(2)}) %collective-permute-start.13) | collective-permute-done | bytes 131104 | tf_op jit(solution)/shard_map/rows_1/ppermute | solution.py:73
  34.6 1.0 %shard_map.116 = bf16[4,128,128]{2,1,0:T(8,128)(2,1)S(1)} custom-call(s32[168]{0:T(256)S(1)} %get-tuple-element.45.refs_0_, bf16[80,128,128]{2,1,0:T(8,128)(2,1)S(1)} %get-tuple-element.46.refs_1_, bf16[4,128,128]{2,1,0:T(8,128)(2,1)S(1)} %get-tuple-element.63.refs_2_, bf16[4,128,128]{2,1,0:T(8,128)(2,1)S(1)} %collective-permute-done.13.refs_3_, ...), custom_call_target="tpu_custom_call" | custom-call | flops 1 | bytes 1 | tf_op jit(solution)/shard_map/pallas_call | solution.py:300
  35.6 2.0 %collective-permute-start.16 = (bf16[4,128,128]{2,1,0:T(8,128)(2,1)S(1)}, bf16[4,128,128]{2,1,0:T(8,128)(2,1)S(1)}, u32[]{:S(2)}, u32[]{:S(2)}) collective-permute-start(bf16[4,128,128]{2,1,0:T(8,128)(2,1)S(1)} %shard_map.116), channel_id=1, source_target_pairs={{0,4},{1,5},{2,6},{3,7},{4,0},{5,1},{6,2},{7,3},{8,12},{9,13},{10,... | collective-permute-start | bytes 393224 | tf_op jit(solution)/shard_map/sums_7/ppermute | solution.py:80
  37.6 1.4 %collective-permute-start.15 = (bf16[144,128]{1,0:T(8,128)(2,1)S(1)}, bf16[144,128]{1,0:T(8,128)(2,1)S(1)}, u32[]{:S(2)}, u32[]{:S(2)}) collective-permute-start(bf16[144,128]{1,0:T(8,128)(2,1)S(1)} %add_convert_fusion.7), channel_id=1, source_target_pairs={{0,8},{1,9},{2,10},{3,11},{4,12},{5,13},{6,14},{7,15},{8,0},{9,1},... | collective-permute-start | bytes 110600 | tf_op jit(solution)/shard_map/gradients_1/ppermute | solution.py:80
  39.0 2.1 %shard_map.117 = (f32[4,128,128]{2,1,0:T(8,128)S(1)}, bf16[4,128,128]{2,1,0:T(8,128)(2,1)S(1)}, bf16[4,128,128]{2,1,0:T(8,128)(2,1)S(1)}, bf16[4,128,128]{2,1,0:...) custom-call(s32[168]{0:T(256)S(1)} %get-tuple-element.45.refs_0_, ...), custom_call_target="tpu_custom_call" | custom-call | flops 1 | bytes 1 | tf_op jit(solution)/shard_map/pallas_call | solution.py:300
  41.2 3.0 %collective-permute-start.19 = (bf16[4,128,128]{2,1,0:T(8,128)(2,1)S(1)}, bf16[4,128,128]{2,1,0:T(8,128)(2,1)S(1)}, u32[]{:S(2)}, u32[]{:S(2)}) collective-permute-start(bf16[4,128,128]{2,1,0:T(8,128)(2,1)S(1)} %get-tuple-element.70), channel_id=1, source_target_pairs={{0,4},{1,5},{2,6},{3,7},{4,0},{5,1},{6,2},{7,3},{8,12},{9,13},{10,... | collective-permute-start | bytes 393224 | tf_op jit(solution)/shard_map/sums_5/ppermute | solution.py:80
  44.6 0.7 %collective-permute-start.18 = (bf16[4,128,128]{2,1,0:T(8,128)(2,1)S(1)}, bf16[4,128,128]{2,1,0:T(8,128)(2,1)S(1)}, u32[]{:S(2)}, u32[]{:S(2)}) collective-permute-start(bf16[4,128,128]{2,1,0:T(8,128)(2,1)S(1)} %get-tuple-element.72), channel_id=1, source_target_pairs={{0,4},{1,5},{2,6},{3,7},{4,0},{5,1},{6,2},{7,3},{8,12},{9,13},{10,... | collective-permute-start | bytes 393224 | tf_op jit(solution)/shard_map/sums_6/ppermute | solution.py:80
  45.2 1.4 %collective-permute-start.22 = (bf16[4,128,128]{2,1,0:T(8,128)(2,1)S(1)}, bf16[4,128,128]{2,1,0:T(8,128)(2,1)S(1)}, u32[]{:S(2)}, u32[]{:S(2)}) collective-permute-start(bf16[4,128,128]{2,1,0:T(8,128)(2,1)S(1)} %get-tuple-element.73), channel_id=1, source_target_pairs={{0,4},{1,5},{2,6},{3,7},{4,0},{5,1},{6,2},{7,3},{8,12},{9,13},{10,... | collective-permute-start | bytes 393224 | tf_op jit(solution)/shard_map/sums_4/ppermute | solution.py:80
  46.6 0.9 %collective-permute-start.17 = (bf16[144,128]{1,0:T(8,128)(2,1)S(1)}, bf16[144,128]{1,0:T(8,128)(2,1)S(1)}, u32[]{:S(2)}, u32[]{:S(2)}) collective-permute-start(bf16[144,128]{1,0:T(8,128)(2,1)S(1)} %add_convert_fusion.6), channel_id=1, source_target_pairs={{0,24},{1,25},{2,26},{3,27},{4,28},{5,29},{6,30},{7,31},{8,16},{9,... | collective-permute-start | bytes 110600 | tf_op jit(solution)/shard_map/gradients_0/ppermute | solution.py:80
  48.1 1.2 %collective-permute-done.20 = bf16[4,128,128]{2,1,0:T(8,128)(2,1)S(1)} collective-permute-done((bf16[4,128,128]{2,1,0:T(8,128)(2,1)S(1)}, bf16[4,128,128]{2,1,0:T(8,128)(2,1)S(1)}, u32[]{:S(2)}, u32[]{:S(2)}) %collective-permute-start.20) | collective-permute-done | bytes 131104 | tf_op jit(solution)/shard_map/sums_3/ppermute | solution.py:80
  49.3 1.4 %collective-permute-start.23 = (bf16[4,128,128]{2,1,0:T(8,128)(2,1)S(1)}, bf16[4,128,128]{2,1,0:T(8,128)(2,1)S(1)}, u32[]{:S(2)}, u32[]{:S(2)}) collective-permute-start(bf16[4,128,128]{2,1,0:T(8,128)(2,1)S(1)} %add_convert_fusion), channel_id=1, source_target_pairs={{0,24},{1,25},{2,26},{3,27},{4,28},{5,29},{6,30},{7,31},{8,16},{9,... | collective-permute-start | bytes 393224 | tf_op jit(solution)/shard_map/sums_1/ppermute | solution.py:80
  51.1 1.3 %collective-permute-start.24 = (bf16[4,128,128]{2,1,0:T(8,128)(2,1)S(1)}, bf16[4,128,128]{2,1,0:T(8,128)(2,1)S(1)}, u32[]{:S(2)}, u32[]{:S(2)}) collective-permute-start(bf16[4,128,128]{2,1,0:T(8,128)(2,1)S(1)} %add_convert_fusion.1), channel_id=1, source_target_pairs={{0,8},{1,9},{2,10},{3,11},{4,12},{5,13},{6,14},{7,15},{8,0},{9,1},... | collective-permute-start | bytes 393224 | tf_op jit(solution)/shard_map/sums_2/ppermute | solution.py:80
  53.0 0.7 %collective-permute-start.21 = (bf16[144,128]{1,0:T(8,128)(2,1)S(1)}, bf16[144,128]{1,0:T(8,128)(2,1)S(1)}, u32[]{:S(2)}, u32[]{:S(2)}) collective-permute-start(bf16[144,128]{1,0:T(8,128)(2,1)S(1)} %add_convert_fusion.5.refs_0_), channel_id=1, source_target_pairs={{0,4},{1,5},{2,6},{3,7},{4,0},{5,1},{6,2},{7,3},{8,12},{9,13},{10,... | collective-permute-start | bytes 110600 | tf_op jit(solution)/shard_map/gradients_2/ppermute | solution.py:80
  53.8 0.7 %copy.13 = bf16[512,128]{1,0:T(8,128)(2,1)} copy(bf16[512,128]{1,0:T(8,128)(2,1)S(1)} %get-tuple-element.86) | data formatting | bytes 262144
  54.4 2.6 %collective-permute-done.21.refs_1_ = bf16[144,128]{1,0:T(8,128)(2,1)S(1)} collective-permute-done((bf16[144,128]{1,0:T(8,128)(2,1)S(1)}, bf16[144,128]{1,0:T(8,128)(2,1)S(1)}, u32[]{:S(2)}, u32[]{:S(2)}) %collective-permute-start.21) | collective-permute-done | bytes 36896 | tf_op jit(solution)/shard_map/gradients_2/ppermute | solution.py:80
  57.5 0.9 %shard_map.118 = (f32[512,128]{1,0:T(8,128)}, f32[128,128]{1,0:T(8,128)}, f32[1,128]{1,0:T(1,128)}) custom-call(bf16[144,128]{1,0:T(8,128)(2,1)S(1)} %add_convert_fusion.5.refs_0_, bf16[144,128]{1,0:T(8,128)(2,1)S(1)} %collective-permute-done.21.refs_1_, f32[4,128,128]{2,1,0:T(8,128)S(1)} %get-tuple-element.82.refs_2_, ...), custom_call_target="tpu_custom_call" | custom-call | flops 1 | bytes 1 | tf_op jit(solution)/shard_map/pallas_call | solution.py:387
  (45 shorter events, 5.5 us)
Async XLA Ops:
  0.6 11.5 %copy-start = (bf16[512,128]{1,0:T(8,128)(2,1)S(1)}, bf16[512,128]{1,0:T(8,128)(2,1)}, u32[]{:S(2)}) copy-start(bf16[512,128]{1,0:T(8,128)(2,1)} %param.8) | copy-start | bytes 393220
  0.6 17.3 %copy-start.1 = (bf16[512,128]{1,0:T(8,128)(2,1)S(1)}, bf16[512,128]{1,0:T(8,128)(2,1)}, u32[]{:S(2)}) copy-start(bf16[512,128]{1,0:T(8,128)(2,1)} %cotangent.1) | copy-start | bytes 393220
  0.7 9.4 %collective-permute-start.1 = (bf16[4,128,128]{2,1,0:T(8,128)(2,1)}, bf16[4,128,128]{2,1,0:T(8,128)(2,1)S(1)}, u32[]{:S(2)}, u32[]{:S(2)}) collective-permute-start(bf16[4,128,128]{2,1,0:T(8,128)(2,1)} %bitcast.6), channel_id=1, source_target_pairs={{0,24},{1,25},{2,26},{3,27},{4,28},{5,29},{6,30},{7,31},{8,16},{9,... | collective-permute-start | bytes 393224 | tf_op jit(solution)/shard_map/features_1/ppermute | solution.py:80
  5.8 8.4 %collective-permute-start = (bf16[4,128,128]{2,1,0:T(8,128)(2,1)}, bf16[4,128,128]{2,1,0:T(8,128)(2,1)S(1)}, u32[]{:S(2)}, u32[]{:S(2)}) collective-permute-start(bf16[4,128,128]{2,1,0:T(8,128)(2,1)} %bitcast.7), channel_id=1, source_target_pairs={{0,8},{1,5},{2,10},{3,7},{4,12},{5,1},{6,14},{7,3},{8,0},{9,13},{1... | collective-permute-start | bytes 393224 | tf_op jit(solution)/shard_map/features_2/ppermute | solution.py:80
  10.1 6.4 %collective-permute-start.3 = (bf16[4,128,128]{2,1,0:T(8,128)(2,1)S(1)}, bf16[4,128,128]{2,1,0:T(8,128)(2,1)S(1)}, u32[]{:S(2)}, u32[]{:S(2)}) collective-permute-start(bf16[4,128,128]{2,1,0:T(8,128)(2,1)S(1)} %collective-permute-done.1.refs_6_), channel_id=1, source_target_pairs={{0,8},{1,5},{2,10},{3,7},{4,12},{5,1},{6,14},{7,3},{8,0},{9,13},{1... | collective-permute-start | bytes 393224 | tf_op jit(solution)/shard_map/features_3/ppermute | solution.py:80
  12.2 7.3 %collective-permute-start.5 = (bf16[4,128,128]{2,1,0:T(8,128)(2,1)S(1)}, bf16[4,128,128]{2,1,0:T(8,128)(2,1)S(1)}, u32[]{:S(2)}, u32[]{:S(2)}) collective-permute-start(bf16[4,128,128]{2,1,0:T(8,128)(2,1)S(1)} %bitcast.8), channel_id=1, source_target_pairs={{0,4},{1,9},{2,6},{3,11},{4,0},{5,13},{6,2},{7,15},{8,12},{9,1},{1... | collective-permute-start | bytes 393224 | tf_op jit(solution)/shard_map/features_4/ppermute | solution.py:80
  13.6 5.8 %collective-permute-start.6 = (bf16[4,128,128]{2,1,0:T(8,128)(2,1)S(1)}, bf16[4,128,128]{2,1,0:T(8,128)(2,1)S(1)}, u32[]{:S(2)}, u32[]{:S(2)}) collective-permute-start(bf16[4,128,128]{2,1,0:T(8,128)(2,1)S(1)} %collective-permute-done.1.refs_6_), channel_id=1, source_target_pairs={{0,4},{1,9},{2,6},{3,11},{4,0},{5,13},{6,2},{7,15},{8,12},{9,1},{1... | collective-permute-start | bytes 393224 | tf_op jit(solution)/shard_map/features_5/ppermute | solution.py:80
  14.2 7.5 %collective-permute-start.2 = (bf16[4,128,128]{2,1,0:T(8,128)(2,1)S(1)}, bf16[4,128,128]{2,1,0:T(8,128)(2,1)S(1)}, u32[]{:S(2)}, u32[]{:S(2)}) collective-permute-start(bf16[4,128,128]{2,1,0:T(8,128)(2,1)S(1)} %collective-permute-done.refs_4_), channel_id=1, source_target_pairs={{0,4},{1,9},{2,6},{3,11},{4,0},{5,13},{6,2},{7,15},{8,12},{9,1},{1... | collective-permute-start | bytes 393224 | tf_op jit(solution)/shard_map/features_6/ppermute | solution.py:80
  16.5 5.2 %collective-permute-start.4 = (bf16[4,128,128]{2,1,0:T(8,128)(2,1)S(1)}, bf16[4,128,128]{2,1,0:T(8,128)(2,1)S(1)}, u32[]{:S(2)}, u32[]{:S(2)}) collective-permute-start(bf16[4,128,128]{2,1,0:T(8,128)(2,1)S(1)} %collective-permute-done.3.refs_5_), channel_id=1, source_target_pairs={{0,4},{1,9},{2,6},{3,11},{4,0},{5,13},{6,2},{7,15},{8,12},{9,1},{1... | collective-permute-start | bytes 393224 | tf_op jit(solution)/shard_map/features_7/ppermute | solution.py:80
  18.0 5.4 %collective-permute-start.7 = (bf16[512,128]{1,0:T(8,128)(2,1)S(1)}, bf16[512,128]{1,0:T(8,128)(2,1)S(1)}, u32[]{:S(2)}, u32[]{:S(2)}) collective-permute-start(bf16[512,128]{1,0:T(8,128)(2,1)S(1)} %copy-done.1), channel_id=1, source_target_pairs={{0,2},{1,3},{2,0},{3,1},{4,6},{5,7},{6,4},{7,5},{8,10},{9,11},{10,... | collective-permute-start | bytes 393224 | tf_op jit(solution)/shard_map/cotangent/ppermute | solution.py:73
  21.6 9.0 %copy-start.2 = (bf16[128,128]{1,0:T(8,128)(2,1)S(1)}, bf16[128,128]{1,0:T(8,128)(2,1)}, u32[]{:S(2)}) copy-start(bf16[128,128]{1,0:T(8,128)(2,1)} %weight.3) | copy-start | bytes 98308
  21.6 9.0 %copy-start.3 = (f32[128]{0:T(128)S(1)}, f32[128]{0:T(128)}, u32[]{:S(2)}) copy-start(f32[128]{0:T(128)} %param.10) | copy-start | bytes 1540
  22.8 1.4 %collective-permute-start.8 = (bf16[4,128,128]{2,1,0:T(8,128)(2,1)S(1)}, bf16[4,128,128]{2,1,0:T(8,128)(2,1)S(1)}, u32[]{:S(2)}, u32[]{:S(2)}) collective-permute-start(bf16[4,128,128]{2,1,0:T(8,128)(2,1)S(1)} %get-tuple-element.57), channel_id=1, source_target_pairs={{0,1},{1,0},{2,3},{3,2},{4,5},{5,4},{6,7},{7,6},{8,9},{9,8},{10,11... | collective-permute-start | bytes 393224 | tf_op jit(solution)/shard_map/aggregate_1/ppermute | solution.py:73
  22.9 2.5 %collective-permute-start.9 = (bf16[4,128,128]{2,1,0:T(8,128)(2,1)S(1)}, bf16[4,128,128]{2,1,0:T(8,128)(2,1)S(1)}, u32[]{:S(2)}, u32[]{:S(2)}) collective-permute-start(bf16[4,128,128]{2,1,0:T(8,128)(2,1)S(1)} %get-tuple-element.59), channel_id=1, source_target_pairs={{0,1},{1,0},{2,3},{3,2},{4,5},{5,4},{6,7},{7,6},{8,9},{9,8},{10,11... | collective-permute-start | bytes 393224 | tf_op jit(solution)/shard_map/aggregate_3/ppermute | solution.py:73
  24.3 6.4 %collective-permute-start.11 = (bf16[4,128,128]{2,1,0:T(8,128)(2,1)S(1)}, bf16[4,128,128]{2,1,0:T(8,128)(2,1)S(1)}, u32[]{:S(2)}, u32[]{:S(2)}) collective-permute-start(bf16[4,128,128]{2,1,0:T(8,128)(2,1)S(1)} %add_convert_fusion.4.mine), channel_id=1, source_target_pairs={{0,2},{1,3},{2,0},{3,1},{4,6},{5,7},{6,4},{7,5},{8,10},{9,11},{10,... | collective-permute-start | bytes 393224 | tf_op jit(solution)/shard_map/swap/ppermute | solution.py:73
  25.4 7.3 %collective-permute-start.10 = (bf16[4,128,128]{2,1,0:T(8,128)(2,1)S(1)}, bf16[4,128,128]{2,1,0:T(8,128)(2,1)S(1)}, u32[]{:S(2)}, u32[]{:S(2)}) collective-permute-start(bf16[4,128,128]{2,1,0:T(8,128)(2,1)S(1)} %add_convert_fusion.3.mine), channel_id=1, source_target_pairs={{0,2},{1,3},{2,0},{3,1},{4,6},{5,7},{6,4},{7,5},{8,10},{9,11},{10,... | collective-permute-start | bytes 393224 | tf_op jit(solution)/shard_map/swap/ppermute | solution.py:73
  31.2 2.7 %collective-permute-start.14 = (bf16[4,128,128]{2,1,0:T(8,128)(2,1)S(1)}, bf16[4,128,128]{2,1,0:T(8,128)(2,1)S(1)}, u32[]{:S(2)}, u32[]{:S(2)}) collective-permute-start(bf16[4,128,128]{2,1,0:T(8,128)(2,1)S(1)} %get-tuple-element.64.refs_4_), channel_id=1, source_target_pairs={{0,1},{1,0},{2,3},{3,2},{4,5},{5,4},{6,7},{7,6},{8,9},{9,8},{10,11... | collective-permute-start | bytes 393224 | tf_op jit(solution)/shard_map/rows_3/ppermute | solution.py:73
  33.2 1.4 %collective-permute-start.13 = (bf16[4,128,128]{2,1,0:T(8,128)(2,1)S(1)}, bf16[4,128,128]{2,1,0:T(8,128)(2,1)S(1)}, u32[]{:S(2)}, u32[]{:S(2)}) collective-permute-start(bf16[4,128,128]{2,1,0:T(8,128)(2,1)S(1)} %get-tuple-element.63.refs_2_), channel_id=1, source_target_pairs={{0,1},{1,0},{2,3},{3,2},{4,5},{5,4},{6,7},{7,6},{8,9},{9,8},{10,11... | collective-permute-start | bytes 393224 | tf_op jit(solution)/shard_map/rows_1/ppermute | solution.py:73
  33.3 4.3 %collective-permute-start.12 = (f32[144,128]{1,0:T(8,128)S(1)}, f32[144,128]{1,0:T(8,128)S(1)}, u32[]{:S(2)}, u32[]{:S(2)}) collective-permute-start(f32[144,128]{1,0:T(8,128)S(1)} %add.32), channel_id=1, source_target_pairs={{0,1},{1,0},{2,3},{3,2},{4,5},{5,4},{6,7},{7,6},{8,9},{9,8},{10,11... | collective-permute-start | bytes 221192 | tf_op jit(solution)/shard_map/swap/ppermute | solution.py:73
  35.6 8.6 %collective-permute-start.16 = (bf16[4,128,128]{2,1,0:T(8,128)(2,1)S(1)}, bf16[4,128,128]{2,1,0:T(8,128)(2,1)S(1)}, u32[]{:S(2)}, u32[]{:S(2)}) collective-permute-start(bf16[4,128,128]{2,1,0:T(8,128)(2,1)S(1)} %shard_map.116), channel_id=1, source_target_pairs={{0,4},{1,5},{2,6},{3,7},{4,0},{5,1},{6,2},{7,3},{8,12},{9,13},{10,... | collective-permute-start | bytes 393224 | tf_op jit(solution)/shard_map/sums_7/ppermute | solution.py:80
  37.6 9.0 %collective-permute-start.15 = (bf16[144,128]{1,0:T(8,128)(2,1)S(1)}, bf16[144,128]{1,0:T(8,128)(2,1)S(1)}, u32[]{:S(2)}, u32[]{:S(2)}) collective-permute-start(bf16[144,128]{1,0:T(8,128)(2,1)S(1)} %add_convert_fusion.7), channel_id=1, source_target_pairs={{0,8},{1,9},{2,10},{3,11},{4,12},{5,13},{6,14},{7,15},{8,0},{9,1},... | collective-permute-start | bytes 110600 | tf_op jit(solution)/shard_map/gradients_1/ppermute | solution.py:80
  41.2 6.9 %collective-permute-start.19 = (bf16[4,128,128]{2,1,0:T(8,128)(2,1)S(1)}, bf16[4,128,128]{2,1,0:T(8,128)(2,1)S(1)}, u32[]{:S(2)}, u32[]{:S(2)}) collective-permute-start(bf16[4,128,128]{2,1,0:T(8,128)(2,1)S(1)} %get-tuple-element.70), channel_id=1, source_target_pairs={{0,4},{1,5},{2,6},{3,7},{4,0},{5,1},{6,2},{7,3},{8,12},{9,13},{10,... | collective-permute-start | bytes 393224 | tf_op jit(solution)/shard_map/sums_5/ppermute | solution.py:80
  44.2 5.0 %collective-permute-start.20 = (bf16[4,128,128]{2,1,0:T(8,128)(2,1)S(1)}, bf16[4,128,128]{2,1,0:T(8,128)(2,1)S(1)}, u32[]{:S(2)}, u32[]{:S(2)}) collective-permute-start(bf16[4,128,128]{2,1,0:T(8,128)(2,1)S(1)} %add_convert_fusion.2), channel_id=1, source_target_pairs={{0,8},{1,9},{2,10},{3,11},{4,12},{5,13},{6,14},{7,15},{8,0},{9,1},... | collective-permute-start | bytes 393224 | tf_op jit(solution)/shard_map/sums_3/ppermute | solution.py:80
  44.6 6.4 %collective-permute-start.18 = (bf16[4,128,128]{2,1,0:T(8,128)(2,1)S(1)}, bf16[4,128,128]{2,1,0:T(8,128)(2,1)S(1)}, u32[]{:S(2)}, u32[]{:S(2)}) collective-permute-start(bf16[4,128,128]{2,1,0:T(8,128)(2,1)S(1)} %get-tuple-element.72), channel_id=1, source_target_pairs={{0,4},{1,5},{2,6},{3,7},{4,0},{5,1},{6,2},{7,3},{8,12},{9,13},{10,... | collective-permute-start | bytes 393224 | tf_op jit(solution)/shard_map/sums_6/ppermute | solution.py:80
  45.2 9.2 %collective-permute-start.22 = (bf16[4,128,128]{2,1,0:T(8,128)(2,1)S(1)}, bf16[4,128,128]{2,1,0:T(8,128)(2,1)S(1)}, u32[]{:S(2)}, u32[]{:S(2)}) collective-permute-start(bf16[4,128,128]{2,1,0:T(8,128)(2,1)S(1)} %get-tuple-element.73), channel_id=1, source_target_pairs={{0,4},{1,5},{2,6},{3,7},{4,0},{5,1},{6,2},{7,3},{8,12},{9,13},{10,... | collective-permute-start | bytes 393224 | tf_op jit(solution)/shard_map/sums_4/ppermute | solution.py:80
  46.6 6.4 %collective-permute-start.17 = (bf16[144,128]{1,0:T(8,128)(2,1)S(1)}, bf16[144,128]{1,0:T(8,128)(2,1)S(1)}, u32[]{:S(2)}, u32[]{:S(2)}) collective-permute-start(bf16[144,128]{1,0:T(8,128)(2,1)S(1)} %add_convert_fusion.6), channel_id=1, source_target_pairs={{0,24},{1,25},{2,26},{3,27},{4,28},{5,29},{6,30},{7,31},{8,16},{9,... | collective-permute-start | bytes 110600 | tf_op jit(solution)/shard_map/gradients_0/ppermute | solution.py:80
  49.3 8.2 %collective-permute-start.23 = (bf16[4,128,128]{2,1,0:T(8,128)(2,1)S(1)}, bf16[4,128,128]{2,1,0:T(8,128)(2,1)S(1)}, u32[]{:S(2)}, u32[]{:S(2)}) collective-permute-start(bf16[4,128,128]{2,1,0:T(8,128)(2,1)S(1)} %add_convert_fusion), channel_id=1, source_target_pairs={{0,24},{1,25},{2,26},{3,27},{4,28},{5,29},{6,30},{7,31},{8,16},{9,... | collective-permute-start | bytes 393224 | tf_op jit(solution)/shard_map/sums_1/ppermute | solution.py:80
  51.1 6.4 %collective-permute-start.24 = (bf16[4,128,128]{2,1,0:T(8,128)(2,1)S(1)}, bf16[4,128,128]{2,1,0:T(8,128)(2,1)S(1)}, u32[]{:S(2)}, u32[]{:S(2)}) collective-permute-start(bf16[4,128,128]{2,1,0:T(8,128)(2,1)S(1)} %add_convert_fusion.1), channel_id=1, source_target_pairs={{0,8},{1,9},{2,10},{3,11},{4,12},{5,13},{6,14},{7,15},{8,0},{9,1},... | collective-permute-start | bytes 393224 | tf_op jit(solution)/shard_map/sums_2/ppermute | solution.py:80
  53.0 4.0 %collective-permute-start.21 = (bf16[144,128]{1,0:T(8,128)(2,1)S(1)}, bf16[144,128]{1,0:T(8,128)(2,1)S(1)}, u32[]{:S(2)}, u32[]{:S(2)}) collective-permute-start(bf16[144,128]{1,0:T(8,128)(2,1)S(1)} %add_convert_fusion.5.refs_0_), channel_id=1, source_target_pairs={{0,4},{1,5},{2,6},{3,7},{4,0},{5,1},{6,2},{7,3},{8,12},{9,13},{10,... | collective-permute-start | bytes 110600 | tf_op jit(solution)/shard_map/gradients_2/ppermute | solution.py:80
